TPU v7x, 512 devices: a whole 4x8x8 slice. The times are simulated.
512 devices in a mesh: rep: 64 (over y, z_hi, x), fsdp: 8 (over z_lo, core).
Axes of the slice: x: 4, y: 8, z: 8 (z_hi: 2, z_lo: 4; z = z_hi * 4 + z_lo), core: 2. Of those that a mesh axis runs over, the one named last changes fastest.
Arguments:
- tokens: bfloat16 [65536, 8192], P(('rep', 'fsdp')), may hold values from -6 to 6
- cotangent: bfloat16 [65536, 512], P(('rep', 'fsdp')), may hold values from -6 to 6
- local_weights: bfloat16 [64, 8192, 512], P('rep', 'fsdp'), may hold values from -16 to 16
- anchor: float32 [8, 1024, 512], P('fsdp', 'rep'), may hold values from -6 to 6
- momentum: float32 [8, 1024, 512], P('fsdp', 'rep'), may hold values from -3 to 3
Outputs:
- mixed: bfloat16 [64, 8192, 512], P('rep', 'fsdp')
- new_anchor: float32 [8, 1024, 512], P('fsdp', 'rep')
- new_momentum: float32 [8, 1024, 512], P('fsdp', 'rep')
All inputs are finite; a program needn't handle non-finite values.
Results may differ from a plain program's by a relative error of at most 0.0085.
Values may be sent and summed in bfloat16 or wider, within the bound.
No kernel may reach another device: no remote copies, remote signals or barrier semaphores. Data moves between devices by JAX's collectives and lax.ppermute only.
A program may use at most 64 MiB of HBM per device.

v0:
```python
import jax
import jax.numpy as jnp
from jax import lax
from jax.sharding import PartitionSpec as P

HD = 128


EPS = 1e-06
ETA = 1.0
MOMENT = 0.9
OUTER_RATE = 0.7
MIX_RATE = 0.5


def body(tokens, cotangent, local_weights, anchor, momentum):
    own_weights = local_weights[0]
    row_count = tokens.shape[0]
    features = own_weights.shape[1]
    columns = lax.all_to_all(tokens, "fsdp", split_axis=1, concat_axis=0, tiled=True)
    segment = tokens
    projected = jnp.dot(
        segment,
        lax.all_gather(own_weights, "fsdp", axis=0, tiled=True),
        preferred_element_type=jnp.float32,
    )
    heads = projected.reshape(row_count, -1, HD)
    scale = lax.rsqrt(jnp.mean(heads * heads, axis=-1, keepdims=True) + EPS)
    normed = heads * scale
    upstream = cotangent.astype(jnp.float32).reshape(row_count, -1, HD)
    back = scale * (upstream - normed * jnp.mean(upstream * normed, axis=-1, keepdims=True))
    key_grad = back.reshape(row_count, features).astype(jnp.bfloat16)
    segment = columns
    grad = lax.dot_general(
        segment,
        lax.all_gather(key_grad, "fsdp", axis=0, tiled=True),
        (((0,), (0,)), ((), ())),
        preferred_element_type=jnp.float32,
    )
    local = (own_weights.astype(jnp.float32) - ETA * grad).astype(jnp.bfloat16)
    widened = local.astype(jnp.float32)
    summed = lax.psum_scatter(widened, "rep", scatter_dimension=0, tiled=True)
    base = anchor[0]
    average = summed / lax.axis_size("rep")
    delta = base - average
    new_mom = MOMENT * momentum[0] + delta
    new_base = base - OUTER_RATE * (delta + MOMENT * new_mom)
    whole_base = lax.all_gather(new_base, "rep", axis=0, tiled=True)
    mixed = ((1.0 - MIX_RATE) * widened + MIX_RATE * whole_base).astype(jnp.bfloat16)
    return (mixed[None], new_base[None], new_mom[None])


def solution(mesh):
    placed = (
        P(("rep", "fsdp"), None),
        P(("rep", "fsdp"), None),
        P("rep", "fsdp", None),
        P("fsdp", "rep", None),
        P("fsdp", "rep", None),
    )
    return jax.shard_map(
        body,
        mesh=mesh,
        in_specs=placed,
        out_specs=(P("rep", "fsdp", None), P("fsdp", "rep", None), P("fsdp", "rep", None)),
        check_vma=False,
    )
```

profile of v0, /device:TPU:6, one launch (start us, length us, event | category | flops | bytes accessed | tf_op | source)
XLA Modules:
  0.0 794.9 jit_solution(3513409430326253593)
XLA Ops:
  7.2 0.0 all-gather.9.cloned.1.call-start
  7.2 0.7 all-gather.9.cloned.1.call-update
  7.9 4.1 copy.29
  12.0 0.0 copy-start.2
  12.0 0.0 copy-start
  12.0 7.4 all-to-all-start
  19.4 0.0 all-gather.5.cloned.1.call-start
  19.4 0.0 copy-done.2
  19.4 0.1 reshape.34
  19.5 117.8 %all-gather.9.cloned.1.call-done = bf16[1,8192,512]{2,1,0:T(8,128)(2,1)} async-done(((bf16[1,1024,512]{2,1,0:T(8,128)(2,1)}), bf16[1,8192,512]{2,1,0:T(8,128)(2,1)}) %all-gather.9.cloned.1.call-update) | async-done | bytes 8388624 | tf_op jit(solution)/shard_map/all_gather | solution.py:24
  137.3 0.0 copy-done
  137.3 4.6 fusion
  141.9 0.0 copy-start.1
  142.0 0.1 reshape.33
  142.1 0.2 multiply_reduce_fusion.1
  142.3 0.4 multiply_reduce_fusion
  142.7 0.2 mul.57
  142.9 0.2 mul.62
  143.1 0.7 fusion.7
  143.8 0.0 all-gather.5.cloned.1.call-update
  143.8 0.0 reduce-scatter.4.cloned.1.call-start
  143.9 0.0 copy-done.1
  143.9 0.5 copy.28
  144.4 0.0 all-to-all-done
  144.5 3.9 copy.30
  148.4 46.7 %all-gather.5.cloned.1.call-done = bf16[1024,512]{1,0:T(8,128)(2,1)} async-done(((bf16[128,512]{1,0:T(8,128)(2,1)}), bf16[1024,512]{1,0:T(8,128)(2,1)}) %all-gather.5.cloned.1.call-update) | async-done | bytes 1048592 | tf_op jit(solution)/shard_map/all_gather | solution.py:36
  195.1 3.2 fusion.3
  198.3 1.8 copy.38
  200.1 0.0 copy-start.3
  200.2 0.0 copy-start.4
  200.2 0.0 reduce-scatter.4.cloned.1.call-update
  200.2 0.0 all-gather.7.cloned.1.call-start
  200.2 0.7 copy-done.3
  200.9 0.1 copy.31
  201.0 0.0 copy-done.4
  201.0 0.1 copy.32
  201.2 427.4 %reduce-scatter.4.cloned.1.call-done = f32[16,512]{1,0:T(8,128)} async-done(((f32[1024,512]{1,0:T(8,128)}), f32[16,512]{1,0:T(8,128)}) %reduce-scatter.4.cloned.1.call-update) | async-done | bytes 32784
  628.6 0.9 copy.39
  629.5 0.1 fusion.8
  629.6 0.7 copy.33
  630.3 0.0 all-gather.7.cloned.1.call-update
  630.3 0.7 copy.37
  631.0 0.7 copy.36
  631.7 150.3 %all-gather.7.cloned.1.call-done = f32[1024,512]{1,0:T(8,128)} async-done(((f32[16,512]{1,0:T(8,128)}), f32[1024,512]{1,0:T(8,128)}) %all-gather.7.cloned.1.call-update) | async-done | bytes 2097168 | tf_op jit(solution)/shard_map/all_gather | solution.py:48
  782.0 2.9 copy.34
  784.9 2.1 fusion.4
  787.0 1.3 copy.35
  (2 shorter events, 0.0 us)
Async XLA Ops:
  7.2 130.1 %all-gather.9.cloned.1.call-start = ((), (), s32[]{:S(2)}) async-start(), calls=%async_computation.4 | async-start | bytes 9437184 | tf_op jit(solution)/shard_map/all_gather | solution.py:24
  12.0 7.4 copy-start.2
  12.0 125.3 %copy-start = (bf16[128,8192]{1,0:T(8,128)(2,1)S(1)}, bf16[128,8192]{1,0:T(8,128)(2,1)}, u32[]{:S(2)}) copy-start(bf16[128,8192]{1,0:T(8,128)(2,1)} %param.5) | copy-start | bytes 6291460
  12.0 132.5 %all-to-all-start = ((bf16[128,8,1024]{0,2,1:T(8,128)(2,1)}), bf16[128,8,1024]{0,2,1:T(8,128)(2,1)}, u32[]{:S(2)}, u32[]{:S(2)}) async-start(bf16[128,8,1024]{0,2,1:T(8,128)(2,1)} %bitcast.55), calls=%async_computation | async-start | bytes 4194304 | tf_op jit(solution)/shard_map/all_to_all | solution.py:20
  19.4 175.7 %all-gather.5.cloned.1.call-start = ((), (), s32[]{:S(2)}) async-start(), calls=%async_computation.2 | async-start | bytes 1179648 | tf_op jit(solution)/shard_map/all_gather | solution.py:36
  141.9 2.0 copy-start.1
  143.8 484.7 %reduce-scatter.4.cloned.1.call-start = ((), (), s32[]{:S(2)}) async-start(), calls=%async_computation.5 | async-start | bytes 2129920
  200.1 0.8 copy-start.3
  200.2 0.9 copy-start.4
  200.2 581.8 %all-gather.7.cloned.1.call-start = ((), (), s32[]{:S(2)}) async-start(), calls=%async_computation.3 | async-start | bytes 2129920 | tf_op jit(solution)/shard_map/all_gather | solution.py:48
Sparse Core Ops, SparseCore 0:
  10.1 127.1 all-gather.8
  144.0 51.1 all-gather.4
  200.3 428.2 reduce-scatter.3
  634.3 147.6 all-gather.6
where the time goes:
time: 795 us
  waiting for transfers between devices  743 us (93%)
  local copies, waits for them, and re-layouts  19.2 us (2%)
  between operations  13.9 us (2%)
    unnamed x5, waiting for transfers between devices  428 us
    all_gather x1, waiting for transfers between devices, body(): whole_base = lax.all_gather(new_base, 'rep', axis=0, tiled=True)  150 us
    all_gather x1, waiting for transfers between devices, body(): lax.all_gather(own_weights, 'fsdp', axis=0, tiled=True)  118 us
    all_gather x1, waiting for transfers between devices, body(): lax.all_gather(key_grad, 'fsdp', axis=0, tiled=True)  46.7 us
  transfers between devices with their start and end apart: 5, of which 4 were waited for; matrix products, arithmetic and copies ran while one was open for 2% of the time, Pallas kernels for 0%

commit v1 on v0

v1 whole, which is shorter than its diff:
```python
import jax
import jax.numpy as jnp
from jax import lax
from jax.experimental import pallas as pl
from jax.experimental.pallas import tpu as pltpu
from jax.sharding import Mesh
from jax.sharding import PartitionSpec as P

HD = 128
EPS = 1e-06
ETA = 1.0
MOMENT = 0.9
OUTER_RATE = 0.7
MIX_RATE = 0.5

AXES = ("y", "zh", "x", "zl", "core")
SIZES = (8, 2, 4, 4, 2)
REP = ("y", "zh", "x")
FSDP = ("zl", "core")
SWAP = [(0, 1), (1, 0)]
BF = jnp.bfloat16
F32 = jnp.float32
LIMIT = 48 * 1024 * 1024


def params():
    return pltpu.CompilerParams(vmem_limit_bytes=LIMIT)


def regroup_kernel(x_ref, out_ref):
    out_ref[0] = x_ref[...]


def regroup(tokens, parts):
    rows, width = tokens.shape
    return pl.pallas_call(
        regroup_kernel,
        grid=(parts,),
        in_specs=[pl.BlockSpec((rows, width // parts), lambda i: (0, i))],
        out_specs=pl.BlockSpec((1, rows, width // parts), lambda i: (i, 0, 0)),
        out_shape=jax.ShapeDtypeStruct((parts, rows, width // parts), tokens.dtype),
        compiler_params=params(),
    )(tokens)


def project_kernel(x_ref, w_ref, out_ref):
    out_ref[0] = jnp.dot(x_ref[0], w_ref[...], preferred_element_type=F32).astype(BF)


def project(x, w):
    n, rows, depth = x.shape
    features = w.shape[1]
    return pl.pallas_call(
        project_kernel,
        grid=(n,),
        in_specs=[
            pl.BlockSpec((1, rows, depth), lambda i: (i, 0, 0)),
            pl.BlockSpec((depth, features), lambda i: (0, 0)),
        ],
        out_specs=pl.BlockSpec((1, rows, features), lambda i: (i, 0, 0)),
        out_shape=jax.ShapeDtypeStruct((n, rows, features), BF),
        compiler_params=params(),
    )(x, w)


def norm_kernel(p_ref, g_ref, out_ref):
    for h in range(g_ref.shape[1] // HD):
        cols = pl.ds(h * HD, HD)
        projected = p_ref[0, :, cols].astype(F32)
        for i in range(1, p_ref.shape[0]):
            projected += p_ref[i, :, cols].astype(F32)
        scale = lax.rsqrt(jnp.mean(projected * projected, axis=-1, keepdims=True) + EPS)
        normed = projected * scale
        upstream = g_ref[:, cols].astype(F32)
        back = scale * (upstream - normed * jnp.mean(upstream * normed, axis=-1, keepdims=True))
        out_ref[:, cols] = back.astype(BF)


def norm_grad(parts, cotangent):
    return pl.pallas_call(
        norm_kernel,
        out_shape=jax.ShapeDtypeStruct(cotangent.shape, BF),
        compiler_params=params(),
    )(parts, cotangent)


def tdot(a, b):
    return lax.dot_general(a, b, (((0,), (0,)), ((), ())), preferred_element_type=F32)


def inner_kernel(core_ref, xs_ref, xo_ref, ks_ref, ko_ref, w_ref, out_ref):
    xs = xs_ref[...].reshape(ks_ref.shape[0], -1)
    grad = tdot(xs, ks_ref[...]) + tdot(xo_ref[...], ko_ref[...])
    out_ref[...] = (w_ref[...].astype(F32) - ETA * grad).astype(BF)


def inner_step(core, x, x_other, k_same, k_other, w, block=256):
    rows, features = w.shape
    n, tokens, _ = x.shape
    steps = rows // block
    half = n * tokens
    return pl.pallas_call(
        inner_kernel,
        grid_spec=pltpu.PrefetchScalarGridSpec(
            num_scalar_prefetch=1,
            grid=(steps,),
            in_specs=[
                pl.BlockSpec((n, tokens, block), lambda i, c: (0, 0, c[0] * steps + i)),
                pl.BlockSpec((half, block), lambda i, c: (0, i)),
                pl.BlockSpec((half, features), lambda i, c: (0, 0)),
                pl.BlockSpec((half, features), lambda i, c: (0, 0)),
                pl.BlockSpec((block, features), lambda i, c: (i, 0)),
            ],
            out_specs=pl.BlockSpec((block, features), lambda i, c: (i, 0)),
        ),
        out_shape=jax.ShapeDtypeStruct((rows, features), BF),
        compiler_params=params(),
    )(core, x, x_other, k_same, k_other, w)


def outer_kernel(l_ref, a_ref, m_ref, base_ref, mom_ref, all_ref):
    n = l_ref.shape[0]
    total = l_ref[0].astype(F32)
    for i in range(1, n):
        total += l_ref[i].astype(F32)
    base = a_ref[0]
    delta = base - total / n
    new_mom = MOMENT * m_ref[0] + delta
    new_base = base - OUTER_RATE * (delta + MOMENT * new_mom)
    mom_ref[0] = new_mom
    base_ref[0] = new_base
    low = new_base.astype(BF)
    for i in range(n):
        all_ref[i] = low


def outer_step(locals_, anchor, momentum):
    return pl.pallas_call(
        outer_kernel,
        out_shape=(
            jax.ShapeDtypeStruct(anchor.shape, F32),
            jax.ShapeDtypeStruct(momentum.shape, F32),
            jax.ShapeDtypeStruct(locals_.shape, BF),
        ),
        compiler_params=params(),
    )(locals_, anchor, momentum)


def mix_kernel(l_ref, b_ref, out_ref):
    mixed = (1.0 - MIX_RATE) * l_ref[...].astype(F32) + MIX_RATE * b_ref[...].astype(F32)
    out_ref[0] = mixed.astype(BF)


def mix(local, base, block=256):
    rows, features = local.shape
    return pl.pallas_call(
        mix_kernel,
        grid=(rows // block,),
        in_specs=[pl.BlockSpec((block, features), lambda i: (i, 0))] * 2,
        out_specs=pl.BlockSpec((1, block, features), lambda i: (0, i, 0)),
        out_shape=jax.ShapeDtypeStruct((1, rows, features), BF),
        compiler_params=params(),
    )(local, base)


def body(tokens, cotangent, local_weights, anchor, momentum):
    own = local_weights[0]
    depth, features = own.shape
    rows = tokens.shape[0]
    chips, n_rep = SIZES[3], SIZES[0] * SIZES[1] * SIZES[2]
    core = lax.axis_index("core")
    x = lax.all_to_all(regroup(tokens, chips), "zl", 0, 0, tiled=True)
    chip_weights = lax.all_gather(own, "core", axis=0, tiled=True)
    parts = project(x, chip_weights)
    send = lax.dynamic_slice_in_dim(x, (1 - core) * depth, depth, 2).reshape(chips * rows, depth)
    x_other = lax.ppermute(send, "core", SWAP)
    mine = lax.all_to_all(parts, "zl", 0, 0, tiled=True)
    key_grad = norm_grad(mine, cotangent)
    spread = jnp.broadcast_to(key_grad[None], (chips, rows, features))
    k_same = lax.all_to_all(spread, "zl", 0, 0, tiled=True).reshape(chips * rows, features)
    k_other = lax.ppermute(k_same, "core", SWAP)
    local = inner_step(core.reshape(1), x, x_other, k_same, k_other, own)
    shares = lax.all_to_all(local.reshape(n_rep, -1, features), REP, 0, 0, tiled=True)
    new_base, new_mom, spread_base = outer_step(shares, anchor, momentum)
    base = lax.all_to_all(spread_base, REP, 0, 0, tiled=True).reshape(depth, features)
    return mix(local, base), new_base, new_mom


def solution(mesh):
    fine = Mesh(mesh.devices.reshape(SIZES), AXES)
    placed = (
        P((*REP, *FSDP), None),
        P((*REP, *FSDP), None),
        P(REP, FSDP, None),
        P(FSDP, REP, None),
        P(FSDP, REP, None),
    )
    return jax.shard_map(
        body,
        mesh=fine,
        in_specs=placed,
        out_specs=(P(REP, FSDP, None), P(FSDP, REP, None), P(FSDP, REP, None)),
        check_vma=False,
    )
```

time: 795 us -> 209 us (0.26)
  waiting for transfers between devices: 743 us -> 60.9 us
  blocking collectives: 0 us -> 102 us
  local copies, waits for them, and re-layouts: 19.2 us -> 7.21 us
  Pallas kernels: 0 us -> 8.63 us
    unnamed x5 -> x1, waiting for transfers between devices: 428 us -> 0.71 us
    all_gather x3 -> x1, waiting for transfers between devices: 315 us -> 23.4 us  [body(): chip_weights = lax.all_gather(own, 'core', axis=0, tiled=True)]
    all_to_all x0 -> x3, blocking collectives: none -> 102 us  [the longest x1 48 us: body(): lax.all_to_all(local.reshape(n_rep, -1, features), REP, 0, 0, tiled=True)]
    all_to_all x1 -> x2, waiting for transfers between devices: 0.01 us -> 34.7 us  [the longest x1 24.1 us: body(): x = lax.all_to_all(regroup(tokens, chips), 'zl', 0, 0, tiled=True)]
    pallas_call x0 -> x6, Pallas kernels: none -> 8.63 us  [the longest x1 3.62 us: inner_step(): pl.pallas_call(inner_kernel, grid_spec=pltpu.PrefetchScalarGridSpec(num_s...]
  transfers between devices with their start and end apart: 5 -> 5, of which waited for: 4 -> 4; matrix products, arithmetic and copies ran while one was open for 2% -> 1% of each run, Pallas kernels for 0% -> 0%
where the time goes in v1:
time: 209 us; the launch traced here: 208 us
  blocking collectives  102 us (49%)
  waiting for transfers between devices  60.9 us (29%)
  starting transfers between devices  15.2 us (7%)
  between operations  14.1 us (7%)
  Pallas kernels  8.63 us (4%)
  local copies, waits for them, and re-layouts  7.21 us (3%)
    all_to_all x1, blocking collectives, body(): lax.all_to_all(local.reshape(n_rep, -1, features), REP, 0, 0, tiled=True)  48 us
    all_to_all x1, blocking collectives, body(): lax.all_to_all(spread_base, REP, 0, 0, tiled=True).reshape(depth, features)  37.9 us
    all_to_all x1, waiting for transfers between devices, body(): x = lax.all_to_all(regroup(tokens, chips), 'zl', 0, 0, tiled=True)  24.1 us
    all_gather x1, waiting for transfers between devices, body(): chip_weights = lax.all_gather(own, 'core', axis=0, tiled=True)  23.4 us
    all_to_all x1, blocking collectives, body(): mine = lax.all_to_all(parts, 'zl', 0, 0, tiled=True)  16.4 us
    all_to_all x1, waiting for transfers between devices, body(): lax.all_to_all(spread, 'zl', 0, 0, tiled=True)  10.6 us
    all_to_all x1, starting transfers between devices, body(): x = lax.all_to_all(regroup(tokens, chips), 'zl', 0, 0, tiled=True)  7.26 us
    unnamed x16, local copies, waits for them, and re-layouts  5.29 us
  transfers between devices with their start and end apart: 5, of which 4 were waited for; matrix products, arithmetic and copies ran while one was open for 1% of the time, Pallas kernels for 0%

profile of v1, /device:TPU:6, one launch (start us, length us, event | category | flops | bytes accessed | tf_op | source)
XLA Modules:
  0.0 208.4 jit_solution(2485587746309617152)
XLA Ops:
  7.2 0.0 copy-start.3
  7.2 1.6 copy-done.3
  8.8 0.4 shard_map.76
  9.1 0.0 copy-start.1
  9.1 1.3 copy-done.1
  10.5 7.3 %all-to-all-start = ((bf16[4,128,2048]{2,1,0:T(8,128)(2,1)}), bf16[4,128,2048]{2,1,0:T(8,128)(2,1)S(1)}, u32[]{:S(2)}, u32[]{:S(2)}) async-start(bf16[4,128,2048]{2,1,0:T(8,128)(2,1)} %copy-done.1), calls=%async_computation | async-start | bytes 4194304 | tf_op jit(solution)/shard_map/all_to_all | solution.py:172
  17.7 0.0 all-gather.3.cloned.1.call-start
  17.7 0.7 all-gather.3.cloned.1.call-update
  18.5 23.4 %all-gather.3.cloned.1.call-done = bf16[1,2048,512]{2,1,0:T(8,128)(2,1)} async-done(((bf16[1,1024,512]{2,1,0:T(8,128)(2,1)}), bf16[1,2048,512]{2,1,0:T(8,128)(2,1)}) %all-gather.3.cloned.1.call-update) | async-done | bytes 2097168 | tf_op jit(solution)/shard_map/all_gather | solution.py:173
  41.8 24.1 %all-to-all-done.x_ref.xs_ref = bf16[4,128,2048]{2,1,0:T(8,128)(2,1)S(1)} async-done(((bf16[4,128,2048]{2,1,0:T(8,128)(2,1)}), bf16[4,128,2048]{2,1,0:T(8,128)(2,1)S(1)}, u32[]{:S(2)}, u32[]{:S(2)}) %all-to-all-start) | async-done | bytes 2097184 | tf_op jit(solution)/shard_map/all_to_all | solution.py:172
  65.9 0.0 copy-start
  65.9 0.0 copy-start.4
  65.9 2.3 %copy-done.4 = bf16[1,2048,512]{2,1,0:T(8,128)(2,1)S(1)} copy-done((bf16[1,2048,512]{2,1,0:T(8,128)(2,1)S(1)}, bf16[1,2048,512]{2,1,0:T(8,128)(2,1)}, u32[]{:S(2)}) %copy-start.4) | copy-done | bytes 2097176
  68.3 0.0 copy-start.5
  68.3 1.8 shard_map.77
  70.1 16.4 %all_to_all.25.p_ref = bf16[4,128,512]{2,1,0:T(8,128)(2,1)S(1)} all-to-all(bf16[4,128,512]{2,1,0:T(8,128)(2,1)S(1)} %shard_map.77), channel_id=1, replica_groups=mesh['y'=8,'zh'=2,'x'=4,'zl'=4,'core'=2] {'zl'}, dimensions={0} | all-to-all | bytes 1048576 | tf_op jit(solution)/shard_map/all_to_all | solution.py:177
  86.5 0.0 copy-done.5
  86.5 0.2 shard_map.78
  86.7 0.0 copy-start.2
  86.8 0.8 broadcast_in_dim.2
  87.6 4.1 %all-to-all-start.2 = ((bf16[4,128,512]{2,1,0:T(8,128)(2,1)}), bf16[4,128,512]{2,1,0:T(8,128)(2,1)}, u32[]{:S(2)}, u32[]{:S(2)}) async-start(bf16[4,128,512]{2,1,0:T(8,128)(2,1)} %broadcast_in_dim.2), calls=%async_computation.2 | async-start | bytes 1048576 | tf_op jit(solution)/shard_map/all_to_all | solution.py:180
  91.8 0.0 copy-done
  91.8 1.1 constant_dynamic-slice_fusion
  92.8 1.9 collective-permute-start
  94.8 10.6 %all-to-all-done.2 = bf16[4,128,512]{2,1,0:T(8,128)(2,1)} async-done(((bf16[4,128,512]{2,1,0:T(8,128)(2,1)}), bf16[4,128,512]{2,1,0:T(8,128)(2,1)}, u32[]{:S(2)}, u32[]{:S(2)}) %all-to-all-start.2) | async-done | bytes 524320 | tf_op jit(solution)/shard_map/all_to_all | solution.py:180
  105.4 1.9 collective-permute-start.1
  107.3 0.0 collective-permute-done.xo_ref
  107.3 2.1 collective-permute-done.1.ko_ref
  109.4 0.0 copy-done.2
  109.4 3.6 %shard_map.79.l_ref = bf16[1024,512]{1,0:T(8,128)(2,1)S(1)} custom-call(s32[1]{0:T(128)} %bitcast.core_ref, bf16[4,128,2048]{2,1,0:T(8,128)(2,1)} %copy-done, bf16[512,1024]{1,0:T(8,128)(2,1)S(1)} %collective-permute-done.xo_ref, bf16[512,512]{1,0:T(8,128)(2,1)} %bitcast.3.ks_ref, bf16[512,512]{1,0:T(8,128)(2,1)S(1)} %collective-permute-done.1.ko_ref, ...), custom_call_target="tpu_custom_call" | custom-call | tf_op jit(solution)/shard_map/pallas_call | solution.py:102
  113.0 0.0 copy-start.6
  113.0 0.0 copy-start.7
  113.0 48.0 %all_to_all.26.l_ref = bf16[64,16,512]{2,1,0:T(8,128)(2,1)S(1)} all-to-all(bf16[64,16,512]{2,1,0:T(8,128)(2,1)S(1)} %bitcast.7), channel_id=1, replica_groups=mesh['y'=8,'zh'=2,'x'=4,'zl'=4,'core'=2] {'y','zh','x'}, dimensions={0} | all-to-all | bytes 2097152 | tf_op jit(solution)/shard_map/all_to_all | solution.py:183
  161.1 0.0 copy-done.6
  161.1 0.0 copy-done.7
  161.1 0.9 shard_map.80
  162.0 37.9 %all_to_all.27 = bf16[64,16,512]{2,1,0:T(8,128)(2,1)S(1)} all-to-all(bf16[64,16,512]{2,1,0:T(8,128)(2,1)S(1)} %get-tuple-element.6), channel_id=1, replica_groups=mesh['y'=8,'zh'=2,'x'=4,'zl'=4,'core'=2] {'y','zh','x'}, dimensions={0} | all-to-all | bytes 2097152 | tf_op jit(solution)/shard_map/all_to_all | solution.py:185
  199.9 1.7 shard_map.81
Async XLA Ops:
  7.2 1.6 copy-start.3
  9.1 1.3 copy-start.1
  10.5 55.5 %all-to-all-start = ((bf16[4,128,2048]{2,1,0:T(8,128)(2,1)}), bf16[4,128,2048]{2,1,0:T(8,128)(2,1)S(1)}, u32[]{:S(2)}, u32[]{:S(2)}) async-start(bf16[4,128,2048]{2,1,0:T(8,128)(2,1)} %copy-done.1), calls=%async_computation | async-start | bytes 4194304 | tf_op jit(solution)/shard_map/all_to_all | solution.py:172
  17.7 24.1 %all-gather.3.cloned.1.call-start = ((), (), s32[]{:S(2)}) async-start(), calls=%async_computation.5 | async-start | bytes 3145728 | tf_op jit(solution)/shard_map/all_gather | solution.py:173
  65.9 25.8 %copy-start = (bf16[4,128,2048]{2,1,0:T(8,128)(2,1)}, bf16[4,128,2048]{2,1,0:T(8,128)(2,1)S(1)}, u32[]{:S(2)}) copy-start(bf16[4,128,2048]{2,1,0:T(8,128)(2,1)S(1)} %all-to-all-done.x_ref.xs_ref) | copy-start | bytes 6291460
  65.9 2.3 %copy-start.4 = (bf16[1,2048,512]{2,1,0:T(8,128)(2,1)S(1)}, bf16[1,2048,512]{2,1,0:T(8,128)(2,1)}, u32[]{:S(2)}) copy-start(bf16[1,2048,512]{2,1,0:T(8,128)(2,1)} %all-gather.3.cloned.1.call-done) | copy-start | bytes 6291460
  68.3 18.2 %copy-start.5 = (bf16[128,512]{1,0:T(8,128)(2,1)S(1)}, bf16[128,512]{1,0:T(8,128)(2,1)}, u32[]{:S(2)}) copy-start(bf16[128,512]{1,0:T(8,128)(2,1)} %g_ref.1) | copy-start | bytes 393220
  86.7 22.6 %copy-start.2 = (bf16[1,1024,512]{2,1,0:T(8,128)(2,1)S(1)}, bf16[1,1024,512]{2,1,0:T(8,128)(2,1)}, u32[]{:S(2)}) copy-start(bf16[1,1024,512]{2,1,0:T(8,128)(2,1)} %param.7) | copy-start | bytes 3145732
  87.6 17.8 %all-to-all-start.2 = ((bf16[4,128,512]{2,1,0:T(8,128)(2,1)}), bf16[4,128,512]{2,1,0:T(8,128)(2,1)}, u32[]{:S(2)}, u32[]{:S(2)}) async-start(bf16[4,128,512]{2,1,0:T(8,128)(2,1)} %broadcast_in_dim.2), calls=%async_computation.2 | async-start | bytes 1048576 | tf_op jit(solution)/shard_map/all_to_all | solution.py:180
  92.8 14.4 %collective-permute-start = (bf16[512,1024]{1,0:T(8,128)(2,1)}, bf16[512,1024]{1,0:T(8,128)(2,1)S(1)}, u32[]{:S(2)}, u32[]{:S(2)}) collective-permute-start(bf16[512,1024]{1,0:T(8,128)(2,1)} %bitcast.1), channel_id=1, source_target_pairs={{0,1},{1,0},{2,3},{3,2},{4,5},{5,4},{6,7},{7,6},{8,9},{9,8},{10,11... | collective-permute-start | bytes 3145736 | tf_op jit(solution)/shard_map/ppermute | solution.py:176
  105.4 4.0 %collective-permute-start.1 = (bf16[512,512]{1,0:T(8,128)(2,1)}, bf16[512,512]{1,0:T(8,128)(2,1)S(1)}, u32[]{:S(2)}, u32[]{:S(2)}) collective-permute-start(bf16[512,512]{1,0:T(8,128)(2,1)} %bitcast.3.ks_ref), channel_id=1, source_target_pairs={{0,1},{1,0},{2,3},{3,2},{4,5},{5,4},{6,7},{7,6},{8,9},{9,8},{10,11... | collective-permute-start | bytes 1572872 | tf_op jit(solution)/shard_map/ppermute | solution.py:181
  113.0 48.1 %copy-start.6 = (f32[1,16,512]{2,1,0:T(8,128)S(1)}, f32[1,16,512]{2,1,0:T(8,128)}, u32[]{:S(2)}) copy-start(f32[1,16,512]{2,1,0:T(8,128)} %a_ref.1) | copy-start | bytes 98308
  113.0 48.1 %copy-start.7 = (f32[1,16,512]{2,1,0:T(8,128)S(1)}, f32[1,16,512]{2,1,0:T(8,128)}, u32[]{:S(2)}) copy-start(f32[1,16,512]{2,1,0:T(8,128)} %m_ref.1) | copy-start | bytes 98308
Sparse Core Ops, SparseCore 0:
  20.6 21.1 all-gather.2

commit v2 on v0

v2 whole, which is shorter than its diff:
```python
import jax
import jax.numpy as jnp
from jax import lax
from jax.experimental import pallas as pl
from jax.experimental.pallas import tpu as pltpu
from jax.sharding import Mesh
from jax.sharding import PartitionSpec as P

HD = 128
EPS = 1e-06
ETA = 1.0
MOMENT = 0.9
OUTER_RATE = 0.7
MIX_RATE = 0.5

AXES = ("y", "zh", "x", "zl", "core")
SIZES = (8, 2, 4, 4, 2)
REP = ("y", "zh", "x")
FSDP = ("zl", "core")
SWAP = [(0, 1), (1, 0)]
BF = jnp.bfloat16
F32 = jnp.float32
LIMIT = 48 * 1024 * 1024


def call(kernel, out_shape, flops=0, moved=0, **more):
    return pl.pallas_call(
        kernel,
        out_shape=out_shape,
        compiler_params=pltpu.CompilerParams(vmem_limit_bytes=LIMIT),
        cost_estimate=pl.CostEstimate(flops=flops, bytes_accessed=moved, transcendentals=0),
        **more,
    )


def project_kernel(x_ref, w_ref, out_ref):
    out_ref[...] = jnp.dot(x_ref[...], w_ref[...], preferred_element_type=F32).astype(BF)


def project(x, w):
    rows, depth = x.shape
    features = w.shape[1]
    return call(
        project_kernel,
        jax.ShapeDtypeStruct((rows, features), BF),
        flops=2 * rows * depth * features,
        moved=2 * (x.size + w.size),
    )(x, w)


def norm_kernel(a_ref, b_ref, c_ref, d_ref, g_ref, out_ref):
    for h in range(g_ref.shape[1] // HD):
        cols = pl.ds(h * HD, HD)
        projected = a_ref[:, cols].astype(F32)
        for ref in (b_ref, c_ref, d_ref):
            projected += ref[:, cols].astype(F32)
        scale = lax.rsqrt(jnp.mean(projected * projected, axis=-1, keepdims=True) + EPS)
        normed = projected * scale
        upstream = g_ref[:, cols].astype(F32)
        back = scale * (upstream - normed * jnp.mean(upstream * normed, axis=-1, keepdims=True))
        out_ref[:, cols] = back.astype(BF)


def norm_grad(parts, cotangent):
    return call(
        norm_kernel,
        jax.ShapeDtypeStruct(cotangent.shape, BF),
        moved=6 * cotangent.size * 2,
    )(*parts, cotangent)


def split_kernel(core_ref, x_ref, mine_ref, send_ref):
    depth = mine_ref.shape[0]
    mine = pl.ds(pl.multiple_of(core_ref[0] * depth, depth), depth)
    other = pl.ds(pl.multiple_of((1 - core_ref[0]) * depth, depth), depth)
    mine_ref[...] = x_ref[:, mine].T
    send_ref[...] = x_ref[:, other].T


def split(core, x):
    rows, width = x.shape
    shape = jax.ShapeDtypeStruct((width // 2, rows), BF)
    vmem = pl.BlockSpec(memory_space=pltpu.VMEM)
    return call(
        split_kernel,
        (shape, shape),
        in_specs=[pl.BlockSpec(memory_space=pltpu.SMEM), vmem],
        out_specs=(vmem, vmem),
    )(core.reshape(1), x)


def inner_kernel(*refs):
    *xs, ks_ref, ko_ref, w_ref, out_ref = refs
    x = jnp.concatenate([ref[...] for ref in xs], axis=1)
    k = jnp.concatenate([ks_ref[...], ko_ref[...]], axis=0)
    grad = jnp.dot(x, k, preferred_element_type=F32)
    local = (w_ref[...].astype(F32) - ETA * grad).astype(BF)
    ny, nx, nz, own, _ = out_ref.shape
    for y in range(ny):
        for z in range(nz):
            for x in range(nx):
                start = ((y * nz + z) * nx + x) * own
                out_ref[y, x, z] = local[start : start + own]


def inner_step(xs, k_same, k_other, w, block=256):
    rows, features = w.shape
    half = k_same.shape[0]
    ny, nz, nx = SIZES[:3]
    own = rows // (ny * nz * nx)
    by = block // (nz * nx * own)
    return call(
        inner_kernel,
        jax.ShapeDtypeStruct((ny, nx, nz, own, features), BF),
        flops=4 * rows * half * features,
        moved=4 * (rows * half + w.size + k_same.size),
        grid=(rows // block,),
        in_specs=[pl.BlockSpec((block, x.shape[1]), lambda i: (i, 0)) for x in xs]
        + [
            pl.BlockSpec((half, features), lambda i: (0, 0)),
            pl.BlockSpec((half, features), lambda i: (0, 0)),
            pl.BlockSpec((block, features), lambda i: (i, 0)),
        ],
        out_specs=pl.BlockSpec((by, nx, nz, own, features), lambda i: (i, 0, 0, 0, 0)),
    )(*xs, k_same, k_other, w)


def total_kernel(l_ref, out_ref, low_ref):
    total = l_ref[0].astype(F32)
    for i in range(1, l_ref.shape[0]):
        total += l_ref[i].astype(F32)
    out_ref[...] = total
    low_ref[...] = total.astype(BF)


def half_total(shares):
    shape = shares.shape[1:]
    return call(
        total_kernel,
        (jax.ShapeDtypeStruct(shape, F32), jax.ShapeDtypeStruct(shape, BF)),
        moved=2 * shares.size,
    )(shares)


def outer_kernel(zh_ref, s_ref, o_ref, am_ref, pam_ref, base_ref, mom_ref, all_ref):
    zh = zh_ref[0]
    own = am_ref.shape[1]
    n_rep = SIZES[0] * SIZES[1] * SIZES[2]

    def step(which, held):
        rows = pl.ds(pl.multiple_of(which * own, own), own)
        average = (s_ref[rows] + o_ref[rows].astype(F32)) / n_rep
        base = held[0]
        delta = base - average
        new_mom = MOMENT * held[1] + delta
        return rows, base - OUTER_RATE * (delta + MOMENT * new_mom), new_mom

    rows, new_base, new_mom = step(zh, am_ref)
    base_ref[0] = new_base
    mom_ref[0] = new_mom
    partner_rows, partner_base, _ = step(1 - zh, pam_ref)
    low, partner_low = new_base.astype(BF), partner_base.astype(BF)
    for i in range(all_ref.shape[0]):
        all_ref[i, rows] = low
        all_ref[i, partner_rows] = partner_low


def outer_step(zh, total, other, held, partner_held, n):
    own, features = held.shape[1:]
    vmem = pl.BlockSpec(memory_space=pltpu.VMEM)
    return call(
        outer_kernel,
        (
            jax.ShapeDtypeStruct((1, own, features), F32),
            jax.ShapeDtypeStruct((1, own, features), F32),
            jax.ShapeDtypeStruct((n, *total.shape), BF),
        ),
        moved=2 * n * total.size,
        in_specs=[pl.BlockSpec(memory_space=pltpu.SMEM)] + [vmem] * 4,
        out_specs=(vmem,) * 3,
    )(zh.reshape(1), total, other, held, partner_held)


def mix_kernel(l_ref, b_ref, out_ref):
    mixed = (1.0 - MIX_RATE) * l_ref[...].astype(F32) + MIX_RATE * b_ref[...].astype(F32)
    mixed = mixed.astype(BF)
    ny, nx, nz, own, _ = l_ref.shape
    for y in range(ny):
        for z in range(nz):
            for x in range(nx):
                out_ref[0, pl.ds(((y * nz + z) * nx + x) * own, own)] = mixed[y, x, z]


def mix(local, base, block=2):
    ny, nx, nz, own, features = local.shape
    rows = nx * nz * own
    return call(
        mix_kernel,
        jax.ShapeDtypeStruct((1, ny * rows, features), BF),
        moved=6 * local.size,
        grid=(ny // block,),
        in_specs=[pl.BlockSpec((block, nx, nz, own, features), lambda i: (i, 0, 0, 0, 0))] * 2,
        out_specs=pl.BlockSpec((1, block * rows, features), lambda i: (0, i, 0)),
    )(local, base)


def across(value, k):
    return lax.ppermute(value, "zl", [(i, i ^ k) for i in range(SIZES[3])])


def body(tokens, cotangent, local_weights, anchor, momentum):
    own = local_weights[0]
    depth, features = own.shape
    width = tokens.shape[1] // SIZES[3]
    core, zl, zh = (lax.axis_index(name) for name in ("core", "zl", "zh"))
    chunk = [lax.dynamic_slice_in_dim(tokens, (zl ^ k) * width, width, 1) for k in range(4)]
    chip_weights = lax.all_gather(own, "core", axis=0, tiled=True)
    got = {k: across(chunk[k], k) for k in (3, 2, 1)}
    got[0] = chunk[0]
    held = jnp.concatenate([anchor, momentum], axis=0)
    partner_held = lax.ppermute(held, "zh", SWAP)
    made = project(got[0], chip_weights)
    got[1], made, partner_held = lax.optimization_barrier((got[1], made, partner_held))
    mine, other = {}, {}
    parts = [made]
    for k in (1, 2, 3):
        got[k], parts, other = lax.optimization_barrier((got[k], parts, other))
        parts.append(across(project(got[k], chip_weights), k))
        mine[k - 1], send = split(core, got[k - 1])
        other[k - 1] = lax.ppermute(send, "core", SWAP)
    parts, other = lax.optimization_barrier((parts, other))
    key_grad = norm_grad(parts, cotangent)
    got[3], key_grad = lax.optimization_barrier((got[3], key_grad))
    mine[3], send = split(core, got[3])
    other[3] = lax.ppermute(send, "core", SWAP)
    k_same = jnp.concatenate([key_grad] + [across(key_grad, k) for k in (1, 2, 3)], axis=0)
    k_other = lax.ppermute(k_same, "core", SWAP)
    xs = [mine[k] for k in range(4)] + [other[k] for k in range(4)]
    local = inner_step(xs, k_same, k_other, own)
    ny, nx, nz, rows, _ = local.shape
    shares = lax.all_to_all(local.reshape(ny * nx, nz * rows, features), ("y", "x"), 0, 0, tiled=True)
    total, low = half_total(shares)
    other = lax.ppermute(low, "zh", SWAP)
    new_base, new_mom, spread = outer_step(zh, total, other, held, partner_held, ny * nx)
    base = lax.all_to_all(spread, ("y", "x"), 0, 0, tiled=True).reshape(local.shape)
    return mix(local, base), new_base, new_mom


def solution(mesh):
    fine = Mesh(mesh.devices.reshape(SIZES), AXES)
    placed = (
        P((*REP, *FSDP), None),
        P((*REP, *FSDP), None),
        P(REP, FSDP, None),
        P(FSDP, REP, None),
        P(FSDP, REP, None),
    )
    return jax.shard_map(
        body,
        mesh=fine,
        in_specs=placed,
        out_specs=(P(REP, FSDP, None), P(FSDP, REP, None), P(FSDP, REP, None)),
        check_vma=False,
    )
```

time: 795 us -> 201 us (0.25)
  waiting for transfers between devices: 743 us -> 47.9 us
  blocking collectives: 0 us -> 69.5 us
  starting transfers between devices: 7.56 us -> 56.2 us
  local copies, waits for them, and re-layouts: 19.2 us -> 4.37 us
    unnamed x5 -> x1, waiting for transfers between devices: 428 us -> 0.68 us
    all_gather x3 -> x1, waiting for transfers between devices: 315 us -> 0.02 us  [body(): chip_weights = lax.all_gather(own, 'core', axis=0, tiled=True)]
    all_to_all x0 -> x2, blocking collectives: none -> 69.5 us  [the longest x1 38.6 us: body(): lax.all_to_all(local.reshape(ny * nx, nz * rows, features), ('y', 'x'), 0...]
    ppermute x0 -> x16, starting transfers between devices: none -> 56.2 us  [the longest x9 30.4 us: across(): return lax.ppermute(value, 'zl', [(i, i ^ k) for i in range(SIZES[3])])]
    ppermute x0 -> x16, waiting for transfers between devices: none -> 47.2 us  [the longest x1 24.3 us: body(): partner_held = lax.ppermute(held, 'zh', SWAP)]
    unnamed x19 -> x16, local copies, waits for them, and re-layouts: 11 us -> 1.64 us
  transfers between devices with their start and end apart: 5 -> 17, of which waited for: 4 -> 7; matrix products, arithmetic and copies ran while one was open for 2% -> 1% of each run, Pallas kernels for 0% -> 1%
where the time goes in v2:
time: 201 us; the launch traced here: 200 us
  blocking collectives  69.5 us (35%)
  starting transfers between devices  56.2 us (28%)
  waiting for transfers between devices  47.9 us (24%)
  between operations  14.4 us (7%)
  Pallas kernels  7.06 us (4%)
  local copies, waits for them, and re-layouts  4.37 us (2%)
    all_to_all x1, blocking collectives, body(): lax.all_to_all(local.reshape(ny * nx, nz * rows, features), ('y', 'x'), 0...  38.6 us
    all_to_all x1, blocking collectives, body(): lax.all_to_all(spread, ('y', 'x'), 0, 0, tiled=True).reshape(local.shape)  30.9 us
    ppermute x9, starting transfers between devices, across(): return lax.ppermute(value, 'zl', [(i, i ^ k) for i in range(SIZES[3])])  30.4 us
    ppermute x1, waiting for transfers between devices, body(): partner_held = lax.ppermute(held, 'zh', SWAP)  24.3 us
    ppermute x9, waiting for transfers between devices, across(): return lax.ppermute(value, 'zl', [(i, i ^ k) for i in range(SIZES[3])])  18.6 us
    ppermute x1, starting transfers between devices, body(): partner_held = lax.ppermute(held, 'zh', SWAP)  8.74 us
    ppermute x1, starting transfers between devices, body(): other = lax.ppermute(low, 'zh', SWAP)  6.85 us
    ppermute x3, starting transfers between devices, body(): other[k - 1] = lax.ppermute(send, 'core', SWAP)  5.89 us
  transfers between devices with their start and end apart: 17, of which 7 were waited for; matrix products, arithmetic and copies ran while one was open for 1% of the time, Pallas kernels for 1%

profile of v2, /device:TPU:6, one launch (start us, length us, event | category | flops | bytes accessed | tf_op | source)
XLA Modules:
  0.0 199.5 jit_solution(6045798707099978845)
XLA Ops:
  7.2 0.0 all-gather.3.cloned.1.call-start
  7.2 0.7 all-gather.3.cloned.1.call-update
  7.9 0.0 copy-start.4
  7.9 0.0 copy-start.5
  7.9 2.7 %constant_dynamic-slice_fusion = (bf16[128,2048]{1,0:T(8,128)(2,1)S(1)}, bf16[128,2048]{1,0:T(8,128)(2,1)}, bf16[128,2048]{1,0:T(8,128)(2,1)S(1)}, bf16[128,2048]{1,0:T(8,128)(2,1)}) fusion(bf16[128,8192]{1,0:T(8,128)(2,1)} %param.5, s32[]{:T(128)S(6)} %select_n.15, s32[]{:T(128)S(6)} %select_n.13, s32[]{:T(128)S(6)} %select_n.12, s32[]{:T(128)S(6)} %select_n.14), kind=kLoop, calls=%fused_computation.6 | loop fusion | bytes 4194320 | tf_op jit(solution)/shard_map/dynamic_slice | solution.py:216
  10.6 4.3 %collective-permute-start = (bf16[128,2048]{1,0:T(8,128)(2,1)}, bf16[128,2048]{1,0:T(8,128)(2,1)S(1)}, u32[]{:S(2)}, u32[]{:S(2)}) collective-permute-start(bf16[128,2048]{1,0:T(8,128)(2,1)} %get-tuple-element.78), channel_id=1, source_target_pairs={{0,2},{2,0},{4,6},{6,4},{1,3},{3,1},{5,7},{7,5},{8,10},{10,8},{12,... | collective-permute-start | bytes 1572872 | tf_op jit(solution)/shard_map/ppermute | solution.py:208
  14.9 6.1 %collective-permute-start.2 = (bf16[128,2048]{1,0:T(8,128)(2,1)}, bf16[128,2048]{1,0:T(8,128)(2,1)S(1)}, u32[]{:S(2)}, u32[]{:S(2)}) collective-permute-start(bf16[128,2048]{1,0:T(8,128)(2,1)} %get-tuple-element.80), channel_id=1, source_target_pairs={{0,4},{2,6},{4,0},{6,2},{1,5},{3,7},{5,1},{7,3},{8,12},{10,14},{12... | collective-permute-start | bytes 1572872 | tf_op jit(solution)/shard_map/ppermute | solution.py:208
  21.0 0.2 shard_map.76
  21.2 1.9 collective-permute-start.4
  23.1 1.9 collective-permute-start.5
  25.1 0.0 copy-done.4
  25.1 0.0 copy-done.5
  25.1 8.7 %collective-permute-start.1 = (f32[2,16,512]{2,1,0:T(8,128)S(1)}, f32[2,16,512]{2,1,0:T(8,128)S(1)}, u32[]{:S(2)}, u32[]{:S(2)}) collective-permute-start(f32[2,16,512]{2,1,0:T(8,128)S(1)} %constant_dynamic-update-slice_fusion.am_ref), channel_id=1, source_target_pairs={{0,32},{32,0},{1,33},{33,1},{2,34},{34,2},{3,35},{35,3},{4,36},{36... | collective-permute-start | bytes 196616 | tf_op jit(solution)/shard_map/ppermute | solution.py:221
  33.9 0.0 all-gather.3.cloned.1.call-done
  33.9 0.0 copy-start
  33.9 1.6 copy-done
  35.5 0.4 shard_map.77.a_ref
  35.9 0.0 copy-start.1
  35.9 24.3 %collective-permute-done.1.pam_ref = f32[2,16,512]{2,1,0:T(8,128)S(1)} collective-permute-done((f32[2,16,512]{2,1,0:T(8,128)S(1)}, f32[2,16,512]{2,1,0:T(8,128)S(1)}, u32[]{:S(2)}, u32[]{:S(2)}) %collective-permute-start.1) | collective-permute-done | bytes 65568 | tf_op jit(solution)/shard_map/ppermute | solution.py:221
  60.2 0.0 collective-permute-done.x_ref
  60.2 0.4 shard_map.79
  60.7 1.9 collective-permute-start.3
  62.6 0.2 shard_map.78
  62.8 1.9 collective-permute-start.7
  64.8 0.0 collective-permute-done.4.refs_4_
  64.8 0.0 collective-permute-done.2.x_ref
  64.8 2.8 %collective-permute-done.3.b_ref = bf16[128,512]{1,0:T(8,128)(2,1)S(1)} collective-permute-done((bf16[128,512]{1,0:T(8,128)(2,1)S(1)}, bf16[128,512]{1,0:T(8,128)(2,1)S(1)}, u32[]{:S(2)}, u32[]{:S(2)}) %collective-permute-start.3) | collective-permute-done | bytes 131104 | tf_op jit(solution)/shard_map/ppermute | solution.py:208
  67.6 0.0 copy-done.1
  67.6 0.4 shard_map.81
  68.0 0.0 copy-start.3
  68.0 3.0 %collective-permute-start.6 = (bf16[128,512]{1,0:T(8,128)(2,1)S(1)}, bf16[128,512]{1,0:T(8,128)(2,1)S(1)}, u32[]{:S(2)}, u32[]{:S(2)}) collective-permute-start(bf16[128,512]{1,0:T(8,128)(2,1)S(1)} %shard_map.81), channel_id=1, source_target_pairs={{0,4},{2,6},{4,0},{6,2},{1,5},{3,7},{5,1},{7,3},{8,12},{10,14},{12... | collective-permute-start | bytes 393224 | tf_op jit(solution)/shard_map/ppermute | solution.py:208
  71.0 0.2 shard_map.80
  71.2 0.0 copy-start.2
  71.2 2.1 %collective-permute-start.9 = (bf16[1024,128]{1,0:T(8,128)(2,1)S(1)}, bf16[1024,128]{1,0:T(8,128)(2,1)S(1)}, u32[]{:S(2)}, u32[]{:S(2)}) collective-permute-start(bf16[1024,128]{1,0:T(8,128)(2,1)S(1)} %get-tuple-element.59), channel_id=1, source_target_pairs={{0,1},{1,0},{2,3},{3,2},{4,5},{5,4},{6,7},{7,6},{8,9},{9,8},{10,11... | collective-permute-start | bytes 786440 | tf_op jit(solution)/shard_map/ppermute | solution.py:230
  73.3 0.0 collective-permute-done.5.x_ref
  73.3 0.0 collective-permute-done.7.refs_5_
  73.3 3.9 %collective-permute-done.6.c_ref = bf16[128,512]{1,0:T(8,128)(2,1)S(1)} collective-permute-done((bf16[128,512]{1,0:T(8,128)(2,1)S(1)}, bf16[128,512]{1,0:T(8,128)(2,1)S(1)}, u32[]{:S(2)}, u32[]{:S(2)}) %collective-permute-start.6) | collective-permute-done | bytes 131104 | tf_op jit(solution)/shard_map/ppermute | solution.py:208
  77.2 0.4 shard_map.82
  77.6 4.0 %collective-permute-start.8 = (bf16[128,512]{1,0:T(8,128)(2,1)S(1)}, bf16[128,512]{1,0:T(8,128)(2,1)S(1)}, u32[]{:S(2)}, u32[]{:S(2)}) collective-permute-start(bf16[128,512]{1,0:T(8,128)(2,1)S(1)} %shard_map.82), channel_id=1, source_target_pairs={{0,6},{2,4},{4,2},{6,0},{1,7},{3,5},{5,3},{7,1},{8,14},{10,12},{12... | collective-permute-start | bytes 393224 | tf_op jit(solution)/shard_map/ppermute | solution.py:208
  81.7 0.0 collective-permute-done.9.refs_6_
  81.7 4.6 %collective-permute-done.8.d_ref = bf16[128,512]{1,0:T(8,128)(2,1)S(1)} collective-permute-done((bf16[128,512]{1,0:T(8,128)(2,1)S(1)}, bf16[128,512]{1,0:T(8,128)(2,1)S(1)}, u32[]{:S(2)}, u32[]{:S(2)}) %collective-permute-start.8) | collective-permute-done | bytes 131104 | tf_op jit(solution)/shard_map/ppermute | solution.py:208
  86.3 0.0 copy-done.3
  86.3 0.2 shard_map.83
  86.5 1.9 collective-permute-start.11
  88.5 4.0 %collective-permute-start.13 = (bf16[128,512]{1,0:T(8,128)(2,1)S(1)}, bf16[128,512]{1,0:T(8,128)(2,1)S(1)}, u32[]{:S(2)}, u32[]{:S(2)}) collective-permute-start(bf16[128,512]{1,0:T(8,128)(2,1)S(1)} %shard_map.83), channel_id=1, source_target_pairs={{0,6},{2,4},{4,2},{6,0},{1,7},{3,5},{5,3},{7,1},{8,14},{10,12},{12... | collective-permute-start | bytes 393224 | tf_op jit(solution)/shard_map/ppermute | solution.py:208
  92.5 3.3 %collective-permute-start.12 = (bf16[128,512]{1,0:T(8,128)(2,1)S(1)}, bf16[128,512]{1,0:T(8,128)(2,1)S(1)}, u32[]{:S(2)}, u32[]{:S(2)}) collective-permute-start(bf16[128,512]{1,0:T(8,128)(2,1)S(1)} %shard_map.83), channel_id=1, source_target_pairs={{0,4},{2,6},{4,0},{6,2},{1,5},{3,7},{5,1},{7,3},{8,12},{10,14},{12... | collective-permute-start | bytes 393224 | tf_op jit(solution)/shard_map/ppermute | solution.py:208
  95.8 0.0 collective-permute-done.11
  95.8 7.3 %collective-permute-done.12 = bf16[128,512]{1,0:T(8,128)(2,1)S(1)} collective-permute-done((bf16[128,512]{1,0:T(8,128)(2,1)S(1)}, bf16[128,512]{1,0:T(8,128)(2,1)S(1)}, u32[]{:S(2)}, u32[]{:S(2)}) %collective-permute-start.12) | collective-permute-done | bytes 131104 | tf_op jit(solution)/shard_map/ppermute | solution.py:208
  103.1 0.0 collective-permute-done.13
  103.1 1.9 collective-permute-start.14
  105.1 0.2 shard_map.84
  105.3 2.4 %collective-permute-start.10 = (bf16[1024,128]{1,0:T(8,128)(2,1)S(1)}, bf16[1024,128]{1,0:T(8,128)(2,1)S(1)}, u32[]{:S(2)}, u32[]{:S(2)}) collective-permute-start(bf16[1024,128]{1,0:T(8,128)(2,1)S(1)} %get-tuple-element.69), channel_id=1, source_target_pairs={{0,1},{1,0},{2,3},{3,2},{4,5},{5,4},{6,7},{7,6},{8,9},{9,8},{10,11... | collective-permute-start | bytes 786440 | tf_op jit(solution)/shard_map/ppermute | solution.py:235
  107.7 1.1 collective-permute-done.10.refs_7_
  108.8 0.0 collective-permute-done.14.refs_9_
  108.8 0.0 copy-done.2
  108.8 1.8 shard_map.85.l_ref
  110.6 38.6 %all_to_all.10.l_ref = bf16[32,32,512]{2,1,0:T(8,128)(2,1)S(1)} all-to-all(bf16[32,32,512]{2,1,0:T(8,128)(2,1)S(1)} %bitcast.10), channel_id=1, replica_groups=mesh['y'=8,'zh'=2,'x'=4,'zl'=4,'core'=2] {'y','x'}, dimensions={0} | all-to-all | bytes 2097152 | tf_op jit(solution)/shard_map/all_to_all | solution.py:241
  149.2 0.2 shard_map.86
  149.4 6.9 %collective-permute-start.15 = (bf16[32,512]{1,0:T(8,128)(2,1)S(1)}, bf16[32,512]{1,0:T(8,128)(2,1)S(1)}, u32[]{:S(2)}, u32[]{:S(2)}) collective-permute-start(bf16[32,512]{1,0:T(8,128)(2,1)S(1)} %get-tuple-element.72), channel_id=1, source_target_pairs={{0,32},{32,0},{1,33},{33,1},{2,34},{34,2},{3,35},{35,3},{4,36},{36... | collective-permute-start | bytes 98312 | tf_op jit(solution)/shard_map/ppermute | solution.py:243
  156.2 3.2 %collective-permute-done.15.o_ref = bf16[32,512]{1,0:T(8,128)(2,1)S(1)} collective-permute-done((bf16[32,512]{1,0:T(8,128)(2,1)S(1)}, bf16[32,512]{1,0:T(8,128)(2,1)S(1)}, u32[]{:S(2)}, u32[]{:S(2)}) %collective-permute-start.15) | collective-permute-done | bytes 32800 | tf_op jit(solution)/shard_map/ppermute | solution.py:243
  159.4 0.6 shard_map.87
  160.0 30.9 %all_to_all.11 = bf16[32,32,512]{2,1,0:T(8,128)(2,1)S(1)} all-to-all(bf16[32,32,512]{2,1,0:T(8,128)(2,1)S(1)} %get-tuple-element.74), channel_id=1, replica_groups=mesh['y'=8,'zh'=2,'x'=4,'zl'=4,'core'=2] {'y','x'}, dimensions={0} | all-to-all | bytes 2097152 | tf_op jit(solution)/shard_map/all_to_all | solution.py:245
  191.0 1.7 shard_map.88
  (6 shorter events, 0.1 us)
Async XLA Ops:
  7.2 26.7 %all-gather.3.cloned.1.call-start = ((), (), s32[]{:S(2)}) async-start(), calls=%async_computation.2 | async-start | bytes 3145728 | tf_op jit(solution)/shard_map/all_gather | solution.py:217
  7.9 17.2 %copy-start.4 = (f32[1,16,512]{2,1,0:T(8,128)S(1)}, f32[1,16,512]{2,1,0:T(8,128)}, u32[]{:S(2)}) copy-start(f32[1,16,512]{2,1,0:T(8,128)} %param.8) | copy-start | bytes 98308
  7.9 17.2 %copy-start.5 = (f32[1,16,512]{2,1,0:T(8,128)S(1)}, f32[1,16,512]{2,1,0:T(8,128)}, u32[]{:S(2)}) copy-start(f32[1,16,512]{2,1,0:T(8,128)} %param.9) | copy-start | bytes 98308
  10.6 49.6 %collective-permute-start = (bf16[128,2048]{1,0:T(8,128)(2,1)}, bf16[128,2048]{1,0:T(8,128)(2,1)S(1)}, u32[]{:S(2)}, u32[]{:S(2)}) collective-permute-start(bf16[128,2048]{1,0:T(8,128)(2,1)} %get-tuple-element.78), channel_id=1, source_target_pairs={{0,2},{2,0},{4,6},{6,4},{1,3},{3,1},{5,7},{7,5},{8,10},{10,8},{12,... | collective-permute-start | bytes 1572872 | tf_op jit(solution)/shard_map/ppermute | solution.py:208
  14.9 49.8 %collective-permute-start.2 = (bf16[128,2048]{1,0:T(8,128)(2,1)}, bf16[128,2048]{1,0:T(8,128)(2,1)S(1)}, u32[]{:S(2)}, u32[]{:S(2)}) collective-permute-start(bf16[128,2048]{1,0:T(8,128)(2,1)} %get-tuple-element.80), channel_id=1, source_target_pairs={{0,4},{2,6},{4,0},{6,2},{1,5},{3,7},{5,1},{7,3},{8,12},{10,14},{12... | collective-permute-start | bytes 1572872 | tf_op jit(solution)/shard_map/ppermute | solution.py:208
  21.2 43.5 %collective-permute-start.4 = (bf16[1024,128]{1,0:T(8,128)(2,1)S(1)}, bf16[1024,128]{1,0:T(8,128)(2,1)S(1)}, u32[]{:S(2)}, u32[]{:S(2)}) collective-permute-start(bf16[1024,128]{1,0:T(8,128)(2,1)S(1)} %get-tuple-element.46), channel_id=1, source_target_pairs={{0,1},{1,0},{2,3},{3,2},{4,5},{5,4},{6,7},{7,6},{8,9},{9,8},{10,11... | collective-permute-start | bytes 786440 | tf_op jit(solution)/shard_map/ppermute | solution.py:230
  23.1 50.1 %collective-permute-start.5 = (bf16[128,2048]{1,0:T(8,128)(2,1)S(1)}, bf16[128,2048]{1,0:T(8,128)(2,1)S(1)}, u32[]{:S(2)}, u32[]{:S(2)}) collective-permute-start(bf16[128,2048]{1,0:T(8,128)(2,1)S(1)} %get-tuple-element.77), channel_id=1, source_target_pairs={{0,6},{2,4},{4,2},{6,0},{1,7},{3,5},{5,3},{7,1},{8,14},{10,12},{12... | collective-permute-start | bytes 1572872 | tf_op jit(solution)/shard_map/ppermute | solution.py:208
  25.1 35.1 %collective-permute-start.1 = (f32[2,16,512]{2,1,0:T(8,128)S(1)}, f32[2,16,512]{2,1,0:T(8,128)S(1)}, u32[]{:S(2)}, u32[]{:S(2)}) collective-permute-start(f32[2,16,512]{2,1,0:T(8,128)S(1)} %constant_dynamic-update-slice_fusion.am_ref), channel_id=1, source_target_pairs={{0,32},{32,0},{1,33},{33,1},{2,34},{34,2},{3,35},{35,3},{4,36},{36... | collective-permute-start | bytes 196616 | tf_op jit(solution)/shard_map/ppermute | solution.py:221
  33.9 1.6 copy-start
  35.9 31.6 %copy-start.1 = (bf16[1,2048,512]{2,1,0:T(8,128)(2,1)S(1)}, bf16[1,2048,512]{2,1,0:T(8,128)(2,1)}, u32[]{:S(2)}) copy-start(bf16[1,2048,512]{2,1,0:T(8,128)(2,1)} %all-gather.3.cloned.1.call-done) | copy-start | bytes 6291460
  60.7 6.9 %collective-permute-start.3 = (bf16[128,512]{1,0:T(8,128)(2,1)S(1)}, bf16[128,512]{1,0:T(8,128)(2,1)S(1)}, u32[]{:S(2)}, u32[]{:S(2)}) collective-permute-start(bf16[128,512]{1,0:T(8,128)(2,1)S(1)} %shard_map.79), channel_id=1, source_target_pairs={{0,2},{2,0},{4,6},{6,4},{1,3},{3,1},{5,7},{7,5},{8,10},{10,8},{12,... | collective-permute-start | bytes 393224 | tf_op jit(solution)/shard_map/ppermute | solution.py:208
  62.8 10.4 %collective-permute-start.7 = (bf16[1024,128]{1,0:T(8,128)(2,1)S(1)}, bf16[1024,128]{1,0:T(8,128)(2,1)S(1)}, u32[]{:S(2)}, u32[]{:S(2)}) collective-permute-start(bf16[1024,128]{1,0:T(8,128)(2,1)S(1)} %get-tuple-element.52), channel_id=1, source_target_pairs={{0,1},{1,0},{2,3},{3,2},{4,5},{5,4},{6,7},{7,6},{8,9},{9,8},{10,11... | collective-permute-start | bytes 786440 | tf_op jit(solution)/shard_map/ppermute | solution.py:230
  68.0 18.3 %copy-start.3 = (bf16[128,512]{1,0:T(8,128)(2,1)S(1)}, bf16[128,512]{1,0:T(8,128)(2,1)}, u32[]{:S(2)}) copy-start(bf16[128,512]{1,0:T(8,128)(2,1)} %g_ref.1) | copy-start | bytes 393220
  68.0 9.2 %collective-permute-start.6 = (bf16[128,512]{1,0:T(8,128)(2,1)S(1)}, bf16[128,512]{1,0:T(8,128)(2,1)S(1)}, u32[]{:S(2)}, u32[]{:S(2)}) collective-permute-start(bf16[128,512]{1,0:T(8,128)(2,1)S(1)} %shard_map.81), channel_id=1, source_target_pairs={{0,4},{2,6},{4,0},{6,2},{1,5},{3,7},{5,1},{7,3},{8,12},{10,14},{12... | collective-permute-start | bytes 393224 | tf_op jit(solution)/shard_map/ppermute | solution.py:208
  71.2 37.6 %copy-start.2 = (bf16[1,1024,512]{2,1,0:T(8,128)(2,1)S(1)}, bf16[1,1024,512]{2,1,0:T(8,128)(2,1)}, u32[]{:S(2)}) copy-start(bf16[1,1024,512]{2,1,0:T(8,128)(2,1)} %param.7) | copy-start | bytes 3145732
  71.2 10.5 %collective-permute-start.9 = (bf16[1024,128]{1,0:T(8,128)(2,1)S(1)}, bf16[1024,128]{1,0:T(8,128)(2,1)S(1)}, u32[]{:S(2)}, u32[]{:S(2)}) collective-permute-start(bf16[1024,128]{1,0:T(8,128)(2,1)S(1)} %get-tuple-element.59), channel_id=1, source_target_pairs={{0,1},{1,0},{2,3},{3,2},{4,5},{5,4},{6,7},{7,6},{8,9},{9,8},{10,11... | collective-permute-start | bytes 786440 | tf_op jit(solution)/shard_map/ppermute | solution.py:230
  77.6 8.7 %collective-permute-start.8 = (bf16[128,512]{1,0:T(8,128)(2,1)S(1)}, bf16[128,512]{1,0:T(8,128)(2,1)S(1)}, u32[]{:S(2)}, u32[]{:S(2)}) collective-permute-start(bf16[128,512]{1,0:T(8,128)(2,1)S(1)} %shard_map.82), channel_id=1, source_target_pairs={{0,6},{2,4},{4,2},{6,0},{1,7},{3,5},{5,3},{7,1},{8,14},{10,12},{12... | collective-permute-start | bytes 393224 | tf_op jit(solution)/shard_map/ppermute | solution.py:208
  86.5 9.3 %collective-permute-start.11 = (bf16[128,512]{1,0:T(8,128)(2,1)S(1)}, bf16[128,512]{1,0:T(8,128)(2,1)S(1)}, u32[]{:S(2)}, u32[]{:S(2)}) collective-permute-start(bf16[128,512]{1,0:T(8,128)(2,1)S(1)} %shard_map.83), channel_id=1, source_target_pairs={{0,2},{2,0},{4,6},{6,4},{1,3},{3,1},{5,7},{7,5},{8,10},{10,8},{12,... | collective-permute-start | bytes 393224 | tf_op jit(solution)/shard_map/ppermute | solution.py:208
  88.5 14.7 %collective-permute-start.13 = (bf16[128,512]{1,0:T(8,128)(2,1)S(1)}, bf16[128,512]{1,0:T(8,128)(2,1)S(1)}, u32[]{:S(2)}, u32[]{:S(2)}) collective-permute-start(bf16[128,512]{1,0:T(8,128)(2,1)S(1)} %shard_map.83), channel_id=1, source_target_pairs={{0,6},{2,4},{4,2},{6,0},{1,7},{3,5},{5,3},{7,1},{8,14},{10,12},{12... | collective-permute-start | bytes 393224 | tf_op jit(solution)/shard_map/ppermute | solution.py:208
  92.5 10.6 %collective-permute-start.12 = (bf16[128,512]{1,0:T(8,128)(2,1)S(1)}, bf16[128,512]{1,0:T(8,128)(2,1)S(1)}, u32[]{:S(2)}, u32[]{:S(2)}) collective-permute-start(bf16[128,512]{1,0:T(8,128)(2,1)S(1)} %shard_map.83), channel_id=1, source_target_pairs={{0,4},{2,6},{4,0},{6,2},{1,5},{3,7},{5,1},{7,3},{8,12},{10,14},{12... | collective-permute-start | bytes 393224 | tf_op jit(solution)/shard_map/ppermute | solution.py:208
  103.1 5.7 %collective-permute-start.14 = (bf16[512,512]{1,0:T(8,128)(2,1)S(1)}, bf16[512,512]{1,0:T(8,128)(2,1)S(1)}, u32[]{:S(2)}, u32[]{:S(2)}) collective-permute-start(bf16[512,512]{1,0:T(8,128)(2,1)S(1)} %constant_dynamic-update-slice_fusion.2.refs_8_), channel_id=1, source_target_pairs={{0,1},{1,0},{2,3},{3,2},{4,5},{5,4},{6,7},{7,6},{8,9},{9,8},{10,11... | collective-permute-start | bytes 1572872 | tf_op jit(solution)/shard_map/ppermute | solution.py:237
  105.3 3.6 %collective-permute-start.10 = (bf16[1024,128]{1,0:T(8,128)(2,1)S(1)}, bf16[1024,128]{1,0:T(8,128)(2,1)S(1)}, u32[]{:S(2)}, u32[]{:S(2)}) collective-permute-start(bf16[1024,128]{1,0:T(8,128)(2,1)S(1)} %get-tuple-element.69), channel_id=1, source_target_pairs={{0,1},{1,0},{2,3},{3,2},{4,5},{5,4},{6,7},{7,6},{8,9},{9,8},{10,11... | collective-permute-start | bytes 786440 | tf_op jit(solution)/shard_map/ppermute | solution.py:235
  149.4 10.0 %collective-permute-start.15 = (bf16[32,512]{1,0:T(8,128)(2,1)S(1)}, bf16[32,512]{1,0:T(8,128)(2,1)S(1)}, u32[]{:S(2)}, u32[]{:S(2)}) collective-permute-start(bf16[32,512]{1,0:T(8,128)(2,1)S(1)} %get-tuple-element.72), channel_id=1, source_target_pairs={{0,32},{32,0},{1,33},{33,1},{2,34},{34,2},{3,35},{35,3},{4,36},{36... | collective-permute-start | bytes 98312 | tf_op jit(solution)/shard_map/ppermute | solution.py:243
Sparse Core Ops, SparseCore 0:
  10.1 23.2 all-gather.2

commit v3 on v2

--- a/solution.py
+++ b/solution.py
@@ -89,40 +89,50 @@
     )(core.reshape(1), x)
 
 
-def inner_kernel(*refs):
-    *xs, ks_ref, ko_ref, w_ref, out_ref = refs
+def inner_kernel(x_ref, *refs):
+    *xs, ks_ref, ko_ref, w_ref, out0, out1, out2, out3, held_ref = refs
     x = jnp.concatenate([ref[...] for ref in xs], axis=1)
     k = jnp.concatenate([ks_ref[...], ko_ref[...]], axis=0)
     grad = jnp.dot(x, k, preferred_element_type=F32)
-    local = (w_ref[...].astype(F32) - ETA * grad).astype(BF)
-    ny, nx, nz, own, _ = out_ref.shape
-    for y in range(ny):
-        for z in range(nz):
-            for x in range(nx):
-                start = ((y * nz + z) * nx + x) * own
-                out_ref[y, x, z] = local[start : start + own]
-
-
-def inner_step(xs, k_same, k_other, w, block=256):
+    n, own, features = out0.shape
+    held_ref[...] = (w_ref[...].astype(F32) - ETA * grad).astype(BF).reshape(held_ref.shape)
+    for k, out in enumerate((out0, out1, out2, out3)):
+        out[...] = held_ref[:, x_ref[0] ^ k]
+
+
+def inner_step(x, xs, k_same, k_other, w, block=256):
     rows, features = w.shape
     half = k_same.shape[0]
     ny, nz, nx = SIZES[:3]
     own = rows // (ny * nz * nx)
-    by = block // (nz * nx * own)
+    part = block // (nx * own)
     return call(
         inner_kernel,
-        jax.ShapeDtypeStruct((ny, nx, nz, own, features), BF),
+        (jax.ShapeDtypeStruct((ny * nz, own, features), BF),) * nx,
         flops=4 * rows * half * features,
         moved=4 * (rows * half + w.size + k_same.size),
         grid=(rows // block,),
-        in_specs=[pl.BlockSpec((block, x.shape[1]), lambda i: (i, 0)) for x in xs]
+        in_specs=[pl.BlockSpec(memory_space=pltpu.SMEM)]
+        + [pl.BlockSpec((block, v.shape[1]), lambda i: (i, 0)) for v in xs]
         + [
             pl.BlockSpec((half, features), lambda i: (0, 0)),
             pl.BlockSpec((half, features), lambda i: (0, 0)),
             pl.BlockSpec((block, features), lambda i: (i, 0)),
         ],
-        out_specs=pl.BlockSpec((by, nx, nz, own, features), lambda i: (i, 0, 0, 0, 0)),
-    )(*xs, k_same, k_other, w)
+        out_specs=(pl.BlockSpec((part, own, features), lambda i: (i, 0, 0)),) * nx,
+        scratch_shapes=[pltpu.VMEM((part, nx, own, features), BF)],
+    )(x.reshape(1), *xs, k_same, k_other, w)
+
+
+def x_sum_kernel(a_ref, b_ref, c_ref, d_ref, out_ref):
+    total = a_ref[...].astype(F32) + b_ref[...].astype(F32)
+    total += c_ref[...].astype(F32)
+    total += d_ref[...].astype(F32)
+    out_ref[...] = total.astype(BF)
+
+
+def x_sum(shares):
+    return call(x_sum_kernel, jax.ShapeDtypeStruct(shares[0].shape, BF), moved=10 * shares[0].size)(*shares)
 
 
 def total_kernel(l_ref, out_ref, low_ref):
@@ -181,51 +191,49 @@
     )(zh.reshape(1), total, other, held, partner_held)
 
 
-def mix_kernel(l_ref, b_ref, out_ref):
-    mixed = (1.0 - MIX_RATE) * l_ref[...].astype(F32) + MIX_RATE * b_ref[...].astype(F32)
-    mixed = mixed.astype(BF)
-    ny, nx, nz, own, _ = l_ref.shape
-    for y in range(ny):
-        for z in range(nz):
-            for x in range(nx):
-                out_ref[0, pl.ds(((y * nz + z) * nx + x) * own, own)] = mixed[y, x, z]
-
-
-def mix(local, base, block=2):
-    ny, nx, nz, own, features = local.shape
-    rows = nx * nz * own
+def mix_kernel(x_ref, *refs):
+    *refs, out_ref = refs
+    n = len(refs) // 2
+    for k in range(n):
+        mixed = (1.0 - MIX_RATE) * refs[k][...].astype(F32) + MIX_RATE * refs[n + k][...].astype(F32)
+        out_ref[:, x_ref[0] ^ k] = mixed.astype(BF)
+
+
+def mix(x, locals_, bases, block=4):
+    n, own, features = locals_[0].shape
+    nx = len(locals_)
+    piece = pl.BlockSpec((block, own, features), lambda i: (i, 0, 0))
     return call(
         mix_kernel,
-        jax.ShapeDtypeStruct((1, ny * rows, features), BF),
-        moved=6 * local.size,
-        grid=(ny // block,),
-        in_specs=[pl.BlockSpec((block, nx, nz, own, features), lambda i: (i, 0, 0, 0, 0))] * 2,
-        out_specs=pl.BlockSpec((1, block * rows, features), lambda i: (0, i, 0)),
-    )(local, base)
-
-
-def across(value, k):
-    return lax.ppermute(value, "zl", [(i, i ^ k) for i in range(SIZES[3])])
+        jax.ShapeDtypeStruct((n, nx, own, features), BF),
+        moved=6 * nx * locals_[0].size,
+        grid=(n // block,),
+        in_specs=[pl.BlockSpec(memory_space=pltpu.SMEM)] + [piece] * (2 * nx),
+        out_specs=pl.BlockSpec((block, nx, own, features), lambda i: (i, 0, 0, 0)),
+    )(x.reshape(1), *locals_, *bases)
+
+
+def across(value, axis, k):
+    return lax.ppermute(value, axis, [(i, i ^ k) for i in range(4)])
 
 
 def body(tokens, cotangent, local_weights, anchor, momentum):
     own = local_weights[0]
     depth, features = own.shape
     width = tokens.shape[1] // SIZES[3]
-    core, zl, zh = (lax.axis_index(name) for name in ("core", "zl", "zh"))
-    chunk = [lax.dynamic_slice_in_dim(tokens, (zl ^ k) * width, width, 1) for k in range(4)]
+    core, zl, zh, x = (lax.axis_index(name) for name in ("core", "zl", "zh", "x"))
     chip_weights = lax.all_gather(own, "core", axis=0, tiled=True)
-    got = {k: across(chunk[k], k) for k in (3, 2, 1)}
-    got[0] = chunk[0]
-    held = jnp.concatenate([anchor, momentum], axis=0)
-    partner_held = lax.ppermute(held, "zh", SWAP)
-    made = project(got[0], chip_weights)
-    got[1], made, partner_held = lax.optimization_barrier((got[1], made, partner_held))
+    got, rest = {}, tokens
+    for k in (3, 2, 1, 0):
+        chunk = lax.dynamic_slice_in_dim(rest, (zl ^ k) * width, width, 1)
+        if k:
+            rest, chunk = lax.optimization_barrier((rest, chunk))
+        got[k] = across(chunk, "zl", k) if k else chunk
     mine, other = {}, {}
-    parts = [made]
+    parts = [project(got[0], chip_weights)]
     for k in (1, 2, 3):
         got[k], parts, other = lax.optimization_barrier((got[k], parts, other))
-        parts.append(across(project(got[k], chip_weights), k))
+        parts.append(across(project(got[k], chip_weights), "zl", k))
         mine[k - 1], send = split(core, got[k - 1])
         other[k - 1] = lax.ppermute(send, "core", SWAP)
     parts, other = lax.optimization_barrier((parts, other))
@@ -233,17 +241,22 @@
     got[3], key_grad = lax.optimization_barrier((got[3], key_grad))
     mine[3], send = split(core, got[3])
     other[3] = lax.ppermute(send, "core", SWAP)
-    k_same = jnp.concatenate([key_grad] + [across(key_grad, k) for k in (1, 2, 3)], axis=0)
+    k_same = jnp.concatenate([key_grad] + [across(key_grad, "zl", k) for k in (1, 2, 3)], axis=0)
     k_other = lax.ppermute(k_same, "core", SWAP)
     xs = [mine[k] for k in range(4)] + [other[k] for k in range(4)]
-    local = inner_step(xs, k_same, k_other, own)
-    ny, nx, nz, rows, _ = local.shape
-    shares = lax.all_to_all(local.reshape(ny * nx, nz * rows, features), ("y", "x"), 0, 0, tiled=True)
-    total, low = half_total(shares)
-    other = lax.ppermute(low, "zh", SWAP)
-    new_base, new_mom, spread = outer_step(zh, total, other, held, partner_held, ny * nx)
-    base = lax.all_to_all(spread, ("y", "x"), 0, 0, tiled=True).reshape(local.shape)
-    return mix(local, base), new_base, new_mom
+    locals_ = inner_step(x, xs, k_same, k_other, own)
+    held, first = lax.optimization_barrier((jnp.concatenate([anchor, momentum], axis=0), locals_[0]))
+    partner_held = lax.ppermute(held, "zh", SWAP)
+    shares = [first] + [across(locals_[k], "x", k) for k in (1, 2, 3)]
+    shares, partner_held = lax.optimization_barrier((shares, partner_held))
+    ny, nz = SIZES[:2]
+    sums = x_sum(shares).reshape(ny, -1, features)
+    total, low = half_total(lax.all_to_all(sums, "y", 0, 0, tiled=True))
+    partner_total = lax.ppermute(low, "zh", SWAP)
+    new_base, new_mom, spread = outer_step(zh, total, partner_total, held, partner_held, ny)
+    base = lax.all_to_all(spread, "y", 0, 0, tiled=True).reshape(first.shape)
+    bases = [base] + [across(base, "x", k) for k in (1, 2, 3)]
+    return mix(x, locals_, bases).reshape(1, depth, features), new_base, new_mom
 
 
 def solution(mesh):

time: 201 us -> 216 us (1.075)
  blocking collectives: 69.5 us -> 31.9 us
  starting transfers between devices: 56.2 us -> 80.1 us
  local copies, waits for them, and re-layouts: 4.37 us -> 23 us
  Pallas kernels: 7.06 us -> 14 us
  waiting for transfers between devices: 47.9 us -> 50.6 us
    all_to_all x2, blocking collectives: 69.5 us -> 31.9 us  [the longest x1 19.1 us: body(): total, low = half_total(lax.all_to_all(sums, 'y', 0, 0, tiled=True))]
    ppermute x10 -> x16, starting transfers between devices: 37.3 us -> 61.4 us  [the longest x15 52.9 us: across(): return lax.ppermute(value, axis, [(i, i ^ k) for i in range(4)])]
    ppermute x1, waiting for transfers between devices: 24.3 us -> 2.23 us  [body(): partner_held = lax.ppermute(held, 'zh', SWAP)]
    ppermute x10 -> x16, waiting for transfers between devices: 21.7 us -> 40 us  [the longest x15 38.2 us: across(): return lax.ppermute(value, axis, [(i, i ^ k) for i in range(4)])]
    unnamed x16 -> x61, local copies, waits for them, and re-layouts: 1.64 us -> 19.8 us
    all_gather x1, waiting for transfers between devices: 0.02 us -> 6.29 us  [body(): chip_weights = lax.all_gather(own, 'core', axis=0, tiled=True)]
    pallas_call x4, Pallas kernels: 0.77 us -> 4.27 us  [split(): call(split_kernel, (shape, shape), in_specs=[pl.BlockSpec(memory_space=pl...]
    pallas_call x2 -> x3, Pallas kernels: 3.48 us -> 4.95 us  [the longest x1 3.08 us: inner_step(): call(inner_kernel, (jax.ShapeDtypeStruct((ny * nz, own, features), BF),)...]
  transfers between devices with their start and end apart: 17 -> 23, of which waited for: 7 -> 14; matrix products, arithmetic and copies ran while one was open for 1% -> 2% of each run, Pallas kernels for 1% -> 4%
where the time goes in v3:
time: 216 us; the launch traced here: 214 us
  starting transfers between devices  80.1 us (37%)
  waiting for transfers between devices  50.6 us (23%)
  blocking collectives  31.9 us (15%)
  local copies, waits for them, and re-layouts  23 us (11%)
  between operations  14.5 us (7%)
  Pallas kernels  14 us (6%)
    ppermute x15, starting transfers between devices, across(): return lax.ppermute(value, axis, [(i, i ^ k) for i in range(4)])  52.9 us
    ppermute x15, waiting for transfers between devices, across(): return lax.ppermute(value, axis, [(i, i ^ k) for i in range(4)])  38.2 us
    unnamed x61, local copies, waits for them, and re-layouts  19.8 us
    all_to_all x1, blocking collectives, body(): total, low = half_total(lax.all_to_all(sums, 'y', 0, 0, tiled=True))  19.1 us
    all_to_all x1, blocking collectives, body(): base = lax.all_to_all(spread, 'y', 0, 0, tiled=True).reshape(first.shape)  12.9 us
    ppermute x1, starting transfers between devices, body(): partner_total = lax.ppermute(low, 'zh', SWAP)  8.47 us
    ppermute x1, starting transfers between devices, body(): partner_held = lax.ppermute(held, 'zh', SWAP)  8.47 us
    all_gather x1, waiting for transfers between devices, body(): chip_weights = lax.all_gather(own, 'core', axis=0, tiled=True)  6.29 us
  transfers between devices with their start and end apart: 23, of which 14 were waited for; matrix products, arithmetic and copies ran while one was open for 2% of the time, Pallas kernels for 4%

profile of v3, /device:TPU:6, one launch (start us, length us, event | category | flops | bytes accessed | tf_op | source)
XLA Modules:
  0.0 214.2 jit_solution(261867615752668474)
XLA Ops:
  7.9 0.8 copy-done
  8.8 0.8 constant_dynamic-slice_fusion.3
  9.6 0.8 constant_dynamic-slice_fusion.2
  10.4 0.8 constant_dynamic-slice_fusion.1
  11.3 4.3 %collective-permute-start = (bf16[128,2048]{1,0:T(8,128)(2,1)}, bf16[128,2048]{1,0:T(8,128)(2,1)}, u32[]{:S(2)}, u32[]{:S(2)}) collective-permute-start(bf16[128,2048]{1,0:T(8,128)(2,1)} %constant_dynamic-slice_fusion.1), channel_id=1, source_target_pairs={{0,2},{2,0},{4,6},{6,4},{1,3},{3,1},{5,7},{7,5},{8,10},{10,8},{12,... | collective-permute-start | bytes 1572872 | tf_op jit(solution)/shard_map/ppermute | solution.py:217
  15.5 6.1 %collective-permute-start.1 = (bf16[128,2048]{1,0:T(8,128)(2,1)}, bf16[128,2048]{1,0:T(8,128)(2,1)S(1)}, u32[]{:S(2)}, u32[]{:S(2)}) collective-permute-start(bf16[128,2048]{1,0:T(8,128)(2,1)} %constant_dynamic-slice_fusion.2), channel_id=1, source_target_pairs={{0,4},{2,6},{4,0},{6,2},{1,5},{3,7},{5,1},{7,3},{8,12},{10,14},{12... | collective-permute-start | bytes 1572872 | tf_op jit(solution)/shard_map/ppermute | solution.py:217
  21.6 1.9 collective-permute-start.4
  23.6 0.9 shard_map.76
  25.2 1.9 collective-permute-start.3
  27.1 6.3 %all-gather.3.cloned.1.call-done = bf16[1,2048,512]{2,1,0:T(8,128)(2,1)} async-done(((bf16[1,1024,512]{2,1,0:T(8,128)(2,1)}), bf16[1,2048,512]{2,1,0:T(8,128)(2,1)}) %all-gather.3.cloned.1.call-update) | async-done | bytes 2097168 | tf_op jit(solution)/shard_map/all_gather | solution.py:225
  33.4 1.6 copy-done.1
  35.5 1.4 collective-permute-done.x_ref
  36.8 1.5 shard_map.79
  38.3 2.4 %collective-permute-start.2 = (bf16[128,512]{1,0:T(8,128)(2,1)S(1)}, bf16[128,512]{1,0:T(8,128)(2,1)S(1)}, u32[]{:S(2)}, u32[]{:S(2)}) collective-permute-start(bf16[128,512]{1,0:T(8,128)(2,1)S(1)} %shard_map.79), channel_id=1, source_target_pairs={{0,2},{2,0},{4,6},{6,4},{1,3},{3,1},{5,7},{7,5},{8,10},{10,8},{12,... | collective-permute-start | bytes 393224 | tf_op jit(solution)/shard_map/ppermute | solution.py:217
  40.7 1.2 shard_map.78
  41.9 0.7 copy-done.8
  42.6 1.9 collective-permute-start.6
  44.6 12.5 %collective-permute-done.1.x_ref = bf16[128,2048]{1,0:T(8,128)(2,1)S(1)} collective-permute-done((bf16[128,2048]{1,0:T(8,128)(2,1)}, bf16[128,2048]{1,0:T(8,128)(2,1)S(1)}, u32[]{:S(2)}, u32[]{:S(2)}) %collective-permute-start.1) | collective-permute-done | bytes 524320 | tf_op jit(solution)/shard_map/ppermute | solution.py:217
  57.1 1.1 collective-permute-done.2.b_ref
  58.7 3.1 %collective-permute-start.5 = (bf16[128,512]{1,0:T(8,128)(2,1)S(1)}, bf16[128,512]{1,0:T(8,128)(2,1)S(1)}, u32[]{:S(2)}, u32[]{:S(2)}) collective-permute-start(bf16[128,512]{1,0:T(8,128)(2,1)S(1)} %shard_map.81), channel_id=1, source_target_pairs={{0,4},{2,6},{4,0},{6,2},{1,5},{3,7},{5,1},{7,3},{8,12},{10,14},{12... | collective-permute-start | bytes 393224 | tf_op jit(solution)/shard_map/ppermute | solution.py:217
  62.0 0.7 copy-done.12
  62.7 2.0 collective-permute-start.8
  64.8 0.7 copy-done.10
  65.5 7.4 %collective-permute-done.5.c_ref = bf16[128,512]{1,0:T(8,128)(2,1)S(1)} collective-permute-done((bf16[128,512]{1,0:T(8,128)(2,1)S(1)}, bf16[128,512]{1,0:T(8,128)(2,1)S(1)}, u32[]{:S(2)}, u32[]{:S(2)}) %collective-permute-start.5) | collective-permute-done | bytes 131104 | tf_op jit(solution)/shard_map/ppermute | solution.py:217
  72.9 1.5 shard_map.82
  74.4 4.3 %collective-permute-start.7 = (bf16[128,512]{1,0:T(8,128)(2,1)S(1)}, bf16[128,512]{1,0:T(8,128)(2,1)S(1)}, u32[]{:S(2)}, u32[]{:S(2)}) collective-permute-start(bf16[128,512]{1,0:T(8,128)(2,1)S(1)} %shard_map.82), channel_id=1, source_target_pairs={{0,6},{2,4},{4,2},{6,0},{1,7},{3,5},{5,3},{7,1},{8,14},{10,12},{12... | collective-permute-start | bytes 393224 | tf_op jit(solution)/shard_map/ppermute | solution.py:217
  78.7 0.7 copy-done.14
  79.4 3.8 %collective-permute-done.7.d_ref = bf16[128,512]{1,0:T(8,128)(2,1)S(1)} collective-permute-done((bf16[128,512]{1,0:T(8,128)(2,1)S(1)}, bf16[128,512]{1,0:T(8,128)(2,1)S(1)}, u32[]{:S(2)}, u32[]{:S(2)}) %collective-permute-start.7) | collective-permute-done | bytes 131104 | tf_op jit(solution)/shard_map/ppermute | solution.py:217
  83.4 2.5 %collective-permute-start.10 = (bf16[128,512]{1,0:T(8,128)(2,1)S(1)}, bf16[128,512]{1,0:T(8,128)(2,1)S(1)}, u32[]{:S(2)}, u32[]{:S(2)}) collective-permute-start(bf16[128,512]{1,0:T(8,128)(2,1)S(1)} %shard_map.83), channel_id=1, source_target_pairs={{0,2},{2,0},{4,6},{6,4},{1,3},{3,1},{5,7},{7,5},{8,10},{10,8},{12,... | collective-permute-start | bytes 393224 | tf_op jit(solution)/shard_map/ppermute | solution.py:217
  85.9 4.2 %collective-permute-start.11 = (bf16[128,512]{1,0:T(8,128)(2,1)S(1)}, bf16[128,512]{1,0:T(8,128)(2,1)S(1)}, u32[]{:S(2)}, u32[]{:S(2)}) collective-permute-start(bf16[128,512]{1,0:T(8,128)(2,1)S(1)} %shard_map.83), channel_id=1, source_target_pairs={{0,4},{2,6},{4,0},{6,2},{1,5},{3,7},{5,1},{7,3},{8,12},{10,14},{12... | collective-permute-start | bytes 393224 | tf_op jit(solution)/shard_map/ppermute | solution.py:217
  90.8 3.4 %collective-permute-start.12 = (bf16[128,512]{1,0:T(8,128)(2,1)S(1)}, bf16[128,512]{1,0:T(8,128)(2,1)S(1)}, u32[]{:S(2)}, u32[]{:S(2)}) collective-permute-start(bf16[128,512]{1,0:T(8,128)(2,1)S(1)} %shard_map.83), channel_id=1, source_target_pairs={{0,6},{2,4},{4,2},{6,0},{1,7},{3,5},{5,3},{7,1},{8,14},{10,12},{12... | collective-permute-start | bytes 393224 | tf_op jit(solution)/shard_map/ppermute | solution.py:217
  94.9 3.1 %collective-permute-done.11 = bf16[128,512]{1,0:T(8,128)(2,1)S(1)} collective-permute-done((bf16[128,512]{1,0:T(8,128)(2,1)S(1)}, bf16[128,512]{1,0:T(8,128)(2,1)S(1)}, u32[]{:S(2)}, u32[]{:S(2)}) %collective-permute-start.11) | collective-permute-done | bytes 131104 | tf_op jit(solution)/shard_map/ppermute | solution.py:217
  98.6 0.9 collective-permute-done.12
  100.2 1.9 collective-permute-start.13
  102.2 1.9 shard_map.84
  104.8 2.4 %collective-permute-start.9 = (bf16[1024,128]{1,0:T(8,128)(2,1)}, bf16[1024,128]{1,0:T(8,128)(2,1)S(1)}, u32[]{:S(2)}, u32[]{:S(2)}) collective-permute-start(bf16[1024,128]{1,0:T(8,128)(2,1)} %get-tuple-element.87), channel_id=1, source_target_pairs={{0,1},{1,0},{2,3},{3,2},{4,5},{5,4},{6,7},{7,6},{8,9},{9,8},{10,11... | collective-permute-start | bytes 786440 | tf_op jit(solution)/shard_map/ppermute | solution.py:243
  107.2 1.3 collective-permute-done.9.refs_7_
  109.2 0.9 copy-done.5
  110.2 0.9 copy-done.7
  111.1 0.9 copy-done.9
  112.1 0.9 copy-done.11
  113.0 0.9 copy-done.13
  114.0 0.9 copy-done.15
  114.9 0.9 copy-done.17
  115.9 0.9 copy-done.19
  116.8 3.1 %shard_map.85 = (bf16[16,16,512]{2,1,0:T(8,128)(2,1)S(1)}, bf16[16,16,512]{2,1,0:T(8,128)(2,1)S(1)}, bf16[16,16,512]{2,1,0:T(8,128)(2,1)S(1)}, bf16[16,16,512]{2,1,0:T(8,128)(2,1)S(1)}) custom-call(s32[1]{0:T(128)} %bitcast.x_ref, bf16[1024,128]{1,0:T(8,128)(2,1)S(1)} %copy-done.5, bf16[1024,128]{1,0:T(8,128)(2,1)S(1)} %copy-done.9, ...), custom_call_target="tpu_custom_call" | custom-call | flops 1073741824 | bytes 5242880 | tf_op jit(solution)/shard_map/pallas_call | solution.py:109
  120.0 2.7 %collective-permute-start.14 = (bf16[16,16,512]{2,1,0:T(8,128)(2,1)S(1)}, bf16[16,16,512]{2,1,0:T(8,128)(2,1)S(1)}, u32[]{:S(2)}, u32[]{:S(2)}) collective-permute-start(bf16[16,16,512]{2,1,0:T(8,128)(2,1)S(1)} %get-tuple-element.90.refs_1_), channel_id=1, source_target_pairs={{0,8},{8,0},{16,24},{24,16},{1,9},{9,1},{17,25},{25,17},{2,10},{10... | collective-permute-start | bytes 786440 | tf_op jit(solution)/shard_map/ppermute | solution.py:217
  122.7 2.9 %collective-permute-start.15 = (bf16[16,16,512]{2,1,0:T(8,128)(2,1)S(1)}, bf16[16,16,512]{2,1,0:T(8,128)(2,1)S(1)}, u32[]{:S(2)}, u32[]{:S(2)}) collective-permute-start(bf16[16,16,512]{2,1,0:T(8,128)(2,1)S(1)} %get-tuple-element.91.refs_2_), channel_id=1, source_target_pairs={{0,16},{8,24},{16,0},{24,8},{1,17},{9,25},{17,1},{25,9},{2,18},{10... | collective-permute-start | bytes 786440 | tf_op jit(solution)/shard_map/ppermute | solution.py:217
  125.6 4.8 %collective-permute-start.16 = (bf16[16,16,512]{2,1,0:T(8,128)(2,1)S(1)}, bf16[16,16,512]{2,1,0:T(8,128)(2,1)S(1)}, u32[]{:S(2)}, u32[]{:S(2)}) collective-permute-start(bf16[16,16,512]{2,1,0:T(8,128)(2,1)S(1)} %get-tuple-element.92.refs_3_), channel_id=1, source_target_pairs={{0,24},{8,16},{16,8},{24,0},{1,25},{9,17},{17,9},{25,1},{2,26},{10... | collective-permute-start | bytes 786440 | tf_op jit(solution)/shard_map/ppermute | solution.py:217
  130.5 8.5 %collective-permute-start.17 = (f32[2,16,512]{2,1,0:T(8,128)S(1)}, f32[2,16,512]{2,1,0:T(8,128)S(1)}, u32[]{:S(2)}, u32[]{:S(2)}) collective-permute-start(f32[2,16,512]{2,1,0:T(8,128)S(1)} %pad_maximum_fusion.am_ref), channel_id=1, source_target_pairs={{0,32},{32,0},{1,33},{33,1},{2,34},{34,2},{3,35},{35,3},{4,36},{36... | collective-permute-start | bytes 196616 | tf_op jit(solution)/shard_map/ppermute | solution.py:249
  138.9 2.2 %collective-permute-done.17.pam_ref = f32[2,16,512]{2,1,0:T(8,128)S(1)} collective-permute-done((f32[2,16,512]{2,1,0:T(8,128)S(1)}, f32[2,16,512]{2,1,0:T(8,128)S(1)}, u32[]{:S(2)}, u32[]{:S(2)}) %collective-permute-start.17) | collective-permute-done | bytes 65568 | tf_op jit(solution)/shard_map/ppermute | solution.py:249
  141.6 19.1 %all_to_all.10.l_ref = bf16[8,32,512]{2,1,0:T(8,128)(2,1)S(1)} all-to-all(bf16[8,32,512]{2,1,0:T(8,128)(2,1)S(1)} %bitcast.13), channel_id=1, replica_groups=mesh['y'=8,'zh'=2,'x'=4,'zl'=4,'core'=2] {'y'}, dimensions={0} | all-to-all | bytes 524288 | tf_op jit(solution)/shard_map/all_to_all | solution.py:254
  160.8 8.5 %collective-permute-start.18 = (bf16[32,512]{1,0:T(8,128)(2,1)S(1)}, bf16[32,512]{1,0:T(8,128)(2,1)S(1)}, u32[]{:S(2)}, u32[]{:S(2)}) collective-permute-start(bf16[32,512]{1,0:T(8,128)(2,1)S(1)} %get-tuple-element.100), channel_id=1, source_target_pairs={{0,32},{32,0},{1,33},{33,1},{2,34},{34,2},{3,35},{35,3},{4,36},{36... | collective-permute-start | bytes 98312 | tf_op jit(solution)/shard_map/ppermute | solution.py:255
  169.2 1.9 collective-permute-done.18.o_ref
  171.8 12.9 %all_to_all.11 = bf16[8,32,512]{2,1,0:T(8,128)(2,1)S(1)} all-to-all(bf16[8,32,512]{2,1,0:T(8,128)(2,1)S(1)} %get-tuple-element.102), channel_id=1, replica_groups=mesh['y'=8,'zh'=2,'x'=4,'zl'=4,'core'=2] {'y'}, dimensions={0} | all-to-all | bytes 524288 | tf_op jit(solution)/shard_map/all_to_all | solution.py:257
  184.6 1.9 collective-permute-start.19
  186.5 6.1 %collective-permute-start.20 = (bf16[16,16,512]{2,1,0:T(8,128)(2,1)S(1)}, bf16[16,16,512]{2,1,0:T(8,128)(2,1)S(1)}, u32[]{:S(2)}, u32[]{:S(2)}) collective-permute-start(bf16[16,16,512]{2,1,0:T(8,128)(2,1)S(1)} %bitcast.15), channel_id=1, source_target_pairs={{0,16},{8,24},{16,0},{24,8},{1,17},{9,25},{17,1},{25,9},{2,18},{10... | collective-permute-start | bytes 786440 | tf_op jit(solution)/shard_map/ppermute | solution.py:217
  192.7 2.4 %collective-permute-start.21 = (bf16[16,16,512]{2,1,0:T(8,128)(2,1)S(1)}, bf16[16,16,512]{2,1,0:T(8,128)(2,1)S(1)}, u32[]{:S(2)}, u32[]{:S(2)}) collective-permute-start(bf16[16,16,512]{2,1,0:T(8,128)(2,1)S(1)} %bitcast.16), channel_id=1, source_target_pairs={{0,24},{8,16},{16,8},{24,0},{1,25},{9,17},{17,9},{25,1},{2,26},{10... | collective-permute-start | bytes 786440 | tf_op jit(solution)/shard_map/ppermute | solution.py:217
  195.1 4.0 %collective-permute-done.20.refs_6_ = bf16[16,16,512]{2,1,0:T(8,128)(2,1)S(1)} collective-permute-done((bf16[16,16,512]{2,1,0:T(8,128)(2,1)S(1)}, bf16[16,16,512]{2,1,0:T(8,128)(2,1)S(1)}, u32[]{:S(2)}, u32[]{:S(2)}) %collective-permute-start.20) | collective-permute-done | bytes 262176 | tf_op jit(solution)/shard_map/ppermute | solution.py:217
  199.1 3.7 %collective-permute-done.21.refs_7_ = bf16[16,16,512]{2,1,0:T(8,128)(2,1)S(1)} collective-permute-done((bf16[16,16,512]{2,1,0:T(8,128)(2,1)S(1)}, bf16[16,16,512]{2,1,0:T(8,128)(2,1)S(1)}, u32[]{:S(2)}, u32[]{:S(2)}) %collective-permute-start.21) | collective-permute-done | bytes 262176 | tf_op jit(solution)/shard_map/ppermute | solution.py:217
  202.7 0.9 copy-done.21
  203.7 0.9 copy-done.23
  204.6 0.9 copy-done.25
  205.6 1.7 shard_map.89
  (66 shorter events, 8.0 us)
Async XLA Ops:
  7.2 1.6 copy-start
  7.2 26.3 %all-gather.3.cloned.1.call-start = ((), (), s32[]{:S(2)}) async-start(), calls=%async_computation.2 | async-start | bytes 3145728 | tf_op jit(solution)/shard_map/all_gather | solution.py:225
  11.3 25.6 %collective-permute-start = (bf16[128,2048]{1,0:T(8,128)(2,1)}, bf16[128,2048]{1,0:T(8,128)(2,1)}, u32[]{:S(2)}, u32[]{:S(2)}) collective-permute-start(bf16[128,2048]{1,0:T(8,128)(2,1)} %constant_dynamic-slice_fusion.1), channel_id=1, source_target_pairs={{0,2},{2,0},{4,6},{6,4},{1,3},{3,1},{5,7},{7,5},{8,10},{10,8},{12,... | collective-permute-start | bytes 1572872 | tf_op jit(solution)/shard_map/ppermute | solution.py:217
  15.5 41.6 %collective-permute-start.1 = (bf16[128,2048]{1,0:T(8,128)(2,1)}, bf16[128,2048]{1,0:T(8,128)(2,1)S(1)}, u32[]{:S(2)}, u32[]{:S(2)}) collective-permute-start(bf16[128,2048]{1,0:T(8,128)(2,1)} %constant_dynamic-slice_fusion.2), channel_id=1, source_target_pairs={{0,4},{2,6},{4,0},{6,2},{1,5},{3,7},{5,1},{7,3},{8,12},{10,14},{12... | collective-permute-start | bytes 1572872 | tf_op jit(solution)/shard_map/ppermute | solution.py:217
  21.6 43.1 %collective-permute-start.4 = (bf16[128,2048]{1,0:T(8,128)(2,1)}, bf16[128,2048]{1,0:T(8,128)(2,1)}, u32[]{:S(2)}, u32[]{:S(2)}) collective-permute-start(bf16[128,2048]{1,0:T(8,128)(2,1)} %constant_dynamic-slice_fusion.3), channel_id=1, source_target_pairs={{0,6},{2,4},{4,2},{6,0},{1,7},{3,5},{5,3},{7,1},{8,14},{10,12},{12... | collective-permute-start | bytes 1572872 | tf_op jit(solution)/shard_map/ppermute | solution.py:217
  24.5 0.7 copy-start.4
  25.2 19.3 %collective-permute-start.3 = (bf16[1024,128]{1,0:T(8,128)(2,1)}, bf16[1024,128]{1,0:T(8,128)(2,1)S(1)}, u32[]{:S(2)}, u32[]{:S(2)}) collective-permute-start(bf16[1024,128]{1,0:T(8,128)(2,1)} %get-tuple-element.63), channel_id=1, source_target_pairs={{0,1},{1,0},{2,3},{3,2},{4,5},{5,4},{6,7},{7,6},{8,9},{9,8},{10,11... | collective-permute-start | bytes 786440 | tf_op jit(solution)/shard_map/ppermute | solution.py:238
  33.4 1.6 copy-start.1
  35.5 22.7 %copy-start.2 = (bf16[1,2048,512]{2,1,0:T(8,128)(2,1)S(1)}, bf16[1,2048,512]{2,1,0:T(8,128)(2,1)}, u32[]{:S(2)}) copy-start(bf16[1,2048,512]{2,1,0:T(8,128)(2,1)} %all-gather.3.cloned.1.call-done) | copy-start | bytes 6291460
  38.3 19.9 %collective-permute-start.2 = (bf16[128,512]{1,0:T(8,128)(2,1)S(1)}, bf16[128,512]{1,0:T(8,128)(2,1)S(1)}, u32[]{:S(2)}, u32[]{:S(2)}) collective-permute-start(bf16[128,512]{1,0:T(8,128)(2,1)S(1)} %shard_map.79), channel_id=1, source_target_pairs={{0,2},{2,0},{4,6},{6,4},{1,3},{3,1},{5,7},{7,5},{8,10},{10,8},{12,... | collective-permute-start | bytes 393224 | tf_op jit(solution)/shard_map/ppermute | solution.py:217
  41.9 0.7 copy-start.8
  42.6 22.1 %collective-permute-start.6 = (bf16[1024,128]{1,0:T(8,128)(2,1)S(1)}, bf16[1024,128]{1,0:T(8,128)(2,1)S(1)}, u32[]{:S(2)}, u32[]{:S(2)}) collective-permute-start(bf16[1024,128]{1,0:T(8,128)(2,1)S(1)} %get-tuple-element.70), channel_id=1, source_target_pairs={{0,1},{1,0},{2,3},{3,2},{4,5},{5,4},{6,7},{7,6},{8,9},{9,8},{10,11... | collective-permute-start | bytes 786440 | tf_op jit(solution)/shard_map/ppermute | solution.py:238
  44.6 29.8 %copy-start.6 = (bf16[1024,128]{1,0:T(8,128)(2,1)}, bf16[1024,128]{1,0:T(8,128)(2,1)S(1)}, u32[]{:S(2)}) copy-start(bf16[1024,128]{1,0:T(8,128)(2,1)S(1)} %collective-permute-done.3.refs_4_) | copy-start | bytes 786436
  58.7 24.5 %copy-start.26 = (bf16[128,512]{1,0:T(8,128)(2,1)S(1)}, bf16[128,512]{1,0:T(8,128)(2,1)}, u32[]{:S(2)}) copy-start(bf16[128,512]{1,0:T(8,128)(2,1)} %g_ref.1) | copy-start | bytes 393220
  58.7 14.2 %collective-permute-start.5 = (bf16[128,512]{1,0:T(8,128)(2,1)S(1)}, bf16[128,512]{1,0:T(8,128)(2,1)S(1)}, u32[]{:S(2)}, u32[]{:S(2)}) collective-permute-start(bf16[128,512]{1,0:T(8,128)(2,1)S(1)} %shard_map.81), channel_id=1, source_target_pairs={{0,4},{2,6},{4,0},{6,2},{1,5},{3,7},{5,1},{7,3},{8,12},{10,14},{12... | collective-permute-start | bytes 393224 | tf_op jit(solution)/shard_map/ppermute | solution.py:217
  61.9 0.7 copy-start.12
  62.7 46.6 %copy-start.3 = (bf16[1,1024,512]{2,1,0:T(8,128)(2,1)S(1)}, bf16[1,1024,512]{2,1,0:T(8,128)(2,1)}, u32[]{:S(2)}) copy-start(bf16[1,1024,512]{2,1,0:T(8,128)(2,1)} %param.7) | copy-start | bytes 3145732
  62.7 16.0 %collective-permute-start.8 = (bf16[1024,128]{1,0:T(8,128)(2,1)S(1)}, bf16[1024,128]{1,0:T(8,128)(2,1)S(1)}, u32[]{:S(2)}, u32[]{:S(2)}) collective-permute-start(bf16[1024,128]{1,0:T(8,128)(2,1)S(1)} %get-tuple-element.77), channel_id=1, source_target_pairs={{0,1},{1,0},{2,3},{3,2},{4,5},{5,4},{6,7},{7,6},{8,9},{9,8},{10,11... | collective-permute-start | bytes 786440 | tf_op jit(solution)/shard_map/ppermute | solution.py:238
  64.7 0.7 copy-start.10
  74.4 8.8 %collective-permute-start.7 = (bf16[128,512]{1,0:T(8,128)(2,1)S(1)}, bf16[128,512]{1,0:T(8,128)(2,1)S(1)}, u32[]{:S(2)}, u32[]{:S(2)}) collective-permute-start(bf16[128,512]{1,0:T(8,128)(2,1)S(1)} %shard_map.82), channel_id=1, source_target_pairs={{0,6},{2,4},{4,2},{6,0},{1,7},{3,5},{5,3},{7,1},{8,14},{10,12},{12... | collective-permute-start | bytes 393224 | tf_op jit(solution)/shard_map/ppermute | solution.py:217
  78.7 0.7 copy-start.14
  83.4 10.8 %collective-permute-start.10 = (bf16[128,512]{1,0:T(8,128)(2,1)S(1)}, bf16[128,512]{1,0:T(8,128)(2,1)S(1)}, u32[]{:S(2)}, u32[]{:S(2)}) collective-permute-start(bf16[128,512]{1,0:T(8,128)(2,1)S(1)} %shard_map.83), channel_id=1, source_target_pairs={{0,2},{2,0},{4,6},{6,4},{1,3},{3,1},{5,7},{7,5},{8,10},{10,8},{12,... | collective-permute-start | bytes 393224 | tf_op jit(solution)/shard_map/ppermute | solution.py:217
  85.9 12.1 %collective-permute-start.11 = (bf16[128,512]{1,0:T(8,128)(2,1)S(1)}, bf16[128,512]{1,0:T(8,128)(2,1)S(1)}, u32[]{:S(2)}, u32[]{:S(2)}) collective-permute-start(bf16[128,512]{1,0:T(8,128)(2,1)S(1)} %shard_map.83), channel_id=1, source_target_pairs={{0,4},{2,6},{4,0},{6,2},{1,5},{3,7},{5,1},{7,3},{8,12},{10,14},{12... | collective-permute-start | bytes 393224 | tf_op jit(solution)/shard_map/ppermute | solution.py:217
  90.8 8.8 %collective-permute-start.12 = (bf16[128,512]{1,0:T(8,128)(2,1)S(1)}, bf16[128,512]{1,0:T(8,128)(2,1)S(1)}, u32[]{:S(2)}, u32[]{:S(2)}) collective-permute-start(bf16[128,512]{1,0:T(8,128)(2,1)S(1)} %shard_map.83), channel_id=1, source_target_pairs={{0,6},{2,4},{4,2},{6,0},{1,7},{3,5},{5,3},{7,1},{8,14},{10,12},{12... | collective-permute-start | bytes 393224 | tf_op jit(solution)/shard_map/ppermute | solution.py:217
  100.2 9.0 %collective-permute-start.13 = (bf16[512,512]{1,0:T(8,128)(2,1)}, bf16[512,512]{1,0:T(8,128)(2,1)}, u32[]{:S(2)}, u32[]{:S(2)}) collective-permute-start(bf16[512,512]{1,0:T(8,128)(2,1)} %constant_dynamic-update-slice_fusion.refs_8_), channel_id=1, source_target_pairs={{0,1},{1,0},{2,3},{3,2},{4,5},{5,4},{6,7},{7,6},{8,9},{9,8},{10,11... | collective-permute-start | bytes 1572872 | tf_op jit(solution)/shard_map/ppermute | solution.py:245
  104.1 0.7 copy-start.16
  104.8 3.8 %collective-permute-start.9 = (bf16[1024,128]{1,0:T(8,128)(2,1)}, bf16[1024,128]{1,0:T(8,128)(2,1)S(1)}, u32[]{:S(2)}, u32[]{:S(2)}) collective-permute-start(bf16[1024,128]{1,0:T(8,128)(2,1)} %get-tuple-element.87), channel_id=1, source_target_pairs={{0,1},{1,0},{2,3},{3,2},{4,5},{5,4},{6,7},{7,6},{8,9},{9,8},{10,11... | collective-permute-start | bytes 786440 | tf_op jit(solution)/shard_map/ppermute | solution.py:243
  108.5 0.7 copy-start.18
  109.2 1.0 copy-start.5
  110.2 0.9 copy-start.7
  111.1 0.9 copy-start.9
  112.1 0.9 copy-start.11
  113.0 0.9 copy-start.13
  114.0 0.9 copy-start.15
  114.9 0.9 copy-start.17
  115.9 0.9 copy-start.19
  116.8 13.6 %copy-start.27 = (f32[1,16,512]{2,1,0:T(8,128)S(1)}, f32[1,16,512]{2,1,0:T(8,128)}, u32[]{:S(2)}) copy-start(f32[1,16,512]{2,1,0:T(8,128)} %param.9) | copy-start | bytes 98308
  116.8 13.6 %copy-start.28 = (f32[1,16,512]{2,1,0:T(8,128)S(1)}, f32[1,16,512]{2,1,0:T(8,128)}, u32[]{:S(2)}) copy-start(f32[1,16,512]{2,1,0:T(8,128)} %param.8) | copy-start | bytes 98308
  119.9 40.8 %copy-start.20 = (bf16[16,16,512]{2,1,0:T(8,128)(2,1)}, bf16[16,16,512]{2,1,0:T(8,128)(2,1)S(1)}, u32[]{:S(2)}) copy-start(bf16[16,16,512]{2,1,0:T(8,128)(2,1)S(1)} %get-tuple-element.90.refs_1_) | copy-start | bytes 786436
  119.9 40.8 %copy-start.22 = (bf16[16,16,512]{2,1,0:T(8,128)(2,1)}, bf16[16,16,512]{2,1,0:T(8,128)(2,1)S(1)}, u32[]{:S(2)}) copy-start(bf16[16,16,512]{2,1,0:T(8,128)(2,1)S(1)} %get-tuple-element.91.refs_2_) | copy-start | bytes 786436
  120.0 40.8 %copy-start.24 = (bf16[16,16,512]{2,1,0:T(8,128)(2,1)}, bf16[16,16,512]{2,1,0:T(8,128)(2,1)S(1)}, u32[]{:S(2)}) copy-start(bf16[16,16,512]{2,1,0:T(8,128)(2,1)S(1)} %get-tuple-element.92.refs_3_) | copy-start | bytes 786436
  120.0 21.2 %collective-permute-start.14 = (bf16[16,16,512]{2,1,0:T(8,128)(2,1)S(1)}, bf16[16,16,512]{2,1,0:T(8,128)(2,1)S(1)}, u32[]{:S(2)}, u32[]{:S(2)}) collective-permute-start(bf16[16,16,512]{2,1,0:T(8,128)(2,1)S(1)} %get-tuple-element.90.refs_1_), channel_id=1, source_target_pairs={{0,8},{8,0},{16,24},{24,16},{1,9},{9,1},{17,25},{25,17},{2,10},{10... | collective-permute-start | bytes 786440 | tf_op jit(solution)/shard_map/ppermute | solution.py:217
  122.7 18.5 %collective-permute-start.15 = (bf16[16,16,512]{2,1,0:T(8,128)(2,1)S(1)}, bf16[16,16,512]{2,1,0:T(8,128)(2,1)S(1)}, u32[]{:S(2)}, u32[]{:S(2)}) collective-permute-start(bf16[16,16,512]{2,1,0:T(8,128)(2,1)S(1)} %get-tuple-element.91.refs_2_), channel_id=1, source_target_pairs={{0,16},{8,24},{16,0},{24,8},{1,17},{9,25},{17,1},{25,9},{2,18},{10... | collective-permute-start | bytes 786440 | tf_op jit(solution)/shard_map/ppermute | solution.py:217
  125.6 15.8 %collective-permute-start.16 = (bf16[16,16,512]{2,1,0:T(8,128)(2,1)S(1)}, bf16[16,16,512]{2,1,0:T(8,128)(2,1)S(1)}, u32[]{:S(2)}, u32[]{:S(2)}) collective-permute-start(bf16[16,16,512]{2,1,0:T(8,128)(2,1)S(1)} %get-tuple-element.92.refs_3_), channel_id=1, source_target_pairs={{0,24},{8,16},{16,8},{24,0},{1,25},{9,17},{17,9},{25,1},{2,26},{10... | collective-permute-start | bytes 786440 | tf_op jit(solution)/shard_map/ppermute | solution.py:217
  130.5 10.7 %collective-permute-start.17 = (f32[2,16,512]{2,1,0:T(8,128)S(1)}, f32[2,16,512]{2,1,0:T(8,128)S(1)}, u32[]{:S(2)}, u32[]{:S(2)}) collective-permute-start(f32[2,16,512]{2,1,0:T(8,128)S(1)} %pad_maximum_fusion.am_ref), channel_id=1, source_target_pairs={{0,32},{32,0},{1,33},{33,1},{2,34},{34,2},{3,35},{35,3},{4,36},{36... | collective-permute-start | bytes 196616 | tf_op jit(solution)/shard_map/ppermute | solution.py:249
  160.8 10.4 %collective-permute-start.18 = (bf16[32,512]{1,0:T(8,128)(2,1)S(1)}, bf16[32,512]{1,0:T(8,128)(2,1)S(1)}, u32[]{:S(2)}, u32[]{:S(2)}) collective-permute-start(bf16[32,512]{1,0:T(8,128)(2,1)S(1)} %get-tuple-element.100), channel_id=1, source_target_pairs={{0,32},{32,0},{1,33},{33,1},{2,34},{34,2},{3,35},{35,3},{4,36},{36... | collective-permute-start | bytes 98312 | tf_op jit(solution)/shard_map/ppermute | solution.py:255
  184.6 10.4 %collective-permute-start.19 = (bf16[16,16,512]{2,1,0:T(8,128)(2,1)S(1)}, bf16[16,16,512]{2,1,0:T(8,128)(2,1)S(1)}, u32[]{:S(2)}, u32[]{:S(2)}) collective-permute-start(bf16[16,16,512]{2,1,0:T(8,128)(2,1)S(1)} %bitcast.14), channel_id=1, source_target_pairs={{0,8},{8,0},{16,24},{24,16},{1,9},{9,1},{17,25},{25,17},{2,10},{10... | collective-permute-start | bytes 786440 | tf_op jit(solution)/shard_map/ppermute | solution.py:217
  186.5 12.5 %collective-permute-start.20 = (bf16[16,16,512]{2,1,0:T(8,128)(2,1)S(1)}, bf16[16,16,512]{2,1,0:T(8,128)(2,1)S(1)}, u32[]{:S(2)}, u32[]{:S(2)}) collective-permute-start(bf16[16,16,512]{2,1,0:T(8,128)(2,1)S(1)} %bitcast.15), channel_id=1, source_target_pairs={{0,16},{8,24},{16,0},{24,8},{1,17},{9,25},{17,1},{25,9},{2,18},{10... | collective-permute-start | bytes 786440 | tf_op jit(solution)/shard_map/ppermute | solution.py:217
  192.7 10.0 %collective-permute-start.21 = (bf16[16,16,512]{2,1,0:T(8,128)(2,1)S(1)}, bf16[16,16,512]{2,1,0:T(8,128)(2,1)S(1)}, u32[]{:S(2)}, u32[]{:S(2)}) collective-permute-start(bf16[16,16,512]{2,1,0:T(8,128)(2,1)S(1)} %bitcast.16), channel_id=1, source_target_pairs={{0,24},{8,16},{16,8},{24,0},{1,25},{9,17},{17,9},{25,1},{2,26},{10... | collective-permute-start | bytes 786440 | tf_op jit(solution)/shard_map/ppermute | solution.py:217
  202.7 1.0 copy-start.21
  203.7 0.9 copy-start.23
  204.6 0.9 copy-start.25
Sparse Core Ops, SparseCore 0:
  10.1 23.2 all-gather.2

commit v4 on v3

--- a/solution.py
+++ b/solution.py
@@ -1,3 +1,5 @@
+import functools
+
 import jax
 import jax.numpy as jnp
 from jax import lax
@@ -20,7 +22,7 @@
 SWAP = [(0, 1), (1, 0)]
 BF = jnp.bfloat16
 F32 = jnp.float32
-LIMIT = 48 * 1024 * 1024
+LIMIT = 16 * 1024 * 1024
 
 
 def call(kernel, out_shape, flops=0, moved=0, **more):
@@ -31,6 +33,30 @@
         cost_estimate=pl.CostEstimate(flops=flops, bytes_accessed=moved, transcendentals=0),
         **more,
     )
+
+
+def slice_kernel(zl_ref, x_ref, *refs):
+    *outs, sems = refs
+    width = outs[0].shape[1]
+    copies = []
+    for k, out in enumerate(outs):
+        start = pl.multiple_of((zl_ref[0] ^ k) * width, width)
+        copies.append(pltpu.make_async_copy(x_ref.at[:, pl.ds(start, width)], out, sems.at[k]))
+    for copy in copies:
+        copy.start()
+    for copy in copies:
+        copy.wait()
+
+
+def slices(zl, tokens, n):
+    rows, width = tokens.shape
+    return call(
+        slice_kernel,
+        (jax.ShapeDtypeStruct((rows, width // n), BF),) * n,
+        in_specs=[pl.BlockSpec(memory_space=pltpu.SMEM), pl.BlockSpec(memory_space=pl.ANY)],
+        out_specs=(pl.BlockSpec(memory_space=pltpu.VMEM),) * n,
+        scratch_shapes=[pltpu.SemaphoreType.DMA((n,))],
+    )(zl.reshape(1), tokens)
 
 
 def project_kernel(x_ref, w_ref, out_ref):
@@ -69,59 +95,60 @@
     )(*parts, cotangent)
 
 
-def split_kernel(core_ref, x_ref, mine_ref, send_ref):
-    depth = mine_ref.shape[0]
-    mine = pl.ds(pl.multiple_of(core_ref[0] * depth, depth), depth)
-    other = pl.ds(pl.multiple_of((1 - core_ref[0]) * depth, depth), depth)
-    mine_ref[...] = x_ref[:, mine].T
-    send_ref[...] = x_ref[:, other].T
-
-
-def split(core, x):
-    rows, width = x.shape
-    shape = jax.ShapeDtypeStruct((width // 2, rows), BF)
+def flip_kernel(x_ref, out_ref):
+    out_ref[...] = x_ref[...].T
+
+
+def flip(x):
+    return call(flip_kernel, jax.ShapeDtypeStruct(x.shape[::-1], BF), moved=4 * x.size)(x)
+
+
+def grad_kernel(half_ref, *refs, block):
+    *refs, out_ref = refs
+    xs, ks = refs[: len(refs) // 2], refs[len(refs) // 2 :]
+    k = jnp.concatenate([ref[...] for ref in ks], axis=0)
+    depth = out_ref.shape[0]
+    for i in range(depth // block):
+        start = pl.multiple_of(half_ref[0] * depth + i * block, block)
+        x = jnp.concatenate([ref[pl.ds(start, block)] for ref in xs], axis=1)
+        grad = jnp.dot(x, k, preferred_element_type=F32)
+        out_ref[pl.ds(i * block, block)] = grad.astype(out_ref.dtype)
+
+
+def gradient(half, xs, ks, dtype, block=256):
+    depth, rows = xs[0].shape
+    features = ks[0].shape[1]
     vmem = pl.BlockSpec(memory_space=pltpu.VMEM)
     return call(
-        split_kernel,
-        (shape, shape),
-        in_specs=[pl.BlockSpec(memory_space=pltpu.SMEM), vmem],
-        out_specs=(vmem, vmem),
-    )(core.reshape(1), x)
-
-
-def inner_kernel(x_ref, *refs):
-    *xs, ks_ref, ko_ref, w_ref, out0, out1, out2, out3, held_ref = refs
-    x = jnp.concatenate([ref[...] for ref in xs], axis=1)
-    k = jnp.concatenate([ks_ref[...], ko_ref[...]], axis=0)
-    grad = jnp.dot(x, k, preferred_element_type=F32)
-    n, own, features = out0.shape
-    held_ref[...] = (w_ref[...].astype(F32) - ETA * grad).astype(BF).reshape(held_ref.shape)
-    for k, out in enumerate((out0, out1, out2, out3)):
-        out[...] = held_ref[:, x_ref[0] ^ k]
-
-
-def inner_step(x, xs, k_same, k_other, w, block=256):
+        functools.partial(grad_kernel, block=block),
+        jax.ShapeDtypeStruct((depth // 2, features), dtype),
+        flops=len(xs) * depth * rows * features,
+        in_specs=[pl.BlockSpec(memory_space=pltpu.SMEM)] + [vmem] * (2 * len(xs)),
+        out_specs=vmem,
+    )(half.reshape(1), *xs, *ks)
+
+
+def inner_kernel(x_ref, s_ref, o_ref, w_ref, *outs):
+    n, own, features = outs[0].shape
+    nx = len(outs)
+    for i in range(n):
+        for d, out in enumerate(outs):
+            rows = pl.ds(pl.multiple_of((i * nx + (x_ref[0] ^ d)) * own, own), own)
+            grad = s_ref[rows] + o_ref[rows].astype(F32)
+            out[i] = (w_ref[rows].astype(F32) - ETA * grad).astype(BF)
+
+
+def inner_step(x, same, other, w):
     rows, features = w.shape
-    half = k_same.shape[0]
     ny, nz, nx = SIZES[:3]
-    own = rows // (ny * nz * nx)
-    part = block // (nx * own)
+    vmem = pl.BlockSpec(memory_space=pltpu.VMEM)
     return call(
         inner_kernel,
-        (jax.ShapeDtypeStruct((ny * nz, own, features), BF),) * nx,
-        flops=4 * rows * half * features,
-        moved=4 * (rows * half + w.size + k_same.size),
-        grid=(rows // block,),
-        in_specs=[pl.BlockSpec(memory_space=pltpu.SMEM)]
-        + [pl.BlockSpec((block, v.shape[1]), lambda i: (i, 0)) for v in xs]
-        + [
-            pl.BlockSpec((half, features), lambda i: (0, 0)),
-            pl.BlockSpec((half, features), lambda i: (0, 0)),
-            pl.BlockSpec((block, features), lambda i: (i, 0)),
-        ],
-        out_specs=(pl.BlockSpec((part, own, features), lambda i: (i, 0, 0)),) * nx,
-        scratch_shapes=[pltpu.VMEM((part, nx, own, features), BF)],
-    )(x.reshape(1), *xs, k_same, k_other, w)
+        (jax.ShapeDtypeStruct((ny * nz, rows // (ny * nz * nx), features), BF),) * nx,
+        moved=8 * w.size,
+        in_specs=[pl.BlockSpec(memory_space=pltpu.SMEM)] + [vmem] * 3,
+        out_specs=(vmem,) * nx,
+    )(x.reshape(1), same, other, w)
 
 
 def x_sum_kernel(a_ref, b_ref, c_ref, d_ref, out_ref):
@@ -223,38 +250,35 @@
     width = tokens.shape[1] // SIZES[3]
     core, zl, zh, x = (lax.axis_index(name) for name in ("core", "zl", "zh", "x"))
     chip_weights = lax.all_gather(own, "core", axis=0, tiled=True)
-    got, rest = {}, tokens
-    for k in (3, 2, 1, 0):
-        chunk = lax.dynamic_slice_in_dim(rest, (zl ^ k) * width, width, 1)
-        if k:
-            rest, chunk = lax.optimization_barrier((rest, chunk))
-        got[k] = across(chunk, "zl", k) if k else chunk
-    mine, other = {}, {}
+    chunks = slices(zl, tokens, SIZES[3])
+    got = {k: across(chunks[k], "zl", k) for k in (3, 2, 1)}
+    got[0] = chunks[0]
+    held = jnp.concatenate([anchor, momentum], axis=0)
+    partner_held = lax.ppermute(held, "zh", SWAP)
     parts = [project(got[0], chip_weights)]
-    for k in (1, 2, 3):
-        got[k], parts, other = lax.optimization_barrier((got[k], parts, other))
-        parts.append(across(project(got[k], chip_weights), "zl", k))
-        mine[k - 1], send = split(core, got[k - 1])
-        other[k - 1] = lax.ppermute(send, "core", SWAP)
-    parts, other = lax.optimization_barrier((parts, other))
+    turned = {0: flip(got[0])}
+    got[1], parts[0], turned[0] = lax.optimization_barrier((got[1], parts[0], turned[0]))
+    parts.append(across(project(got[1], chip_weights), "zl", 1))
+    turned[1] = flip(got[1])
+    got[2], parts, turned = lax.optimization_barrier((got[2], parts, turned))
+    made = project(got[2], chip_weights)
+    parts.append(across(made, "zl", 2))
+    got[3], made, partner_held = lax.optimization_barrier((got[3], made, partner_held))
+    parts.append(across(project(got[3], chip_weights), "zl", 3))
+    turned[2], turned[3] = flip(got[2]), flip(got[3])
     key_grad = norm_grad(parts, cotangent)
-    got[3], key_grad = lax.optimization_barrier((got[3], key_grad))
-    mine[3], send = split(core, got[3])
-    other[3] = lax.ppermute(send, "core", SWAP)
-    k_same = jnp.concatenate([key_grad] + [across(key_grad, "zl", k) for k in (1, 2, 3)], axis=0)
-    k_other = lax.ppermute(k_same, "core", SWAP)
-    xs = [mine[k] for k in range(4)] + [other[k] for k in range(4)]
-    locals_ = inner_step(x, xs, k_same, k_other, own)
-    held, first = lax.optimization_barrier((jnp.concatenate([anchor, momentum], axis=0), locals_[0]))
-    partner_held = lax.ppermute(held, "zh", SWAP)
-    shares = [first] + [across(locals_[k], "x", k) for k in (1, 2, 3)]
-    shares, partner_held = lax.optimization_barrier((shares, partner_held))
+    ks = [key_grad] + [across(key_grad, "zl", k) for k in (1, 2, 3)]
+    xs = [turned[k] for k in range(4)]
+    send = gradient(1 - core, xs, ks, BF)
+    same = gradient(core, xs, ks, F32)
+    locals_ = inner_step(x, same, lax.ppermute(send, "core", SWAP), own)
+    shares = [locals_[0]] + [across(locals_[k], "x", k) for k in (1, 2, 3)]
     ny, nz = SIZES[:2]
     sums = x_sum(shares).reshape(ny, -1, features)
     total, low = half_total(lax.all_to_all(sums, "y", 0, 0, tiled=True))
     partner_total = lax.ppermute(low, "zh", SWAP)
     new_base, new_mom, spread = outer_step(zh, total, partner_total, held, partner_held, ny)
-    base = lax.all_to_all(spread, "y", 0, 0, tiled=True).reshape(first.shape)
+    base = lax.all_to_all(spread, "y", 0, 0, tiled=True).reshape(locals_[0].shape)
     bases = [base] + [across(base, "x", k) for k in (1, 2, 3)]
     return mix(x, locals_, bases).reshape(1, depth, features), new_base, new_mom
 

time: 216 us -> 201 us (0.931)
  local copies, waits for them, and re-layouts: 23 us -> 3.21 us
  waiting for transfers between devices: 50.6 us -> 57.7 us
  Pallas kernels: 14 us -> 10.5 us
  starting transfers between devices: 80.1 us -> 83.2 us
    unnamed x61 -> x15, local copies, waits for them, and re-layouts: 19.8 us -> 3.2 us
    ppermute x15, starting transfers between devices: 52.9 us -> 63.2 us  [across(): return lax.ppermute(value, axis, [(i, i ^ k) for i in range(4)])]
    ppermute x5 -> x1, starting transfers between devices: 10.2 us -> 1.91 us  [body(): locals_ = inner_step(x, same, lax.ppermute(send, 'core', SWAP), own)]
    all_gather x1, waiting for transfers between devices: 6.29 us -> 10.2 us  [body(): chip_weights = lax.all_gather(own, 'core', axis=0, tiled=True)]
    dynamic_slice x4 -> x0, local copies, waits for them, and re-layouts: 2.54 us -> none  [body(): chunk = lax.dynamic_slice_in_dim(rest, (zl ^ k) * width, width, 1)]
    ppermute x15, waiting for transfers between devices: 38.2 us -> 40.6 us  [across(): return lax.ppermute(value, axis, [(i, i ^ k) for i in range(4)])]
    pallas_call x5 -> x8, Pallas kernels: 7.34 us -> 5.94 us  [the longest x2 2.39 us: gradient(): call(functools.partial(grad_kernel, block=block), jax.ShapeDtypeStruct((d...]
  transfers between devices with their start and end apart: 23 -> 19, of which waited for: 14 -> 15; matrix products, arithmetic and copies ran while one was open for 2% -> 0% of each run, Pallas kernels for 4% -> 2%
where the time goes in v4:
time: 201 us; the launch traced here: 200 us
  starting transfers between devices  83.2 us (41%)
  waiting for transfers between devices  57.7 us (29%)
  blocking collectives  31 us (15%)
  between operations  14.4 us (7%)
  Pallas kernels  10.5 us (5%)
  local copies, waits for them, and re-layouts  3.21 us (2%)
    ppermute x15, starting transfers between devices, across(): return lax.ppermute(value, axis, [(i, i ^ k) for i in range(4)])  63.2 us
    ppermute x15, waiting for transfers between devices, across(): return lax.ppermute(value, axis, [(i, i ^ k) for i in range(4)])  40.6 us
    all_to_all x1, blocking collectives, body(): total, low = half_total(lax.all_to_all(sums, 'y', 0, 0, tiled=True))  18.1 us
    all_to_all x1, blocking collectives, body(): lax.all_to_all(spread, 'y', 0, 0, tiled=True).reshape(locals_[0].shape)  12.9 us
    all_gather x1, waiting for transfers between devices, body(): chip_weights = lax.all_gather(own, 'core', axis=0, tiled=True)  10.2 us
    ppermute x1, starting transfers between devices, body(): partner_total = lax.ppermute(low, 'zh', SWAP)  9.3 us
    ppermute x1, starting transfers between devices, body(): partner_held = lax.ppermute(held, 'zh', SWAP)  8.79 us
  transfers between devices with their start and end apart: 19, of which 15 were waited for; matrix products, arithmetic and copies ran while one was open for 0% of the time, Pallas kernels for 2%

profile of v4, /device:TPU:6, one launch (start us, length us, event | category | flops | bytes accessed | tf_op | source)
XLA Modules:
  0.0 200.0 jit_solution(6744128078905437852)
XLA Ops:
  7.2 0.0 copy-start.5
  7.2 0.0 all-gather.3.cloned.1.call-start
  7.2 0.7 all-gather.3.cloned.1.call-update
  7.9 1.6 copy-done.3
  9.5 1.2 shard_map.76
  10.7 4.3 %collective-permute-start.1 = (bf16[128,2048]{1,0:T(8,128)(2,1)S(1)}, bf16[128,2048]{1,0:T(8,128)(2,1)S(1)}, u32[]{:S(2)}, u32[]{:S(2)}) collective-permute-start(bf16[128,2048]{1,0:T(8,128)(2,1)S(1)} %get-tuple-element.27), channel_id=1, source_target_pairs={{0,2},{2,0},{4,6},{6,4},{1,3},{3,1},{5,7},{7,5},{8,10},{10,8},{12,... | collective-permute-start | bytes 1572872 | tf_op jit(solution)/shard_map/ppermute | solution.py:244
  15.0 6.1 %collective-permute-start = (bf16[128,2048]{1,0:T(8,128)(2,1)}, bf16[128,2048]{1,0:T(8,128)(2,1)S(1)}, u32[]{:S(2)}, u32[]{:S(2)}) collective-permute-start(bf16[128,2048]{1,0:T(8,128)(2,1)} %get-tuple-element.26), channel_id=1, source_target_pairs={{0,4},{2,6},{4,0},{6,2},{1,5},{3,7},{5,1},{7,3},{8,12},{10,14},{12... | collective-permute-start | bytes 1572872 | tf_op jit(solution)/shard_map/ppermute | solution.py:244
  21.1 1.9 collective-permute-start.3
  23.0 0.2 shard_map.78.refs_0_
  23.2 0.0 copy-done.5
  23.2 10.2 %all-gather.3.cloned.1.call-done = bf16[1,2048,512]{2,1,0:T(8,128)(2,1)} async-done(((bf16[1,1024,512]{2,1,0:T(8,128)(2,1)}), bf16[1,2048,512]{2,1,0:T(8,128)(2,1)}) %all-gather.3.cloned.1.call-update) | async-done | bytes 2097168 | tf_op jit(solution)/shard_map/all_gather | solution.py:252
  33.4 1.6 copy-done
  35.0 0.4 shard_map.77.a_ref
  35.5 0.0 copy-start.1
  35.5 0.3 collective-permute-done.1.x_ref
  35.8 0.4 shard_map.79
  36.2 3.4 %collective-permute-start.2 = (bf16[128,512]{1,0:T(8,128)(2,1)S(1)}, bf16[128,512]{1,0:T(8,128)(2,1)S(1)}, u32[]{:S(2)}, u32[]{:S(2)}) collective-permute-start(bf16[128,512]{1,0:T(8,128)(2,1)S(1)} %shard_map.79), channel_id=1, source_target_pairs={{0,2},{2,0},{4,6},{6,4},{1,3},{3,1},{5,7},{7,5},{8,10},{10,8},{12,... | collective-permute-start | bytes 393224 | tf_op jit(solution)/shard_map/ppermute | solution.py:244
  39.7 8.8 %collective-permute-start.4 = (f32[2,16,512]{2,1,0:T(8,128)S(1)}, f32[2,16,512]{2,1,0:T(8,128)S(1)}, u32[]{:S(2)}, u32[]{:S(2)}) collective-permute-start(f32[2,16,512]{2,1,0:T(8,128)S(1)} %constant_dynamic-update-slice_fusion.am_ref), channel_id=1, source_target_pairs={{0,32},{32,0},{1,33},{33,1},{2,34},{34,2},{3,35},{35,3},{4,36},{36... | collective-permute-start | bytes 196616 | tf_op jit(solution)/shard_map/ppermute | solution.py:257
  48.5 0.2 shard_map.80.refs_1_
  48.6 0.0 copy-start.4
  48.7 9.3 %collective-permute-done.x_ref = bf16[128,2048]{1,0:T(8,128)(2,1)S(1)} collective-permute-done((bf16[128,2048]{1,0:T(8,128)(2,1)}, bf16[128,2048]{1,0:T(8,128)(2,1)S(1)}, u32[]{:S(2)}, u32[]{:S(2)}) %collective-permute-start) | collective-permute-done | bytes 524320 | tf_op jit(solution)/shard_map/ppermute | solution.py:244
  58.0 1.1 collective-permute-done.2.b_ref
  59.1 0.4 shard_map.82
  59.6 2.1 %collective-permute-done.4.pam_ref = f32[2,16,512]{2,1,0:T(8,128)S(1)} collective-permute-done((f32[2,16,512]{2,1,0:T(8,128)S(1)}, f32[2,16,512]{2,1,0:T(8,128)S(1)}, u32[]{:S(2)}, u32[]{:S(2)}) %collective-permute-start.4) | collective-permute-done | bytes 65568 | tf_op jit(solution)/shard_map/ppermute | solution.py:257
  61.6 0.0 collective-permute-done.3.x_ref
  61.6 0.4 shard_map.84
  62.1 4.5 %collective-permute-start.6 = (bf16[128,512]{1,0:T(8,128)(2,1)S(1)}, bf16[128,512]{1,0:T(8,128)(2,1)S(1)}, u32[]{:S(2)}, u32[]{:S(2)}) collective-permute-start(bf16[128,512]{1,0:T(8,128)(2,1)S(1)} %shard_map.84), channel_id=1, source_target_pairs={{0,6},{2,4},{4,2},{6,0},{1,7},{3,5},{5,3},{7,1},{8,14},{10,12},{12... | collective-permute-start | bytes 393224 | tf_op jit(solution)/shard_map/ppermute | solution.py:244
  66.6 12.1 %collective-permute-start.5 = (bf16[128,512]{1,0:T(8,128)(2,1)S(1)}, bf16[128,512]{1,0:T(8,128)(2,1)S(1)}, u32[]{:S(2)}, u32[]{:S(2)}) collective-permute-start(bf16[128,512]{1,0:T(8,128)(2,1)S(1)} %shard_map.82), channel_id=1, source_target_pairs={{0,4},{2,6},{4,0},{6,2},{1,5},{3,7},{5,1},{7,3},{8,12},{10,14},{12... | collective-permute-start | bytes 393224 | tf_op jit(solution)/shard_map/ppermute | solution.py:244
  78.6 0.0 collective-permute-done.6.d_ref
  78.6 6.6 %collective-permute-done.5.c_ref = bf16[128,512]{1,0:T(8,128)(2,1)S(1)} collective-permute-done((bf16[128,512]{1,0:T(8,128)(2,1)S(1)}, bf16[128,512]{1,0:T(8,128)(2,1)S(1)}, u32[]{:S(2)}, u32[]{:S(2)}) %collective-permute-start.5) | collective-permute-done | bytes 131104 | tf_op jit(solution)/shard_map/ppermute | solution.py:244
  85.2 0.2 shard_map.85.refs_4_
  85.5 1.9 collective-permute-start.7
  87.4 4.8 %collective-permute-start.8 = (bf16[128,512]{1,0:T(8,128)(2,1)S(1)}, bf16[128,512]{1,0:T(8,128)(2,1)S(1)}, u32[]{:S(2)}, u32[]{:S(2)}) collective-permute-start(bf16[128,512]{1,0:T(8,128)(2,1)S(1)} %shard_map.85.refs_4_), channel_id=1, source_target_pairs={{0,4},{2,6},{4,0},{6,2},{1,5},{3,7},{5,1},{7,3},{8,12},{10,14},{12... | collective-permute-start | bytes 393224 | tf_op jit(solution)/shard_map/ppermute | solution.py:244
  92.2 3.4 %collective-permute-start.9 = (bf16[128,512]{1,0:T(8,128)(2,1)S(1)}, bf16[128,512]{1,0:T(8,128)(2,1)S(1)}, u32[]{:S(2)}, u32[]{:S(2)}) collective-permute-start(bf16[128,512]{1,0:T(8,128)(2,1)S(1)} %shard_map.85.refs_4_), channel_id=1, source_target_pairs={{0,6},{2,4},{4,2},{6,0},{1,7},{3,5},{5,3},{7,1},{8,14},{10,12},{12... | collective-permute-start | bytes 393224 | tf_op jit(solution)/shard_map/ppermute | solution.py:244
  95.6 0.2 shard_map.83.refs_3_
  95.8 0.2 shard_map.81.refs_2_
  96.0 0.0 collective-permute-done.7.refs_5_
  96.0 2.9 %collective-permute-done.8.refs_6_ = bf16[128,512]{1,0:T(8,128)(2,1)S(1)} collective-permute-done((bf16[128,512]{1,0:T(8,128)(2,1)S(1)}, bf16[128,512]{1,0:T(8,128)(2,1)S(1)}, u32[]{:S(2)}, u32[]{:S(2)}) %collective-permute-start.8) | collective-permute-done | bytes 131104 | tf_op jit(solution)/shard_map/ppermute | solution.py:244
  98.9 2.1 %collective-permute-done.9.refs_7_ = bf16[128,512]{1,0:T(8,128)(2,1)S(1)} collective-permute-done((bf16[128,512]{1,0:T(8,128)(2,1)S(1)}, bf16[128,512]{1,0:T(8,128)(2,1)S(1)}, u32[]{:S(2)}, u32[]{:S(2)}) %collective-permute-start.9) | collective-permute-done | bytes 131104 | tf_op jit(solution)/shard_map/ppermute | solution.py:244
  101.0 1.7 shard_map.87
  102.7 1.9 collective-permute-start.10
  104.6 0.0 copy-start.2
  104.6 0.7 shard_map.86.s_ref
  105.3 2.2 %collective-permute-done.10.o_ref = bf16[1024,512]{1,0:T(8,128)(2,1)} collective-permute-done((bf16[1024,512]{1,0:T(8,128)(2,1)}, bf16[1024,512]{1,0:T(8,128)(2,1)}, u32[]{:S(2)}, u32[]{:S(2)}) %collective-permute-start.10) | collective-permute-done | bytes 1048608 | tf_op jit(solution)/shard_map/ppermute | solution.py:274
  107.6 1.6 shard_map.88
  109.2 2.7 %collective-permute-start.11 = (bf16[16,16,512]{2,1,0:T(8,128)(2,1)S(1)}, bf16[16,16,512]{2,1,0:T(8,128)(2,1)S(1)}, u32[]{:S(2)}, u32[]{:S(2)}) collective-permute-start(bf16[16,16,512]{2,1,0:T(8,128)(2,1)S(1)} %get-tuple-element.40.refs_1_), channel_id=1, source_target_pairs={{0,8},{8,0},{16,24},{24,16},{1,9},{9,1},{17,25},{25,17},{2,10},{10... | collective-permute-start | bytes 786440 | tf_op jit(solution)/shard_map/ppermute | solution.py:244
  111.9 2.5 %collective-permute-start.12 = (bf16[16,16,512]{2,1,0:T(8,128)(2,1)S(1)}, bf16[16,16,512]{2,1,0:T(8,128)(2,1)S(1)}, u32[]{:S(2)}, u32[]{:S(2)}) collective-permute-start(bf16[16,16,512]{2,1,0:T(8,128)(2,1)S(1)} %get-tuple-element.41.refs_2_), channel_id=1, source_target_pairs={{0,16},{8,24},{16,0},{24,8},{1,17},{9,25},{17,1},{25,9},{2,18},{10... | collective-permute-start | bytes 786440 | tf_op jit(solution)/shard_map/ppermute | solution.py:244
  114.4 5.2 %collective-permute-start.13 = (bf16[16,16,512]{2,1,0:T(8,128)(2,1)S(1)}, bf16[16,16,512]{2,1,0:T(8,128)(2,1)S(1)}, u32[]{:S(2)}, u32[]{:S(2)}) collective-permute-start(bf16[16,16,512]{2,1,0:T(8,128)(2,1)S(1)} %get-tuple-element.42.refs_3_), channel_id=1, source_target_pairs={{0,24},{8,16},{16,8},{24,0},{1,25},{9,17},{17,9},{25,1},{2,26},{10... | collective-permute-start | bytes 786440 | tf_op jit(solution)/shard_map/ppermute | solution.py:244
  119.6 0.6 collective-permute-done.11.b_ref
  120.2 4.6 %collective-permute-done.12.c_ref = bf16[16,16,512]{2,1,0:T(8,128)(2,1)S(1)} collective-permute-done((bf16[16,16,512]{2,1,0:T(8,128)(2,1)S(1)}, bf16[16,16,512]{2,1,0:T(8,128)(2,1)S(1)}, u32[]{:S(2)}, u32[]{:S(2)}) %collective-permute-start.12) | collective-permute-done | bytes 262176 | tf_op jit(solution)/shard_map/ppermute | solution.py:244
  124.8 5.5 %collective-permute-done.13.d_ref = bf16[16,16,512]{2,1,0:T(8,128)(2,1)S(1)} collective-permute-done((bf16[16,16,512]{2,1,0:T(8,128)(2,1)S(1)}, bf16[16,16,512]{2,1,0:T(8,128)(2,1)S(1)}, u32[]{:S(2)}, u32[]{:S(2)}) %collective-permute-start.13) | collective-permute-done | bytes 262176 | tf_op jit(solution)/shard_map/ppermute | solution.py:244
  130.3 0.1 shard_map.89
  130.5 18.1 %all_to_all.10.l_ref = bf16[8,32,512]{2,1,0:T(8,128)(2,1)S(1)} all-to-all(bf16[8,32,512]{2,1,0:T(8,128)(2,1)S(1)} %bitcast.15), channel_id=1, replica_groups=mesh['y'=8,'zh'=2,'x'=4,'zl'=4,'core'=2] {'y'}, dimensions={0} | all-to-all | bytes 524288 | tf_op jit(solution)/shard_map/all_to_all | solution.py:278
  148.6 9.3 %collective-permute-start.14 = (bf16[32,512]{1,0:T(8,128)(2,1)S(1)}, bf16[32,512]{1,0:T(8,128)(2,1)S(1)}, u32[]{:S(2)}, u32[]{:S(2)}) collective-permute-start(bf16[32,512]{1,0:T(8,128)(2,1)S(1)} %get-tuple-element.44), channel_id=1, source_target_pairs={{0,32},{32,0},{1,33},{33,1},{2,34},{34,2},{3,35},{35,3},{4,36},{36... | collective-permute-start | bytes 98312 | tf_op jit(solution)/shard_map/ppermute | solution.py:279
  157.9 1.9 collective-permute-done.14.o_ref
  159.8 0.6 shard_map.91
  160.4 12.9 %all_to_all.11 = bf16[8,32,512]{2,1,0:T(8,128)(2,1)S(1)} all-to-all(bf16[8,32,512]{2,1,0:T(8,128)(2,1)S(1)} %get-tuple-element.46), channel_id=1, replica_groups=mesh['y'=8,'zh'=2,'x'=4,'zl'=4,'core'=2] {'y'}, dimensions={0} | all-to-all | bytes 524288 | tf_op jit(solution)/shard_map/all_to_all | solution.py:281
  173.3 1.9 collective-permute-start.15
  175.2 6.1 %collective-permute-start.16 = (bf16[16,16,512]{2,1,0:T(8,128)(2,1)S(1)}, bf16[16,16,512]{2,1,0:T(8,128)(2,1)S(1)}, u32[]{:S(2)}, u32[]{:S(2)}) collective-permute-start(bf16[16,16,512]{2,1,0:T(8,128)(2,1)S(1)} %bitcast.17), channel_id=1, source_target_pairs={{0,16},{8,24},{16,0},{24,8},{1,17},{9,25},{17,1},{25,9},{2,18},{10... | collective-permute-start | bytes 786440 | tf_op jit(solution)/shard_map/ppermute | solution.py:244
  181.3 2.4 %collective-permute-start.17 = (bf16[16,16,512]{2,1,0:T(8,128)(2,1)S(1)}, bf16[16,16,512]{2,1,0:T(8,128)(2,1)S(1)}, u32[]{:S(2)}, u32[]{:S(2)}) collective-permute-start(bf16[16,16,512]{2,1,0:T(8,128)(2,1)S(1)} %bitcast.18), channel_id=1, source_target_pairs={{0,24},{8,16},{16,8},{24,0},{1,25},{9,17},{17,9},{25,1},{2,26},{10... | collective-permute-start | bytes 786440 | tf_op jit(solution)/shard_map/ppermute | solution.py:244
  183.7 0.0 collective-permute-done.15.refs_5_
  183.7 4.0 %collective-permute-done.16.refs_6_ = bf16[16,16,512]{2,1,0:T(8,128)(2,1)S(1)} collective-permute-done((bf16[16,16,512]{2,1,0:T(8,128)(2,1)S(1)}, bf16[16,16,512]{2,1,0:T(8,128)(2,1)S(1)}, u32[]{:S(2)}, u32[]{:S(2)}) %collective-permute-start.16) | collective-permute-done | bytes 262176 | tf_op jit(solution)/shard_map/ppermute | solution.py:244
  187.7 3.7 %collective-permute-done.17.refs_7_ = bf16[16,16,512]{2,1,0:T(8,128)(2,1)S(1)} collective-permute-done((bf16[16,16,512]{2,1,0:T(8,128)(2,1)S(1)}, bf16[16,16,512]{2,1,0:T(8,128)(2,1)S(1)}, u32[]{:S(2)}, u32[]{:S(2)}) %collective-permute-start.17) | collective-permute-done | bytes 262176 | tf_op jit(solution)/shard_map/ppermute | solution.py:244
  191.4 1.8 shard_map.92
  (10 shorter events, 0.1 us)
Async XLA Ops:
  7.2 16.0 %copy-start.5 = (f32[1,16,512]{2,1,0:T(8,128)S(1)}, f32[1,16,512]{2,1,0:T(8,128)}, u32[]{:S(2)}) copy-start(f32[1,16,512]{2,1,0:T(8,128)} %param.8) | copy-start | bytes 98308
  7.2 26.3 %all-gather.3.cloned.1.call-start = ((), (), s32[]{:S(2)}) async-start(), calls=%async_computation.2 | async-start | bytes 3145728 | tf_op jit(solution)/shard_map/all_gather | solution.py:252
  7.9 1.6 copy-start.3
  10.7 25.1 %collective-permute-start.1 = (bf16[128,2048]{1,0:T(8,128)(2,1)S(1)}, bf16[128,2048]{1,0:T(8,128)(2,1)S(1)}, u32[]{:S(2)}, u32[]{:S(2)}) collective-permute-start(bf16[128,2048]{1,0:T(8,128)(2,1)S(1)} %get-tuple-element.27), channel_id=1, source_target_pairs={{0,2},{2,0},{4,6},{6,4},{1,3},{3,1},{5,7},{7,5},{8,10},{10,8},{12,... | collective-permute-start | bytes 1572872 | tf_op jit(solution)/shard_map/ppermute | solution.py:244
  15.0 43.0 %collective-permute-start = (bf16[128,2048]{1,0:T(8,128)(2,1)}, bf16[128,2048]{1,0:T(8,128)(2,1)S(1)}, u32[]{:S(2)}, u32[]{:S(2)}) collective-permute-start(bf16[128,2048]{1,0:T(8,128)(2,1)} %get-tuple-element.26), channel_id=1, source_target_pairs={{0,4},{2,6},{4,0},{6,2},{1,5},{3,7},{5,1},{7,3},{8,12},{10,14},{12... | collective-permute-start | bytes 1572872 | tf_op jit(solution)/shard_map/ppermute | solution.py:244
  21.1 40.6 %collective-permute-start.3 = (bf16[128,2048]{1,0:T(8,128)(2,1)}, bf16[128,2048]{1,0:T(8,128)(2,1)S(1)}, u32[]{:S(2)}, u32[]{:S(2)}) collective-permute-start(bf16[128,2048]{1,0:T(8,128)(2,1)} %get-tuple-element.35), channel_id=1, source_target_pairs={{0,6},{2,4},{4,2},{6,0},{1,7},{3,5},{5,3},{7,1},{8,14},{10,12},{12... | collective-permute-start | bytes 1572872 | tf_op jit(solution)/shard_map/ppermute | solution.py:244
  33.4 1.6 copy-start
  35.0 4.6 %copy-start.6 = (f32[1,16,512]{2,1,0:T(8,128)S(1)}, f32[1,16,512]{2,1,0:T(8,128)}, u32[]{:S(2)}) copy-start(f32[1,16,512]{2,1,0:T(8,128)} %param.9) | copy-start | bytes 98308
  35.5 23.6 %copy-start.1 = (bf16[1,2048,512]{2,1,0:T(8,128)(2,1)S(1)}, bf16[1,2048,512]{2,1,0:T(8,128)(2,1)}, u32[]{:S(2)}) copy-start(bf16[1,2048,512]{2,1,0:T(8,128)(2,1)} %all-gather.3.cloned.1.call-done) | copy-start | bytes 6291460
  36.2 22.9 %collective-permute-start.2 = (bf16[128,512]{1,0:T(8,128)(2,1)S(1)}, bf16[128,512]{1,0:T(8,128)(2,1)S(1)}, u32[]{:S(2)}, u32[]{:S(2)}) collective-permute-start(bf16[128,512]{1,0:T(8,128)(2,1)S(1)} %shard_map.79), channel_id=1, source_target_pairs={{0,2},{2,0},{4,6},{6,4},{1,3},{3,1},{5,7},{7,5},{8,10},{10,8},{12,... | collective-permute-start | bytes 393224 | tf_op jit(solution)/shard_map/ppermute | solution.py:244
  39.7 22.0 %collective-permute-start.4 = (f32[2,16,512]{2,1,0:T(8,128)S(1)}, f32[2,16,512]{2,1,0:T(8,128)S(1)}, u32[]{:S(2)}, u32[]{:S(2)}) collective-permute-start(f32[2,16,512]{2,1,0:T(8,128)S(1)} %constant_dynamic-update-slice_fusion.am_ref), channel_id=1, source_target_pairs={{0,32},{32,0},{1,33},{33,1},{2,34},{34,2},{3,35},{35,3},{4,36},{36... | collective-permute-start | bytes 196616 | tf_op jit(solution)/shard_map/ppermute | solution.py:257
  48.6 36.6 %copy-start.4 = (bf16[128,512]{1,0:T(8,128)(2,1)S(1)}, bf16[128,512]{1,0:T(8,128)(2,1)}, u32[]{:S(2)}) copy-start(bf16[128,512]{1,0:T(8,128)(2,1)} %g_ref.1) | copy-start | bytes 393220
  62.1 16.6 %collective-permute-start.6 = (bf16[128,512]{1,0:T(8,128)(2,1)S(1)}, bf16[128,512]{1,0:T(8,128)(2,1)S(1)}, u32[]{:S(2)}, u32[]{:S(2)}) collective-permute-start(bf16[128,512]{1,0:T(8,128)(2,1)S(1)} %shard_map.84), channel_id=1, source_target_pairs={{0,6},{2,4},{4,2},{6,0},{1,7},{3,5},{5,3},{7,1},{8,14},{10,12},{12... | collective-permute-start | bytes 393224 | tf_op jit(solution)/shard_map/ppermute | solution.py:244
  66.6 18.7 %collective-permute-start.5 = (bf16[128,512]{1,0:T(8,128)(2,1)S(1)}, bf16[128,512]{1,0:T(8,128)(2,1)S(1)}, u32[]{:S(2)}, u32[]{:S(2)}) collective-permute-start(bf16[128,512]{1,0:T(8,128)(2,1)S(1)} %shard_map.82), channel_id=1, source_target_pairs={{0,4},{2,6},{4,0},{6,2},{1,5},{3,7},{5,1},{7,3},{8,12},{10,14},{12... | collective-permute-start | bytes 393224 | tf_op jit(solution)/shard_map/ppermute | solution.py:244
  85.5 10.5 %collective-permute-start.7 = (bf16[128,512]{1,0:T(8,128)(2,1)S(1)}, bf16[128,512]{1,0:T(8,128)(2,1)S(1)}, u32[]{:S(2)}, u32[]{:S(2)}) collective-permute-start(bf16[128,512]{1,0:T(8,128)(2,1)S(1)} %shard_map.85.refs_4_), channel_id=1, source_target_pairs={{0,2},{2,0},{4,6},{6,4},{1,3},{3,1},{5,7},{7,5},{8,10},{10,8},{12,... | collective-permute-start | bytes 393224 | tf_op jit(solution)/shard_map/ppermute | solution.py:244
  87.4 11.5 %collective-permute-start.8 = (bf16[128,512]{1,0:T(8,128)(2,1)S(1)}, bf16[128,512]{1,0:T(8,128)(2,1)S(1)}, u32[]{:S(2)}, u32[]{:S(2)}) collective-permute-start(bf16[128,512]{1,0:T(8,128)(2,1)S(1)} %shard_map.85.refs_4_), channel_id=1, source_target_pairs={{0,4},{2,6},{4,0},{6,2},{1,5},{3,7},{5,1},{7,3},{8,12},{10,14},{12... | collective-permute-start | bytes 393224 | tf_op jit(solution)/shard_map/ppermute | solution.py:244
  92.2 8.8 %collective-permute-start.9 = (bf16[128,512]{1,0:T(8,128)(2,1)S(1)}, bf16[128,512]{1,0:T(8,128)(2,1)S(1)}, u32[]{:S(2)}, u32[]{:S(2)}) collective-permute-start(bf16[128,512]{1,0:T(8,128)(2,1)S(1)} %shard_map.85.refs_4_), channel_id=1, source_target_pairs={{0,6},{2,4},{4,2},{6,0},{1,7},{3,5},{5,3},{7,1},{8,14},{10,12},{12... | collective-permute-start | bytes 393224 | tf_op jit(solution)/shard_map/ppermute | solution.py:244
  102.7 4.9 %collective-permute-start.10 = (bf16[1024,512]{1,0:T(8,128)(2,1)}, bf16[1024,512]{1,0:T(8,128)(2,1)}, u32[]{:S(2)}, u32[]{:S(2)}) collective-permute-start(bf16[1024,512]{1,0:T(8,128)(2,1)} %shard_map.87), channel_id=1, source_target_pairs={{0,1},{1,0},{2,3},{3,2},{4,5},{5,4},{6,7},{7,6},{8,9},{9,8},{10,11... | collective-permute-start | bytes 3145736 | tf_op jit(solution)/shard_map/ppermute | solution.py:274
  104.6 3.0 %copy-start.2 = (bf16[1,1024,512]{2,1,0:T(8,128)(2,1)S(1)}, bf16[1,1024,512]{2,1,0:T(8,128)(2,1)}, u32[]{:S(2)}) copy-start(bf16[1,1024,512]{2,1,0:T(8,128)(2,1)} %param.7) | copy-start | bytes 3145732
  109.2 11.0 %collective-permute-start.11 = (bf16[16,16,512]{2,1,0:T(8,128)(2,1)S(1)}, bf16[16,16,512]{2,1,0:T(8,128)(2,1)S(1)}, u32[]{:S(2)}, u32[]{:S(2)}) collective-permute-start(bf16[16,16,512]{2,1,0:T(8,128)(2,1)S(1)} %get-tuple-element.40.refs_1_), channel_id=1, source_target_pairs={{0,8},{8,0},{16,24},{24,16},{1,9},{9,1},{17,25},{25,17},{2,10},{10... | collective-permute-start | bytes 786440 | tf_op jit(solution)/shard_map/ppermute | solution.py:244
  111.9 12.9 %collective-permute-start.12 = (bf16[16,16,512]{2,1,0:T(8,128)(2,1)S(1)}, bf16[16,16,512]{2,1,0:T(8,128)(2,1)S(1)}, u32[]{:S(2)}, u32[]{:S(2)}) collective-permute-start(bf16[16,16,512]{2,1,0:T(8,128)(2,1)S(1)} %get-tuple-element.41.refs_2_), channel_id=1, source_target_pairs={{0,16},{8,24},{16,0},{24,8},{1,17},{9,25},{17,1},{25,9},{2,18},{10... | collective-permute-start | bytes 786440 | tf_op jit(solution)/shard_map/ppermute | solution.py:244
  114.4 15.9 %collective-permute-start.13 = (bf16[16,16,512]{2,1,0:T(8,128)(2,1)S(1)}, bf16[16,16,512]{2,1,0:T(8,128)(2,1)S(1)}, u32[]{:S(2)}, u32[]{:S(2)}) collective-permute-start(bf16[16,16,512]{2,1,0:T(8,128)(2,1)S(1)} %get-tuple-element.42.refs_3_), channel_id=1, source_target_pairs={{0,24},{8,16},{16,8},{24,0},{1,25},{9,17},{17,9},{25,1},{2,26},{10... | collective-permute-start | bytes 786440 | tf_op jit(solution)/shard_map/ppermute | solution.py:244
  148.6 11.2 %collective-permute-start.14 = (bf16[32,512]{1,0:T(8,128)(2,1)S(1)}, bf16[32,512]{1,0:T(8,128)(2,1)S(1)}, u32[]{:S(2)}, u32[]{:S(2)}) collective-permute-start(bf16[32,512]{1,0:T(8,128)(2,1)S(1)} %get-tuple-element.44), channel_id=1, source_target_pairs={{0,32},{32,0},{1,33},{33,1},{2,34},{34,2},{3,35},{35,3},{4,36},{36... | collective-permute-start | bytes 98312 | tf_op jit(solution)/shard_map/ppermute | solution.py:279
  173.3 10.4 %collective-permute-start.15 = (bf16[16,16,512]{2,1,0:T(8,128)(2,1)S(1)}, bf16[16,16,512]{2,1,0:T(8,128)(2,1)S(1)}, u32[]{:S(2)}, u32[]{:S(2)}) collective-permute-start(bf16[16,16,512]{2,1,0:T(8,128)(2,1)S(1)} %bitcast.16), channel_id=1, source_target_pairs={{0,8},{8,0},{16,24},{24,16},{1,9},{9,1},{17,25},{25,17},{2,10},{10... | collective-permute-start | bytes 786440 | tf_op jit(solution)/shard_map/ppermute | solution.py:244
  175.2 12.5 %collective-permute-start.16 = (bf16[16,16,512]{2,1,0:T(8,128)(2,1)S(1)}, bf16[16,16,512]{2,1,0:T(8,128)(2,1)S(1)}, u32[]{:S(2)}, u32[]{:S(2)}) collective-permute-start(bf16[16,16,512]{2,1,0:T(8,128)(2,1)S(1)} %bitcast.17), channel_id=1, source_target_pairs={{0,16},{8,24},{16,0},{24,8},{1,17},{9,25},{17,1},{25,9},{2,18},{10... | collective-permute-start | bytes 786440 | tf_op jit(solution)/shard_map/ppermute | solution.py:244
  181.3 10.0 %collective-permute-start.17 = (bf16[16,16,512]{2,1,0:T(8,128)(2,1)S(1)}, bf16[16,16,512]{2,1,0:T(8,128)(2,1)S(1)}, u32[]{:S(2)}, u32[]{:S(2)}) collective-permute-start(bf16[16,16,512]{2,1,0:T(8,128)(2,1)S(1)} %bitcast.18), channel_id=1, source_target_pairs={{0,24},{8,16},{16,8},{24,0},{1,25},{9,17},{17,9},{25,1},{2,26},{10... | collective-permute-start | bytes 786440 | tf_op jit(solution)/shard_map/ppermute | solution.py:244
Sparse Core Ops, SparseCore 0:
  10.1 23.2 all-gather.2

commit v5 on v4

v5 whole, which is shorter than its diff:
```python
import functools

import jax
import jax.numpy as jnp
from jax import lax
from jax.experimental import pallas as pl
from jax.experimental.pallas import tpu as pltpu
from jax.sharding import Mesh
from jax.sharding import PartitionSpec as P

HD = 128
EPS = 1e-06
ETA = 1.0
MOMENT = 0.9
OUTER_RATE = 0.7
MIX_RATE = 0.5

AXES = ("y", "zh", "x", "zl", "core")
SIZES = (8, 2, 4, 4, 2)
REP = ("y", "zh", "x")
FSDP = ("zl", "core")
N_REP = SIZES[0] * SIZES[1] * SIZES[2]
SHARE = OUTER_RATE * (1.0 + MOMENT)
SWAP = [(0, 1), (1, 0)]
BF = jnp.bfloat16
F32 = jnp.float32
LIMIT = 12 * 1024 * 1024


def call(kernel, out_shape, flops=0, moved=0, limit=LIMIT, **more):
    return pl.pallas_call(
        kernel,
        out_shape=out_shape,
        compiler_params=pltpu.CompilerParams(vmem_limit_bytes=limit),
        cost_estimate=pl.CostEstimate(flops=flops, bytes_accessed=moved, transcendentals=0),
        **more,
    )


def slice_kernel(zl_ref, x_ref, *refs):
    *outs, sems = refs
    width = outs[0].shape[1]
    copies = []
    for k, out in enumerate(outs):
        start = pl.multiple_of((zl_ref[0] ^ k) * width, width)
        copies.append(pltpu.make_async_copy(x_ref.at[:, pl.ds(start, width)], out, sems.at[k]))
    for copy in copies:
        copy.start()
    for copy in copies:
        copy.wait()


def slices(zl, tokens, n):
    rows, width = tokens.shape
    return call(
        slice_kernel,
        (pltpu.VMEM((rows, width // n), BF),) * n,
        limit=56 * 1024 * 1024,
        in_specs=[pl.BlockSpec(memory_space=pltpu.SMEM), pl.BlockSpec(memory_space=pl.ANY)],
        out_specs=(pl.BlockSpec(memory_space=pltpu.VMEM),) * n,
        scratch_shapes=[pltpu.SemaphoreType.DMA((n,))],
    )(zl.reshape(1), tokens)


def project_kernel(x_ref, w_ref, out_ref):
    out_ref[...] = jnp.dot(x_ref[...], w_ref[...], preferred_element_type=F32).astype(BF)


def project(x, w):
    rows, depth = x.shape
    features = w.shape[1]
    return call(
        project_kernel,
        jax.ShapeDtypeStruct((rows, features), BF),
        flops=2 * rows * depth * features,
        moved=2 * (x.size + w.size),
    )(x, w)


def norm_kernel(a_ref, b_ref, c_ref, d_ref, g_ref, out_ref):
    for h in range(g_ref.shape[1] // HD):
        cols = pl.ds(h * HD, HD)
        projected = a_ref[:, cols].astype(F32)
        for ref in (b_ref, c_ref, d_ref):
            projected += ref[:, cols].astype(F32)
        scale = lax.rsqrt(jnp.mean(projected * projected, axis=-1, keepdims=True) + EPS)
        normed = projected * scale
        upstream = g_ref[:, cols].astype(F32)
        back = scale * (upstream - normed * jnp.mean(upstream * normed, axis=-1, keepdims=True))
        out_ref[:, cols] = back.astype(BF)


def norm_grad(parts, cotangent):
    return call(
        norm_kernel,
        jax.ShapeDtypeStruct(cotangent.shape, BF),
        moved=6 * cotangent.size * 2,
    )(*parts, cotangent)


def flip_kernel(x_ref, out_ref):
    out_ref[...] = x_ref[...].T


def flip(x):
    return call(flip_kernel, jax.ShapeDtypeStruct(x.shape[::-1], BF), moved=4 * x.size)(x)


def grad_kernel(half_ref, *refs, block):
    *refs, out_ref = refs
    xs, ks = refs[: len(refs) // 2], refs[len(refs) // 2 :]
    k = jnp.concatenate([ref[...] for ref in ks], axis=0)
    depth = out_ref.shape[0]
    for i in range(depth // block):
        start = pl.multiple_of(half_ref[0] * depth + i * block, block)
        x = jnp.concatenate([ref[pl.ds(start, block)] for ref in xs], axis=1)
        grad = jnp.dot(x, k, preferred_element_type=F32)
        out_ref[pl.ds(i * block, block)] = grad.astype(out_ref.dtype)


def gradient(half, xs, ks, dtype, block=256):
    depth, rows = xs[0].shape
    features = ks[0].shape[1]
    vmem = pl.BlockSpec(memory_space=pltpu.VMEM)
    return call(
        functools.partial(grad_kernel, block=block),
        pltpu.VMEM((depth // 2, features), dtype),
        flops=len(xs) * depth * rows * features,
        in_specs=[pl.BlockSpec(memory_space=pltpu.SMEM)] + [vmem] * (2 * len(xs)),
        out_specs=vmem,
    )(half.reshape(1), *xs, *ks)


def inner_kernel(s_ref, o_ref, w_ref, out_ref):
    ny, nx, nz, own, _ = out_ref.shape
    for y in range(ny):
        rows = pl.ds(y * nz * nx * own, nz * nx * own)
        grad = s_ref[rows] + o_ref[rows].astype(F32)
        local = (w_ref[rows].astype(F32) - ETA * grad).astype(BF)
        for z in range(nz):
            for x in range(nx):
                start = (z * nx + x) * own
                out_ref[y, x, z] = local[start : start + own]


def inner_step(same, other, w):
    rows, features = w.shape
    ny, nz, nx = SIZES[:3]
    return call(
        inner_kernel,
        pltpu.VMEM((ny, nx, nz, rows // (ny * nz * nx), features), BF),
        moved=8 * w.size,
        in_specs=[pl.BlockSpec(memory_space=pltpu.VMEM)] * 3,
        out_specs=pl.BlockSpec(memory_space=pltpu.VMEM),
    )(same, other, w)


def total_kernel(zh_ref, l_ref, a_ref, m_ref, out_ref, low_ref):
    own = a_ref.shape[1]
    total = l_ref[0].astype(F32)
    for i in range(1, l_ref.shape[0]):
        total += l_ref[i].astype(F32)
    out_ref[...] = total
    low_ref[...] = total.astype(BF)
    rows = pl.ds(pl.multiple_of(zh_ref[0] * own, own), own)
    from_base = (1.0 - SHARE) * a_ref[0] - OUTER_RATE * MOMENT * MOMENT * m_ref[0]
    low_ref[rows] = (out_ref[rows] + from_base * (N_REP / SHARE)).astype(BF)


def half_total(zh, shares, anchor, momentum):
    shape = shares.shape[1:]
    vmem = pl.BlockSpec(memory_space=pltpu.VMEM)
    return call(
        total_kernel,
        (jax.ShapeDtypeStruct(shape, F32), jax.ShapeDtypeStruct(shape, BF)),
        moved=2 * shares.size,
        in_specs=[pl.BlockSpec(memory_space=pltpu.SMEM)] + [vmem] * 3,
        out_specs=(vmem,) * 2,
    )(zh.reshape(1), shares, anchor, momentum)


def outer_kernel(zh_ref, s_ref, o_ref, a_ref, m_ref, base_ref, mom_ref, all_ref):
    own = a_ref.shape[1]
    rows = pl.ds(pl.multiple_of(zh_ref[0] * own, own), own)
    partner_rows = pl.ds(pl.multiple_of((1 - zh_ref[0]) * own, own), own)
    average = (s_ref[rows] + o_ref[rows].astype(F32)) / N_REP
    base = a_ref[0]
    delta = base - average
    new_mom = MOMENT * m_ref[0] + delta
    new_base = base - OUTER_RATE * (delta + MOMENT * new_mom)
    mom_ref[0] = new_mom
    base_ref[0] = new_base
    low = new_base.astype(BF)
    partner_low = ((s_ref[partner_rows] + o_ref[partner_rows].astype(F32)) * (SHARE / N_REP)).astype(BF)
    for i in range(all_ref.shape[0]):
        all_ref[i, rows] = low
        all_ref[i, partner_rows] = partner_low


def outer_step(zh, total, other, anchor, momentum, n):
    vmem = pl.BlockSpec(memory_space=pltpu.VMEM)
    return call(
        outer_kernel,
        (
            jax.ShapeDtypeStruct(anchor.shape, F32),
            jax.ShapeDtypeStruct(anchor.shape, F32),
            jax.ShapeDtypeStruct((n, *total.shape), BF),
        ),
        moved=2 * n * total.size,
        in_specs=[pl.BlockSpec(memory_space=pltpu.SMEM)] + [vmem] * 4,
        out_specs=(vmem,) * 3,
    )(zh.reshape(1), total, other, anchor, momentum)


def mix_kernel(l_ref, b_ref, out_ref):
    mixed = (1.0 - MIX_RATE) * l_ref[...].astype(F32) + MIX_RATE * b_ref[...].astype(F32)
    mixed = mixed.astype(BF)
    ny, nx, nz, own, _ = l_ref.shape
    for y in range(ny):
        for z in range(nz):
            for x in range(nx):
                out_ref[0, pl.ds(((y * nz + z) * nx + x) * own, own)] = mixed[y, x, z]


def mix(local, base, block=2):
    ny, nx, nz, own, features = local.shape
    rows = nx * nz * own
    return call(
        mix_kernel,
        jax.ShapeDtypeStruct((1, ny * rows, features), BF),
        moved=6 * local.size,
        grid=(ny // block,),
        in_specs=[pl.BlockSpec((block, nx, nz, own, features), lambda i: (i, 0, 0, 0, 0))] * 2,
        out_specs=pl.BlockSpec((1, block * rows, features), lambda i: (0, i, 0)),
    )(local, base)


def across(value, axis, k):
    return lax.ppermute(value, axis, [(i, i ^ k) for i in range(4)])


def body(tokens, cotangent, local_weights, anchor, momentum):
    own = local_weights[0]
    depth, features = own.shape
    width = tokens.shape[1] // SIZES[3]
    core, zl, zh = (lax.axis_index(name) for name in ("core", "zl", "zh"))
    chip_weights = lax.all_gather(own, "core", axis=0, tiled=True)
    chunks = slices(zl, tokens, SIZES[3])
    got = {k: across(chunks[k], "zl", k) for k in (3, 2, 1)}
    got[0] = chunks[0]
    parts = [project(got[0], chip_weights)]
    turned = {0: flip(got[0])}
    got[1], parts[0], turned[0] = lax.optimization_barrier((got[1], parts[0], turned[0]))
    parts.append(across(project(got[1], chip_weights), "zl", 1))
    turned[1] = flip(got[1])
    got[2], parts, turned = lax.optimization_barrier((got[2], parts, turned))
    made = project(got[2], chip_weights)
    parts.append(across(made, "zl", 2))
    got[3], made = lax.optimization_barrier((got[3], made))
    parts.append(across(project(got[3], chip_weights), "zl", 3))
    turned[2], turned[3] = flip(got[2]), flip(got[3])
    key_grad = norm_grad(parts, cotangent)
    ks = [key_grad] + [across(key_grad, "zl", k) for k in (1, 2, 3)]
    xs = [turned[k] for k in range(4)]
    send = gradient(1 - core, xs, ks, BF)
    same = gradient(core, xs, ks, F32)
    local = inner_step(same, lax.ppermute(send, "core", SWAP), own)
    ny, nx, nz, rows, _ = local.shape
    shares = lax.all_to_all(local.reshape(ny * nx, nz * rows, features), ("y", "x"), 0, 0, tiled=True)
    total, low = half_total(zh, shares, anchor, momentum)
    partner_total = lax.ppermute(low, "zh", SWAP)
    new_base, new_mom, spread = outer_step(zh, total, partner_total, anchor, momentum, ny * nx)
    base = lax.all_to_all(spread, ("y", "x"), 0, 0, tiled=True).reshape(local.shape)
    return mix(local, base), new_base, new_mom


def solution(mesh):
    fine = Mesh(mesh.devices.reshape(SIZES), AXES)
    placed = (
        P((*REP, *FSDP), None),
        P((*REP, *FSDP), None),
        P(REP, FSDP, None),
        P(FSDP, REP, None),
        P(FSDP, REP, None),
    )
    return jax.shard_map(
        body,
        mesh=fine,
        in_specs=placed,
        out_specs=(P(REP, FSDP, None), P(FSDP, REP, None), P(FSDP, REP, None)),
        check_vma=False,
    )
```

time: 201 us -> 196 us (0.975)
  starting transfers between devices: 83.2 us -> 60.4 us
  waiting for transfers between devices: 57.7 us -> 75.3 us
    all_to_all x0 -> x1, waiting for transfers between devices: none -> 28.4 us  [body(): lax.all_to_all(local.reshape(ny * nx, nz * rows, features), ('y', 'x'), 0...]
    ppermute x15 -> x9, starting transfers between devices: 63.2 us -> 36 us  [across(): return lax.ppermute(value, axis, [(i, i ^ k) for i in range(4)])]
    all_to_all x0 -> x1, starting transfers between devices: none -> 10.3 us  [body(): lax.all_to_all(local.reshape(ny * nx, nz * rows, features), ('y', 'x'), 0...]
    ppermute x2 -> x1, starting transfers between devices: 10.7 us -> 1.92 us  [body(): local = inner_step(same, lax.ppermute(send, 'core', SWAP), own)]
    ppermute x15 -> x9, waiting for transfers between devices: 40.6 us -> 32 us  [across(): return lax.ppermute(value, axis, [(i, i ^ k) for i in range(4)])]
    ppermute x1, starting transfers between devices: 9.3 us -> 12 us  [body(): partner_total = lax.ppermute(low, 'zh', SWAP)]
    ppermute x2 -> x1, waiting for transfers between devices: 4.3 us -> 1.9 us  [body(): local = inner_step(same, lax.ppermute(send, 'core', SWAP), own)]
    pallas_call x7 -> x6, Pallas kernels: 7.71 us -> 9.39 us  [the longest x1 3.52 us: mix(): call(mix_kernel, jax.ShapeDtypeStruct((1, ny * rows, features), BF), move...]
  transfers between devices with their start and end apart: 19 -> 13, of which waited for: 15 -> 10; matrix products, arithmetic and copies ran while one was open for 0% -> 0% of each run, Pallas kernels for 2% -> 3%
where the time goes in v5:
time: 196 us; the launch traced here: 195 us
  waiting for transfers between devices  75.3 us (38%)
  starting transfers between devices  60.4 us (31%)
  blocking collectives  31.5 us (16%)
  between operations  14.3 us (7%)
  Pallas kernels  12.3 us (6%)
    ppermute x9, starting transfers between devices, across(): return lax.ppermute(value, axis, [(i, i ^ k) for i in range(4)])  36 us
    ppermute x9, waiting for transfers between devices, across(): return lax.ppermute(value, axis, [(i, i ^ k) for i in range(4)])  32 us
    all_to_all x1, blocking collectives, body(): lax.all_to_all(spread, ('y', 'x'), 0, 0, tiled=True).reshape(local.shape)  31.5 us
    all_to_all x1, waiting for transfers between devices, body(): lax.all_to_all(local.reshape(ny * nx, nz * rows, features), ('y', 'x'), 0...  28.4 us
    ppermute x1, starting transfers between devices, body(): partner_total = lax.ppermute(low, 'zh', SWAP)  12 us
    all_gather x1, waiting for transfers between devices, body(): chip_weights = lax.all_gather(own, 'core', axis=0, tiled=True)  10.5 us
    all_to_all x1, starting transfers between devices, body(): lax.all_to_all(local.reshape(ny * nx, nz * rows, features), ('y', 'x'), 0...  10.3 us
  transfers between devices with their start and end apart: 13, of which 10 were waited for; matrix products, arithmetic and copies ran while one was open for 0% of the time, Pallas kernels for 3%

profile of v5, /device:TPU:6, one launch (start us, length us, event | category | flops | bytes accessed | tf_op | source)
XLA Modules:
  0.0 195.3 jit_solution(17697944028581975003)
XLA Ops:
  7.2 0.0 all-gather.3.cloned.1.call-start
  7.2 0.7 all-gather.3.cloned.1.call-update
  7.9 2.5 %shard_map.76 = (bf16[128,2048]{1,0:T(8,128)(2,1)S(1)}, bf16[128,2048]{1,0:T(8,128)(2,1)}, bf16[128,2048]{1,0:T(8,128)(2,1)}, bf16[128,2048]{1,0:T(8,128)(2,1)S(1)}) custom-call(s32[1]{0:T(128)} %bitcast.1.zl_ref, bf16[128,8192]{1,0:T(8,128)(2,1)} %x_ref.1), custom_call_target="tpu_custom_call" | custom-call | tf_op jit(solution)/shard_map/pallas_call | solution.py:55
  10.4 4.3 %collective-permute-start.1 = (bf16[128,2048]{1,0:T(8,128)(2,1)}, bf16[128,2048]{1,0:T(8,128)(2,1)S(1)}, u32[]{:S(2)}, u32[]{:S(2)}) collective-permute-start(bf16[128,2048]{1,0:T(8,128)(2,1)} %get-tuple-element.22), channel_id=1, source_target_pairs={{0,2},{2,0},{4,6},{6,4},{1,3},{3,1},{5,7},{7,5},{8,10},{10,8},{12,... | collective-permute-start | bytes 1572872 | tf_op jit(solution)/shard_map/ppermute | solution.py:239
  14.7 6.1 %collective-permute-start = (bf16[128,2048]{1,0:T(8,128)(2,1)}, bf16[128,2048]{1,0:T(8,128)(2,1)S(1)}, u32[]{:S(2)}, u32[]{:S(2)}) collective-permute-start(bf16[128,2048]{1,0:T(8,128)(2,1)} %get-tuple-element.21), channel_id=1, source_target_pairs={{0,4},{2,6},{4,0},{6,2},{1,5},{3,7},{5,1},{7,3},{8,12},{10,14},{12... | collective-permute-start | bytes 1572872 | tf_op jit(solution)/shard_map/ppermute | solution.py:239
  20.8 1.9 collective-permute-start.3
  22.8 0.2 shard_map.78.refs_0_
  22.9 10.5 %all-gather.3.cloned.1.call-done = bf16[1,2048,512]{2,1,0:T(8,128)(2,1)} async-done(((bf16[1,1024,512]{2,1,0:T(8,128)(2,1)}), bf16[1,2048,512]{2,1,0:T(8,128)(2,1)}) %all-gather.3.cloned.1.call-update) | async-done | bytes 2097168 | tf_op jit(solution)/shard_map/all_gather | solution.py:247
  33.4 0.0 copy-start
  33.4 1.6 copy-done
  35.0 0.4 shard_map.77.a_ref
  35.5 0.0 copy-start.1
  35.5 0.5 collective-permute-done.1.x_ref
  35.9 0.4 shard_map.79
  36.4 3.2 %collective-permute-start.2 = (bf16[128,512]{1,0:T(8,128)(2,1)S(1)}, bf16[128,512]{1,0:T(8,128)(2,1)S(1)}, u32[]{:S(2)}, u32[]{:S(2)}) collective-permute-start(bf16[128,512]{1,0:T(8,128)(2,1)S(1)} %shard_map.79), channel_id=1, source_target_pairs={{0,2},{2,0},{4,6},{6,4},{1,3},{3,1},{5,7},{7,5},{8,10},{10,8},{12,... | collective-permute-start | bytes 393224 | tf_op jit(solution)/shard_map/ppermute | solution.py:239
  39.6 0.2 shard_map.80.refs_1_
  39.8 0.0 copy-start.5
  39.8 16.5 %collective-permute-done.x_ref = bf16[128,2048]{1,0:T(8,128)(2,1)S(1)} collective-permute-done((bf16[128,2048]{1,0:T(8,128)(2,1)}, bf16[128,2048]{1,0:T(8,128)(2,1)S(1)}, u32[]{:S(2)}, u32[]{:S(2)}) %collective-permute-start) | collective-permute-done | bytes 524320 | tf_op jit(solution)/shard_map/ppermute | solution.py:239
  56.3 0.7 collective-permute-done.2.b_ref
  57.0 0.0 copy-done.1
  57.0 0.4 shard_map.82
  57.5 3.3 %collective-permute-start.4 = (bf16[128,512]{1,0:T(8,128)(2,1)S(1)}, bf16[128,512]{1,0:T(8,128)(2,1)S(1)}, u32[]{:S(2)}, u32[]{:S(2)}) collective-permute-start(bf16[128,512]{1,0:T(8,128)(2,1)S(1)} %shard_map.82), channel_id=1, source_target_pairs={{0,4},{2,6},{4,0},{6,2},{1,5},{3,7},{5,1},{7,3},{8,12},{10,14},{12... | collective-permute-start | bytes 393224 | tf_op jit(solution)/shard_map/ppermute | solution.py:239
  60.8 0.0 collective-permute-done.3.x_ref
  60.8 0.4 shard_map.84
  61.3 3.8 %collective-permute-start.5 = (bf16[128,512]{1,0:T(8,128)(2,1)S(1)}, bf16[128,512]{1,0:T(8,128)(2,1)S(1)}, u32[]{:S(2)}, u32[]{:S(2)}) collective-permute-start(bf16[128,512]{1,0:T(8,128)(2,1)S(1)} %shard_map.84), channel_id=1, source_target_pairs={{0,6},{2,4},{4,2},{6,0},{1,7},{3,5},{5,3},{7,1},{8,14},{10,12},{12... | collective-permute-start | bytes 393224 | tf_op jit(solution)/shard_map/ppermute | solution.py:239
  65.1 9.8 %collective-permute-done.4.c_ref = bf16[128,512]{1,0:T(8,128)(2,1)S(1)} collective-permute-done((bf16[128,512]{1,0:T(8,128)(2,1)S(1)}, bf16[128,512]{1,0:T(8,128)(2,1)S(1)}, u32[]{:S(2)}, u32[]{:S(2)}) %collective-permute-start.4) | collective-permute-done | bytes 131104 | tf_op jit(solution)/shard_map/ppermute | solution.py:239
  74.9 0.0 collective-permute-done.5.d_ref
  74.9 0.0 copy-done.5
  74.9 0.2 shard_map.85.refs_4_
  75.1 4.3 %collective-permute-start.8 = (bf16[128,512]{1,0:T(8,128)(2,1)S(1)}, bf16[128,512]{1,0:T(8,128)(2,1)S(1)}, u32[]{:S(2)}, u32[]{:S(2)}) collective-permute-start(bf16[128,512]{1,0:T(8,128)(2,1)S(1)} %shard_map.85.refs_4_), channel_id=1, source_target_pairs={{0,6},{2,4},{4,2},{6,0},{1,7},{3,5},{5,3},{7,1},{8,14},{10,12},{12... | collective-permute-start | bytes 393224 | tf_op jit(solution)/shard_map/ppermute | solution.py:239
  79.4 7.2 %collective-permute-start.7 = (bf16[128,512]{1,0:T(8,128)(2,1)S(1)}, bf16[128,512]{1,0:T(8,128)(2,1)S(1)}, u32[]{:S(2)}, u32[]{:S(2)}) collective-permute-start(bf16[128,512]{1,0:T(8,128)(2,1)S(1)} %shard_map.85.refs_4_), channel_id=1, source_target_pairs={{0,4},{2,6},{4,0},{6,2},{1,5},{3,7},{5,1},{7,3},{8,12},{10,14},{12... | collective-permute-start | bytes 393224 | tf_op jit(solution)/shard_map/ppermute | solution.py:239
  86.6 1.9 collective-permute-start.6
  88.5 0.2 shard_map.81.refs_2_
  88.7 0.2 shard_map.83.refs_3_
  88.9 0.0 collective-permute-done.8.refs_7_
  88.9 1.5 collective-permute-done.7.refs_6_
  90.4 3.1 %collective-permute-done.6.refs_5_ = bf16[128,512]{1,0:T(8,128)(2,1)S(1)} collective-permute-done((bf16[128,512]{1,0:T(8,128)(2,1)S(1)}, bf16[128,512]{1,0:T(8,128)(2,1)S(1)}, u32[]{:S(2)}, u32[]{:S(2)}) %collective-permute-start.6) | collective-permute-done | bytes 131104 | tf_op jit(solution)/shard_map/ppermute | solution.py:239
  93.5 0.7 shard_map.87
  94.2 1.9 collective-permute-start.9
  96.1 0.0 copy-start.2
  96.1 0.7 shard_map.86.s_ref
  96.8 1.9 collective-permute-done.9.o_ref
  98.7 0.0 copy-done.2
  98.7 1.3 shard_map.88.l_ref
  100.0 0.0 copy-start.3
  100.0 0.0 copy-start.4
  100.0 10.3 %all-to-all-start = ((bf16[32,32,512]{2,1,0:T(8,128)(2,1)}), bf16[32,32,512]{2,1,0:T(8,128)(2,1)S(1)}, u32[]{:S(2)}, u32[]{:S(2)}) async-start(bf16[32,32,512]{2,1,0:T(8,128)(2,1)} %bitcast.6), calls=%async_computation | async-start | bytes 2097152 | tf_op jit(solution)/shard_map/all_to_all | solution.py:269
  110.4 28.4 %all-to-all-done.l_ref = bf16[32,32,512]{2,1,0:T(8,128)(2,1)S(1)} async-done(((bf16[32,32,512]{2,1,0:T(8,128)(2,1)}), bf16[32,32,512]{2,1,0:T(8,128)(2,1)S(1)}, u32[]{:S(2)}, u32[]{:S(2)}) %all-to-all-start) | async-done | bytes 1048608 | tf_op jit(solution)/shard_map/all_to_all | solution.py:269
  138.7 0.0 copy-done.3
  138.7 0.0 copy-done.4
  138.7 0.1 shard_map.89
  138.9 12.0 %collective-permute-start.10 = (bf16[32,512]{1,0:T(8,128)(2,1)S(1)}, bf16[32,512]{1,0:T(8,128)(2,1)S(1)}, u32[]{:S(2)}, u32[]{:S(2)}) collective-permute-start(bf16[32,512]{1,0:T(8,128)(2,1)S(1)} %get-tuple-element.35), channel_id=1, source_target_pairs={{0,32},{32,0},{1,33},{33,1},{2,34},{34,2},{3,35},{35,3},{4,36},{36... | collective-permute-start | bytes 98312 | tf_op jit(solution)/shard_map/ppermute | solution.py:271
  150.9 1.9 collective-permute-done.10.o_ref
  152.8 0.6 shard_map.90
  153.5 31.5 %all_to_all.10 = bf16[32,32,512]{2,1,0:T(8,128)(2,1)S(1)} all-to-all(bf16[32,32,512]{2,1,0:T(8,128)(2,1)S(1)} %get-tuple-element.36), channel_id=1, replica_groups=mesh['y'=8,'zh'=2,'x'=4,'zl'=4,'core'=2] {'y','x'}, dimensions={0} | all-to-all | bytes 2097152 | tf_op jit(solution)/shard_map/all_to_all | solution.py:273
  184.9 3.5 %shard_map.91 = bf16[1,1024,512]{2,1,0:T(8,128)(2,1)} custom-call(bf16[8,4,2,16,512]{4,3,2,1,0:T(8,128)(2,1)} %shard_map.88.l_ref, bf16[8,4,2,16,512]{4,3,2,1,0:T(8,128)(2,1)S(1)} %bitcast.13), custom_call_target="tpu_custom_call" | custom-call | bytes 3145728 | tf_op jit(solution)/shard_map/pallas_call | solution.py:228
Async XLA Ops:
  7.2 26.3 %all-gather.3.cloned.1.call-start = ((), (), s32[]{:S(2)}) async-start(), calls=%async_computation.2 | async-start | bytes 3145728 | tf_op jit(solution)/shard_map/all_gather | solution.py:247
  10.4 25.5 %collective-permute-start.1 = (bf16[128,2048]{1,0:T(8,128)(2,1)}, bf16[128,2048]{1,0:T(8,128)(2,1)S(1)}, u32[]{:S(2)}, u32[]{:S(2)}) collective-permute-start(bf16[128,2048]{1,0:T(8,128)(2,1)} %get-tuple-element.22), channel_id=1, source_target_pairs={{0,2},{2,0},{4,6},{6,4},{1,3},{3,1},{5,7},{7,5},{8,10},{10,8},{12,... | collective-permute-start | bytes 1572872 | tf_op jit(solution)/shard_map/ppermute | solution.py:239
  14.7 41.6 %collective-permute-start = (bf16[128,2048]{1,0:T(8,128)(2,1)}, bf16[128,2048]{1,0:T(8,128)(2,1)S(1)}, u32[]{:S(2)}, u32[]{:S(2)}) collective-permute-start(bf16[128,2048]{1,0:T(8,128)(2,1)} %get-tuple-element.21), channel_id=1, source_target_pairs={{0,4},{2,6},{4,0},{6,2},{1,5},{3,7},{5,1},{7,3},{8,12},{10,14},{12... | collective-permute-start | bytes 1572872 | tf_op jit(solution)/shard_map/ppermute | solution.py:239
  20.8 40.0 %collective-permute-start.3 = (bf16[128,2048]{1,0:T(8,128)(2,1)S(1)}, bf16[128,2048]{1,0:T(8,128)(2,1)S(1)}, u32[]{:S(2)}, u32[]{:S(2)}) collective-permute-start(bf16[128,2048]{1,0:T(8,128)(2,1)S(1)} %get-tuple-element.30), channel_id=1, source_target_pairs={{0,6},{2,4},{4,2},{6,0},{1,7},{3,5},{5,3},{7,1},{8,14},{10,12},{12... | collective-permute-start | bytes 1572872 | tf_op jit(solution)/shard_map/ppermute | solution.py:239
  33.4 1.6 copy-start
  35.5 21.6 %copy-start.1 = (bf16[1,2048,512]{2,1,0:T(8,128)(2,1)S(1)}, bf16[1,2048,512]{2,1,0:T(8,128)(2,1)}, u32[]{:S(2)}) copy-start(bf16[1,2048,512]{2,1,0:T(8,128)(2,1)} %all-gather.3.cloned.1.call-done) | copy-start | bytes 6291460
  36.4 20.7 %collective-permute-start.2 = (bf16[128,512]{1,0:T(8,128)(2,1)S(1)}, bf16[128,512]{1,0:T(8,128)(2,1)S(1)}, u32[]{:S(2)}, u32[]{:S(2)}) collective-permute-start(bf16[128,512]{1,0:T(8,128)(2,1)S(1)} %shard_map.79), channel_id=1, source_target_pairs={{0,2},{2,0},{4,6},{6,4},{1,3},{3,1},{5,7},{7,5},{8,10},{10,8},{12,... | collective-permute-start | bytes 393224 | tf_op jit(solution)/shard_map/ppermute | solution.py:239
  39.8 35.1 %copy-start.5 = (bf16[128,512]{1,0:T(8,128)(2,1)S(1)}, bf16[128,512]{1,0:T(8,128)(2,1)}, u32[]{:S(2)}) copy-start(bf16[128,512]{1,0:T(8,128)(2,1)} %g_ref.1) | copy-start | bytes 393220
  57.5 17.4 %collective-permute-start.4 = (bf16[128,512]{1,0:T(8,128)(2,1)S(1)}, bf16[128,512]{1,0:T(8,128)(2,1)S(1)}, u32[]{:S(2)}, u32[]{:S(2)}) collective-permute-start(bf16[128,512]{1,0:T(8,128)(2,1)S(1)} %shard_map.82), channel_id=1, source_target_pairs={{0,4},{2,6},{4,0},{6,2},{1,5},{3,7},{5,1},{7,3},{8,12},{10,14},{12... | collective-permute-start | bytes 393224 | tf_op jit(solution)/shard_map/ppermute | solution.py:239
  61.3 13.6 %collective-permute-start.5 = (bf16[128,512]{1,0:T(8,128)(2,1)S(1)}, bf16[128,512]{1,0:T(8,128)(2,1)S(1)}, u32[]{:S(2)}, u32[]{:S(2)}) collective-permute-start(bf16[128,512]{1,0:T(8,128)(2,1)S(1)} %shard_map.84), channel_id=1, source_target_pairs={{0,6},{2,4},{4,2},{6,0},{1,7},{3,5},{5,3},{7,1},{8,14},{10,12},{12... | collective-permute-start | bytes 393224 | tf_op jit(solution)/shard_map/ppermute | solution.py:239
  75.1 13.8 %collective-permute-start.8 = (bf16[128,512]{1,0:T(8,128)(2,1)S(1)}, bf16[128,512]{1,0:T(8,128)(2,1)S(1)}, u32[]{:S(2)}, u32[]{:S(2)}) collective-permute-start(bf16[128,512]{1,0:T(8,128)(2,1)S(1)} %shard_map.85.refs_4_), channel_id=1, source_target_pairs={{0,6},{2,4},{4,2},{6,0},{1,7},{3,5},{5,3},{7,1},{8,14},{10,12},{12... | collective-permute-start | bytes 393224 | tf_op jit(solution)/shard_map/ppermute | solution.py:239
  79.4 11.0 %collective-permute-start.7 = (bf16[128,512]{1,0:T(8,128)(2,1)S(1)}, bf16[128,512]{1,0:T(8,128)(2,1)S(1)}, u32[]{:S(2)}, u32[]{:S(2)}) collective-permute-start(bf16[128,512]{1,0:T(8,128)(2,1)S(1)} %shard_map.85.refs_4_), channel_id=1, source_target_pairs={{0,4},{2,6},{4,0},{6,2},{1,5},{3,7},{5,1},{7,3},{8,12},{10,14},{12... | collective-permute-start | bytes 393224 | tf_op jit(solution)/shard_map/ppermute | solution.py:239
  86.6 6.9 %collective-permute-start.6 = (bf16[128,512]{1,0:T(8,128)(2,1)S(1)}, bf16[128,512]{1,0:T(8,128)(2,1)S(1)}, u32[]{:S(2)}, u32[]{:S(2)}) collective-permute-start(bf16[128,512]{1,0:T(8,128)(2,1)S(1)} %shard_map.85.refs_4_), channel_id=1, source_target_pairs={{0,2},{2,0},{4,6},{6,4},{1,3},{3,1},{5,7},{7,5},{8,10},{10,8},{12,... | collective-permute-start | bytes 393224 | tf_op jit(solution)/shard_map/ppermute | solution.py:239
  94.2 4.6 %collective-permute-start.9 = (bf16[1024,512]{1,0:T(8,128)(2,1)S(1)}, bf16[1024,512]{1,0:T(8,128)(2,1)S(1)}, u32[]{:S(2)}, u32[]{:S(2)}) collective-permute-start(bf16[1024,512]{1,0:T(8,128)(2,1)S(1)} %shard_map.87), channel_id=1, source_target_pairs={{0,1},{1,0},{2,3},{3,2},{4,5},{5,4},{6,7},{7,6},{8,9},{9,8},{10,11... | collective-permute-start | bytes 3145736 | tf_op jit(solution)/shard_map/ppermute | solution.py:267
  96.1 2.6 %copy-start.2 = (bf16[1,1024,512]{2,1,0:T(8,128)(2,1)S(1)}, bf16[1,1024,512]{2,1,0:T(8,128)(2,1)}, u32[]{:S(2)}) copy-start(bf16[1,1024,512]{2,1,0:T(8,128)(2,1)} %param.7) | copy-start | bytes 3145732
  100.0 38.7 %copy-start.3 = (f32[1,16,512]{2,1,0:T(8,128)S(1)}, f32[1,16,512]{2,1,0:T(8,128)}, u32[]{:S(2)}) copy-start(f32[1,16,512]{2,1,0:T(8,128)} %a_ref.3) | copy-start | bytes 98308
  100.0 38.7 %copy-start.4 = (f32[1,16,512]{2,1,0:T(8,128)S(1)}, f32[1,16,512]{2,1,0:T(8,128)}, u32[]{:S(2)}) copy-start(f32[1,16,512]{2,1,0:T(8,128)} %m_ref.3) | copy-start | bytes 98308
  100.0 38.7 %all-to-all-start = ((bf16[32,32,512]{2,1,0:T(8,128)(2,1)}), bf16[32,32,512]{2,1,0:T(8,128)(2,1)S(1)}, u32[]{:S(2)}, u32[]{:S(2)}) async-start(bf16[32,32,512]{2,1,0:T(8,128)(2,1)} %bitcast.6), calls=%async_computation | async-start | bytes 2097152 | tf_op jit(solution)/shard_map/all_to_all | solution.py:269
  138.9 13.9 %collective-permute-start.10 = (bf16[32,512]{1,0:T(8,128)(2,1)S(1)}, bf16[32,512]{1,0:T(8,128)(2,1)S(1)}, u32[]{:S(2)}, u32[]{:S(2)}) collective-permute-start(bf16[32,512]{1,0:T(8,128)(2,1)S(1)} %get-tuple-element.35), channel_id=1, source_target_pairs={{0,32},{32,0},{1,33},{33,1},{2,34},{34,2},{3,35},{35,3},{4,36},{36... | collective-permute-start | bytes 98312 | tf_op jit(solution)/shard_map/ppermute | solution.py:271
Sparse Core Ops, SparseCore 0:
  10.1 23.2 all-gather.2

commit v6 on v5

--- a/solution.py
+++ b/solution.py
@@ -37,24 +37,25 @@
     )
 
 
-def slice_kernel(zl_ref, x_ref, *refs):
+def slice_kernel(zl_ref, x_ref, *refs, distances):
     *outs, sems = refs
     width = outs[0].shape[1]
     copies = []
-    for k, out in enumerate(outs):
+    for i, (k, out) in enumerate(zip(distances, outs)):
         start = pl.multiple_of((zl_ref[0] ^ k) * width, width)
-        copies.append(pltpu.make_async_copy(x_ref.at[:, pl.ds(start, width)], out, sems.at[k]))
+        copies.append(pltpu.make_async_copy(x_ref.at[:, pl.ds(start, width)], out, sems.at[i]))
     for copy in copies:
         copy.start()
     for copy in copies:
         copy.wait()
 
 
-def slices(zl, tokens, n):
+def slices(zl, tokens, distances):
     rows, width = tokens.shape
-    return call(
-        slice_kernel,
-        (pltpu.VMEM((rows, width // n), BF),) * n,
+    n = len(distances)
+    return call(
+        functools.partial(slice_kernel, distances=distances),
+        (pltpu.VMEM((rows, width // SIZES[3]), BF),) * n,
         limit=56 * 1024 * 1024,
         in_specs=[pl.BlockSpec(memory_space=pltpu.SMEM), pl.BlockSpec(memory_space=pl.ANY)],
         out_specs=(pl.BlockSpec(memory_space=pltpu.VMEM),) * n,
@@ -62,19 +63,26 @@
     )(zl.reshape(1), tokens)
 
 
-def project_kernel(x_ref, w_ref, out_ref):
-    out_ref[...] = jnp.dot(x_ref[...], w_ref[...], preferred_element_type=F32).astype(BF)
-
-
-def project(x, w):
+def project_kernel(core_ref, x_ref, own_ref, other_ref, out_ref):
+    depth = own_ref.shape[0]
+    mine = pl.ds(pl.multiple_of(core_ref[0] * depth, depth), depth)
+    others = pl.ds(pl.multiple_of((1 - core_ref[0]) * depth, depth), depth)
+    total = jnp.dot(x_ref[:, mine], own_ref[...], preferred_element_type=F32)
+    total += jnp.dot(x_ref[:, others], other_ref[...], preferred_element_type=F32)
+    out_ref[...] = total.astype(BF)
+
+
+def project(core, x, own, other):
     rows, depth = x.shape
-    features = w.shape[1]
+    features = own.shape[1]
+    vmem = pl.BlockSpec(memory_space=pltpu.VMEM)
     return call(
         project_kernel,
         jax.ShapeDtypeStruct((rows, features), BF),
         flops=2 * rows * depth * features,
-        moved=2 * (x.size + w.size),
-    )(x, w)
+        in_specs=[pl.BlockSpec(memory_space=pltpu.SMEM)] + [vmem] * 3,
+        out_specs=vmem,
+    )(core.reshape(1), x, own, other)
 
 
 def norm_kernel(a_ref, b_ref, c_ref, d_ref, g_ref, out_ref):
@@ -103,7 +111,7 @@
 
 
 def flip(x):
-    return call(flip_kernel, jax.ShapeDtypeStruct(x.shape[::-1], BF), moved=4 * x.size)(x)
+    return call(flip_kernel, jax.ShapeDtypeStruct(x.shape[::-1], BF))(x)
 
 
 def grad_kernel(half_ref, *refs, block):
@@ -212,26 +220,33 @@
     )(zh.reshape(1), total, other, anchor, momentum)
 
 
-def mix_kernel(l_ref, b_ref, out_ref):
-    mixed = (1.0 - MIX_RATE) * l_ref[...].astype(F32) + MIX_RATE * b_ref[...].astype(F32)
-    mixed = mixed.astype(BF)
+def mix_kernel(l_ref, b_ref, out_ref, held_ref, sems):
     ny, nx, nz, own, _ = l_ref.shape
+    rows = nz * nx * own
+    copies = []
     for y in range(ny):
+        mixed = (1.0 - MIX_RATE) * l_ref[y].astype(F32) + MIX_RATE * b_ref[y].astype(F32)
+        mixed = mixed.astype(BF)
         for z in range(nz):
             for x in range(nx):
-                out_ref[0, pl.ds(((y * nz + z) * nx + x) * own, own)] = mixed[y, x, z]
-
-
-def mix(local, base, block=2):
+                held_ref[pl.ds(((y * nz + z) * nx + x) * own, own)] = mixed[x, z]
+        part = pl.ds(y * rows, rows)
+        copies.append(pltpu.make_async_copy(held_ref.at[part], out_ref.at[0, part], sems.at[y]))
+        copies[-1].start()
+    for copy in copies:
+        copy.wait()
+
+
+def mix(local, base):
     ny, nx, nz, own, features = local.shape
-    rows = nx * nz * own
+    rows = ny * nx * nz * own
     return call(
         mix_kernel,
-        jax.ShapeDtypeStruct((1, ny * rows, features), BF),
+        jax.ShapeDtypeStruct((1, rows, features), BF),
         moved=6 * local.size,
-        grid=(ny // block,),
-        in_specs=[pl.BlockSpec((block, nx, nz, own, features), lambda i: (i, 0, 0, 0, 0))] * 2,
-        out_specs=pl.BlockSpec((1, block * rows, features), lambda i: (0, i, 0)),
+        in_specs=[pl.BlockSpec(memory_space=pltpu.VMEM)] * 2,
+        out_specs=pl.BlockSpec(memory_space=pl.ANY),
+        scratch_shapes=[pltpu.VMEM((rows, features), BF), pltpu.SemaphoreType.DMA((ny,))],
     )(local, base)
 
 
@@ -244,23 +259,30 @@
     depth, features = own.shape
     width = tokens.shape[1] // SIZES[3]
     core, zl, zh = (lax.axis_index(name) for name in ("core", "zl", "zh"))
-    chip_weights = lax.all_gather(own, "core", axis=0, tiled=True)
-    chunks = slices(zl, tokens, SIZES[3])
-    got = {k: across(chunks[k], "zl", k) for k in (3, 2, 1)}
-    got[0] = chunks[0]
-    parts = [project(got[0], chip_weights)]
+    got = dict(enumerate(slices(zl, tokens, (0, 1, 2, 3))))
+    for k in (3, 2, 1):
+        got[k] = across(got[k], "zl", k)
+    swapped = lax.ppermute(own, "core", SWAP)
+
+    def partial(k):
+        return project(core, got[k], own, swapped)
+
     turned = {0: flip(got[0])}
-    got[1], parts[0], turned[0] = lax.optimization_barrier((got[1], parts[0], turned[0]))
-    parts.append(across(project(got[1], chip_weights), "zl", 1))
+    parts = [partial(0)]
+    got[1], parts, turned = lax.optimization_barrier((got[1], parts, turned))
+    parts.append(across(partial(1), "zl", 1))
     turned[1] = flip(got[1])
     got[2], parts, turned = lax.optimization_barrier((got[2], parts, turned))
-    made = project(got[2], chip_weights)
+    made = partial(2)
     parts.append(across(made, "zl", 2))
     got[3], made = lax.optimization_barrier((got[3], made))
-    parts.append(across(project(got[3], chip_weights), "zl", 3))
-    turned[2], turned[3] = flip(got[2]), flip(got[3])
+    parts.append(across(partial(3), "zl", 3))
     key_grad = norm_grad(parts, cotangent)
     ks = [key_grad] + [across(key_grad, "zl", k) for k in (1, 2, 3)]
+    for k, near in ((3, 1), (2, 2)):
+        got[k], ks[near] = lax.optimization_barrier((got[k], ks[near]))
+        turned[k] = flip(got[k])
+    xs = [turned[k] for k in range(4)]
     xs = [turned[k] for k in range(4)]
     send = gradient(1 - core, xs, ks, BF)
     same = gradient(core, xs, ks, F32)

time: 196 us -> 184 us (0.939)
  between operations: 14.3 us -> 0.91 us
  Pallas kernels: 12.3 us -> 15.5 us
  waiting for transfers between devices: 75.3 us -> 72.4 us
    all_gather x1 -> x0, waiting for transfers between devices: 10.5 us -> none  [body(): chip_weights = lax.all_gather(own, 'core', axis=0, tiled=True)]
    ppermute x9, waiting for transfers between devices: 32 us -> 40.3 us  [across(): return lax.ppermute(value, axis, [(i, i ^ k) for i in range(4)])]
    ppermute x1, starting transfers between devices: 12 us -> 8.8 us  [body(): partner_total = lax.ppermute(low, 'zh', SWAP)]
    pallas_call x4, Pallas kernels: 1.78 us -> 3.87 us  [project(): call(project_kernel, jax.ShapeDtypeStruct((rows, features), BF), flops=2...]
    ppermute x0 -> x1, starting transfers between devices: none -> 2.05 us  [body(): swapped = lax.ppermute(own, 'core', SWAP)]
  transfers between devices with their start and end apart: 13 -> 13, of which waited for: 10 -> 9; matrix products, arithmetic and copies ran while one was open for 0% -> 0% of each run, Pallas kernels for 3% -> 6%
where the time goes in v6:
time: 184 us; the launch traced here: 182 us
  waiting for transfers between devices  72.4 us (39%)
  starting transfers between devices  58.7 us (32%)
  blocking collectives  31.5 us (17%)
  Pallas kernels  15.5 us (8%)
  local copies, waits for them, and re-layouts  3.22 us (2%)
    ppermute x9, waiting for transfers between devices, across(): return lax.ppermute(value, axis, [(i, i ^ k) for i in range(4)])  40.3 us
    ppermute x9, starting transfers between devices, across(): return lax.ppermute(value, axis, [(i, i ^ k) for i in range(4)])  35.6 us
    all_to_all x1, blocking collectives, body(): lax.all_to_all(spread, ('y', 'x'), 0, 0, tiled=True).reshape(local.shape)  31.5 us
    all_to_all x1, waiting for transfers between devices, body(): lax.all_to_all(local.reshape(ny * nx, nz * rows, features), ('y', 'x'), 0...  28.4 us
    all_to_all x1, starting transfers between devices, body(): lax.all_to_all(local.reshape(ny * nx, nz * rows, features), ('y', 'x'), 0...  10.3 us
    ppermute x1, starting transfers between devices, body(): partner_total = lax.ppermute(low, 'zh', SWAP)  8.8 us
    pallas_call x4, Pallas kernels, project(): call(project_kernel, jax.ShapeDtypeStruct((rows, features), BF), flops=2...  3.87 us
  transfers between devices with their start and end apart: 13, of which 9 were waited for; matrix products, arithmetic and copies ran while one was open for 0% of the time, Pallas kernels for 6%

profile of v6, /device:TPU:6, one launch (start us, length us, event | category | flops | bytes accessed | tf_op | source)
XLA Modules:
  0.0 182.2 jit_solution(10787646958630741674)
XLA Ops:
  0.6 0.0 copy-start
  0.6 2.1 %collective-permute-start.2 = (bf16[1024,512]{1,0:T(8,128)(2,1)}, bf16[1024,512]{1,0:T(8,128)(2,1)S(1)}, u32[]{:S(2)}, u32[]{:S(2)}) collective-permute-start(bf16[1024,512]{1,0:T(8,128)(2,1)} %bitcast.7), channel_id=1, source_target_pairs={{0,1},{1,0},{2,3},{3,2},{4,5},{5,4},{6,7},{7,6},{8,9},{9,8},{10,11... | collective-permute-start | bytes 3145736 | tf_op jit(solution)/shard_map/ppermute | solution.py:265
  2.7 2.7 %shard_map.76 = (bf16[128,2048]{1,0:T(8,128)(2,1)S(1)}, bf16[128,2048]{1,0:T(8,128)(2,1)}, bf16[128,2048]{1,0:T(8,128)(2,1)}, bf16[128,2048]{1,0:T(8,128)(2,1)}) custom-call(s32[1]{0:T(128)} %bitcast.1.zl_ref, bf16[128,8192]{1,0:T(8,128)(2,1)} %x_ref.1), custom_call_target="tpu_custom_call" | custom-call | tf_op jit(solution)/shard_map/pallas_call | solution.py:56
  5.4 0.0 copy-start.3
  5.4 0.8 copy-done.3
  6.2 4.3 %collective-permute-start.1 = (bf16[128,2048]{1,0:T(8,128)(2,1)}, bf16[128,2048]{1,0:T(8,128)(2,1)S(1)}, u32[]{:S(2)}, u32[]{:S(2)}) collective-permute-start(bf16[128,2048]{1,0:T(8,128)(2,1)} %get-tuple-element.26), channel_id=1, source_target_pairs={{0,2},{2,0},{4,6},{6,4},{1,3},{3,1},{5,7},{7,5},{8,10},{10,8},{12,... | collective-permute-start | bytes 1572872 | tf_op jit(solution)/shard_map/ppermute | solution.py:254
  10.5 6.1 %collective-permute-start = (bf16[128,2048]{1,0:T(8,128)(2,1)}, bf16[128,2048]{1,0:T(8,128)(2,1)}, u32[]{:S(2)}, u32[]{:S(2)}) collective-permute-start(bf16[128,2048]{1,0:T(8,128)(2,1)} %get-tuple-element.25), channel_id=1, source_target_pairs={{0,4},{2,6},{4,0},{6,2},{1,5},{3,7},{5,1},{7,3},{8,12},{10,14},{12... | collective-permute-start | bytes 1572872 | tf_op jit(solution)/shard_map/ppermute | solution.py:254
  16.6 1.9 %collective-permute-start.5 = (bf16[128,2048]{1,0:T(8,128)(2,1)}, bf16[128,2048]{1,0:T(8,128)(2,1)}, u32[]{:S(2)}, u32[]{:S(2)}) collective-permute-start(bf16[128,2048]{1,0:T(8,128)(2,1)} %get-tuple-element.36), channel_id=1, source_target_pairs={{0,6},{2,4},{4,2},{6,0},{1,7},{3,5},{5,3},{7,1},{8,14},{10,12},{12... | collective-permute-start | bytes 1572872 | tf_op jit(solution)/shard_map/ppermute | solution.py:254
  18.5 0.0 copy-start.4
  18.5 1.0 copy-done.4
  19.6 0.2 shard_map.78.refs_0_
  19.8 0.0 collective-permute-done.2.other_ref
  19.8 0.0 copy-done
  19.8 0.4 shard_map.77.a_ref
  20.2 12.1 %collective-permute-done.1.x_ref = bf16[128,2048]{1,0:T(8,128)(2,1)S(1)} collective-permute-done((bf16[128,2048]{1,0:T(8,128)(2,1)}, bf16[128,2048]{1,0:T(8,128)(2,1)S(1)}, u32[]{:S(2)}, u32[]{:S(2)}) %collective-permute-start.1) | collective-permute-done | bytes 524320 | tf_op jit(solution)/shard_map/ppermute | solution.py:254
  32.4 0.0 copy-start.1
  32.4 0.4 shard_map.79
  32.8 0.3 copy-done.1
  33.2 1.9 %collective-permute-start.3 = (bf16[128,512]{1,0:T(8,128)(2,1)S(1)}, bf16[128,512]{1,0:T(8,128)(2,1)S(1)}, u32[]{:S(2)}, u32[]{:S(2)}) collective-permute-start(bf16[128,512]{1,0:T(8,128)(2,1)S(1)} %shard_map.79), channel_id=1, source_target_pairs={{0,2},{2,0},{4,6},{6,4},{1,3},{3,1},{5,7},{7,5},{8,10},{10,8},{12,... | collective-permute-start | bytes 393224 | tf_op jit(solution)/shard_map/ppermute | solution.py:254
  35.1 0.0 copy-start.2
  35.1 1.0 copy-done.2
  36.1 0.2 shard_map.80.refs_1_
  36.3 0.0 copy-start.7
  36.3 15.8 %collective-permute-done.x_ref = bf16[128,2048]{1,0:T(8,128)(2,1)} collective-permute-done((bf16[128,2048]{1,0:T(8,128)(2,1)}, bf16[128,2048]{1,0:T(8,128)(2,1)}, u32[]{:S(2)}, u32[]{:S(2)}) %collective-permute-start) | collective-permute-done | bytes 524320 | tf_op jit(solution)/shard_map/ppermute | solution.py:254
  52.2 1.7 collective-permute-done.3.b_ref
  53.9 1.5 shard_map.81
  55.3 2.9 %collective-permute-start.4 = (bf16[128,512]{1,0:T(8,128)(2,1)S(1)}, bf16[128,512]{1,0:T(8,128)(2,1)S(1)}, u32[]{:S(2)}, u32[]{:S(2)}) collective-permute-start(bf16[128,512]{1,0:T(8,128)(2,1)S(1)} %shard_map.81), channel_id=1, source_target_pairs={{0,4},{2,6},{4,0},{6,2},{1,5},{3,7},{5,1},{7,3},{8,12},{10,14},{12... | collective-permute-start | bytes 393224 | tf_op jit(solution)/shard_map/ppermute | solution.py:254
  58.3 0.0 collective-permute-done.5.x_ref
  58.3 1.5 shard_map.82
  59.8 3.8 %collective-permute-start.6 = (bf16[128,512]{1,0:T(8,128)(2,1)S(1)}, bf16[128,512]{1,0:T(8,128)(2,1)S(1)}, u32[]{:S(2)}, u32[]{:S(2)}) collective-permute-start(bf16[128,512]{1,0:T(8,128)(2,1)S(1)} %shard_map.82), channel_id=1, source_target_pairs={{0,6},{2,4},{4,2},{6,0},{1,7},{3,5},{5,3},{7,1},{8,14},{10,12},{12... | collective-permute-start | bytes 393224 | tf_op jit(solution)/shard_map/ppermute | solution.py:254
  63.6 7.7 %collective-permute-done.4.c_ref = bf16[128,512]{1,0:T(8,128)(2,1)S(1)} collective-permute-done((bf16[128,512]{1,0:T(8,128)(2,1)S(1)}, bf16[128,512]{1,0:T(8,128)(2,1)S(1)}, u32[]{:S(2)}, u32[]{:S(2)}) %collective-permute-start.4) | collective-permute-done | bytes 131104 | tf_op jit(solution)/shard_map/ppermute | solution.py:254
  71.3 0.0 collective-permute-done.6.d_ref
  71.3 0.0 copy-done.7
  71.3 0.2 shard_map.83.refs_4_
  71.6 8.5 %collective-permute-start.8 = (bf16[128,512]{1,0:T(8,128)(2,1)S(1)}, bf16[128,512]{1,0:T(8,128)(2,1)S(1)}, u32[]{:S(2)}, u32[]{:S(2)}) collective-permute-start(bf16[128,512]{1,0:T(8,128)(2,1)S(1)} %shard_map.83.refs_4_), channel_id=1, source_target_pairs={{0,2},{2,0},{4,6},{6,4},{1,3},{3,1},{5,7},{7,5},{8,10},{10,8},{12,... | collective-permute-start | bytes 393224 | tf_op jit(solution)/shard_map/ppermute | solution.py:254
  80.1 2.8 %collective-permute-start.7 = (bf16[128,512]{1,0:T(8,128)(2,1)S(1)}, bf16[128,512]{1,0:T(8,128)(2,1)S(1)}, u32[]{:S(2)}, u32[]{:S(2)}) collective-permute-start(bf16[128,512]{1,0:T(8,128)(2,1)S(1)} %shard_map.83.refs_4_), channel_id=1, source_target_pairs={{0,4},{2,6},{4,0},{6,2},{1,5},{3,7},{5,1},{7,3},{8,12},{10,14},{12... | collective-permute-start | bytes 393224 | tf_op jit(solution)/shard_map/ppermute | solution.py:254
  82.9 3.4 %collective-permute-start.9 = (bf16[128,512]{1,0:T(8,128)(2,1)S(1)}, bf16[128,512]{1,0:T(8,128)(2,1)S(1)}, u32[]{:S(2)}, u32[]{:S(2)}) collective-permute-start(bf16[128,512]{1,0:T(8,128)(2,1)S(1)} %shard_map.83.refs_4_), channel_id=1, source_target_pairs={{0,6},{2,4},{4,2},{6,0},{1,7},{3,5},{5,3},{7,1},{8,14},{10,12},{12... | collective-permute-start | bytes 393224 | tf_op jit(solution)/shard_map/ppermute | solution.py:254
  86.3 0.0 collective-permute-done.8.refs_5_
  86.3 1.2 shard_map.85.refs_3_
  87.5 2.0 %collective-permute-done.7.refs_6_ = bf16[128,512]{1,0:T(8,128)(2,1)S(1)} collective-permute-done((bf16[128,512]{1,0:T(8,128)(2,1)S(1)}, bf16[128,512]{1,0:T(8,128)(2,1)S(1)}, u32[]{:S(2)}, u32[]{:S(2)}) %collective-permute-start.7) | collective-permute-done | bytes 131104 | tf_op jit(solution)/shard_map/ppermute | solution.py:254
  89.6 1.2 shard_map.84.refs_2_
  90.8 0.9 collective-permute-done.9.refs_7_
  91.7 0.7 shard_map.87
  92.4 1.9 %collective-permute-start.10 = (bf16[1024,512]{1,0:T(8,128)(2,1)S(1)}, bf16[1024,512]{1,0:T(8,128)(2,1)S(1)}, u32[]{:S(2)}, u32[]{:S(2)}) collective-permute-start(bf16[1024,512]{1,0:T(8,128)(2,1)S(1)} %shard_map.87), channel_id=1, source_target_pairs={{0,1},{1,0},{2,3},{3,2},{4,5},{5,4},{6,7},{7,6},{8,9},{9,8},{10,11... | collective-permute-start | bytes 3145736 | tf_op jit(solution)/shard_map/ppermute | solution.py:289
  94.3 0.7 shard_map.86.s_ref
  95.0 1.9 %collective-permute-done.10.o_ref = bf16[1024,512]{1,0:T(8,128)(2,1)S(1)} collective-permute-done((bf16[1024,512]{1,0:T(8,128)(2,1)S(1)}, bf16[1024,512]{1,0:T(8,128)(2,1)S(1)}, u32[]{:S(2)}, u32[]{:S(2)}) %collective-permute-start.10) | collective-permute-done | bytes 1048608 | tf_op jit(solution)/shard_map/ppermute | solution.py:289
  97.0 1.3 shard_map.88.l_ref
  98.2 0.0 copy-start.5
  98.3 0.0 copy-start.6
  98.3 10.3 %all-to-all-start = ((bf16[32,32,512]{2,1,0:T(8,128)(2,1)}), bf16[32,32,512]{2,1,0:T(8,128)(2,1)S(1)}, u32[]{:S(2)}, u32[]{:S(2)}) async-start(bf16[32,32,512]{2,1,0:T(8,128)(2,1)} %bitcast.5), calls=%async_computation | async-start | bytes 2097152 | tf_op jit(solution)/shard_map/all_to_all | solution.py:291
  108.6 28.4 %all-to-all-done.l_ref = bf16[32,32,512]{2,1,0:T(8,128)(2,1)S(1)} async-done(((bf16[32,32,512]{2,1,0:T(8,128)(2,1)}), bf16[32,32,512]{2,1,0:T(8,128)(2,1)S(1)}, u32[]{:S(2)}, u32[]{:S(2)}) %all-to-all-start) | async-done | bytes 1048608 | tf_op jit(solution)/shard_map/all_to_all | solution.py:291
  137.0 0.0 copy-done.5
  137.0 0.0 copy-done.6
  137.0 0.1 shard_map.89
  137.1 8.8 %collective-permute-start.11 = (bf16[32,512]{1,0:T(8,128)(2,1)S(1)}, bf16[32,512]{1,0:T(8,128)(2,1)S(1)}, u32[]{:S(2)}, u32[]{:S(2)}) collective-permute-start(bf16[32,512]{1,0:T(8,128)(2,1)S(1)} %get-tuple-element.43), channel_id=1, source_target_pairs={{0,32},{32,0},{1,33},{33,1},{2,34},{34,2},{3,35},{35,3},{4,36},{36... | collective-permute-start | bytes 98312 | tf_op jit(solution)/shard_map/ppermute | solution.py:293
  145.9 1.9 %collective-permute-done.11.o_ref = bf16[32,512]{1,0:T(8,128)(2,1)S(1)} collective-permute-done((bf16[32,512]{1,0:T(8,128)(2,1)S(1)}, bf16[32,512]{1,0:T(8,128)(2,1)S(1)}, u32[]{:S(2)}, u32[]{:S(2)}) %collective-permute-start.11) | collective-permute-done | bytes 32800 | tf_op jit(solution)/shard_map/ppermute | solution.py:293
  147.8 0.6 shard_map.90
  148.4 31.5 %all_to_all.10 = bf16[32,32,512]{2,1,0:T(8,128)(2,1)S(1)} all-to-all(bf16[32,32,512]{2,1,0:T(8,128)(2,1)S(1)} %get-tuple-element.44), channel_id=1, replica_groups=mesh['y'=8,'zh'=2,'x'=4,'zl'=4,'core'=2] {'y','x'}, dimensions={0} | all-to-all | bytes 2097152 | tf_op jit(solution)/shard_map/all_to_all | solution.py:295
  179.9 2.3 %shard_map.91 = bf16[1,1024,512]{2,1,0:T(8,128)(2,1)} custom-call(bf16[8,4,2,16,512]{4,3,2,1,0:T(8,128)(2,1)} %shard_map.88.l_ref, bf16[8,4,2,16,512]{4,3,2,1,0:T(8,128)(2,1)S(1)} %bitcast.13), custom_call_target="tpu_custom_call" | custom-call | bytes 3145728 | tf_op jit(solution)/shard_map/pallas_call | solution.py:243
Async XLA Ops:
  0.6 19.1 %copy-start = (bf16[1,1024,512]{2,1,0:T(8,128)(2,1)S(1)}, bf16[1,1024,512]{2,1,0:T(8,128)(2,1)}, u32[]{:S(2)}) copy-start(bf16[1,1024,512]{2,1,0:T(8,128)(2,1)} %param.7) | copy-start | bytes 3145732
  0.6 19.1 %collective-permute-start.2 = (bf16[1024,512]{1,0:T(8,128)(2,1)}, bf16[1024,512]{1,0:T(8,128)(2,1)S(1)}, u32[]{:S(2)}, u32[]{:S(2)}) collective-permute-start(bf16[1024,512]{1,0:T(8,128)(2,1)} %bitcast.7), channel_id=1, source_target_pairs={{0,1},{1,0},{2,3},{3,2},{4,5},{5,4},{6,7},{7,6},{8,9},{9,8},{10,11... | collective-permute-start | bytes 3145736 | tf_op jit(solution)/shard_map/ppermute | solution.py:265
  5.4 0.8 copy-start.3
  6.2 26.1 %collective-permute-start.1 = (bf16[128,2048]{1,0:T(8,128)(2,1)}, bf16[128,2048]{1,0:T(8,128)(2,1)S(1)}, u32[]{:S(2)}, u32[]{:S(2)}) collective-permute-start(bf16[128,2048]{1,0:T(8,128)(2,1)} %get-tuple-element.26), channel_id=1, source_target_pairs={{0,2},{2,0},{4,6},{6,4},{1,3},{3,1},{5,7},{7,5},{8,10},{10,8},{12,... | collective-permute-start | bytes 1572872 | tf_op jit(solution)/shard_map/ppermute | solution.py:254
  10.5 41.7 %collective-permute-start = (bf16[128,2048]{1,0:T(8,128)(2,1)}, bf16[128,2048]{1,0:T(8,128)(2,1)}, u32[]{:S(2)}, u32[]{:S(2)}) collective-permute-start(bf16[128,2048]{1,0:T(8,128)(2,1)} %get-tuple-element.25), channel_id=1, source_target_pairs={{0,4},{2,6},{4,0},{6,2},{1,5},{3,7},{5,1},{7,3},{8,12},{10,14},{12... | collective-permute-start | bytes 1572872 | tf_op jit(solution)/shard_map/ppermute | solution.py:254
  16.6 41.7 %collective-permute-start.5 = (bf16[128,2048]{1,0:T(8,128)(2,1)}, bf16[128,2048]{1,0:T(8,128)(2,1)}, u32[]{:S(2)}, u32[]{:S(2)}) collective-permute-start(bf16[128,2048]{1,0:T(8,128)(2,1)} %get-tuple-element.36), channel_id=1, source_target_pairs={{0,6},{2,4},{4,2},{6,0},{1,7},{3,5},{5,3},{7,1},{8,14},{10,12},{12... | collective-permute-start | bytes 1572872 | tf_op jit(solution)/shard_map/ppermute | solution.py:254
  18.5 1.0 copy-start.4
  32.4 0.8 copy-start.1
  33.2 20.7 %collective-permute-start.3 = (bf16[128,512]{1,0:T(8,128)(2,1)S(1)}, bf16[128,512]{1,0:T(8,128)(2,1)S(1)}, u32[]{:S(2)}, u32[]{:S(2)}) collective-permute-start(bf16[128,512]{1,0:T(8,128)(2,1)S(1)} %shard_map.79), channel_id=1, source_target_pairs={{0,2},{2,0},{4,6},{6,4},{1,3},{3,1},{5,7},{7,5},{8,10},{10,8},{12,... | collective-permute-start | bytes 393224 | tf_op jit(solution)/shard_map/ppermute | solution.py:254
  35.1 1.0 copy-start.2
  36.3 35.0 %copy-start.7 = (bf16[128,512]{1,0:T(8,128)(2,1)S(1)}, bf16[128,512]{1,0:T(8,128)(2,1)}, u32[]{:S(2)}) copy-start(bf16[128,512]{1,0:T(8,128)(2,1)} %g_ref.1) | copy-start | bytes 393220
  55.3 16.0 %collective-permute-start.4 = (bf16[128,512]{1,0:T(8,128)(2,1)S(1)}, bf16[128,512]{1,0:T(8,128)(2,1)S(1)}, u32[]{:S(2)}, u32[]{:S(2)}) collective-permute-start(bf16[128,512]{1,0:T(8,128)(2,1)S(1)} %shard_map.81), channel_id=1, source_target_pairs={{0,4},{2,6},{4,0},{6,2},{1,5},{3,7},{5,1},{7,3},{8,12},{10,14},{12... | collective-permute-start | bytes 393224 | tf_op jit(solution)/shard_map/ppermute | solution.py:254
  59.8 11.5 %collective-permute-start.6 = (bf16[128,512]{1,0:T(8,128)(2,1)S(1)}, bf16[128,512]{1,0:T(8,128)(2,1)S(1)}, u32[]{:S(2)}, u32[]{:S(2)}) collective-permute-start(bf16[128,512]{1,0:T(8,128)(2,1)S(1)} %shard_map.82), channel_id=1, source_target_pairs={{0,6},{2,4},{4,2},{6,0},{1,7},{3,5},{5,3},{7,1},{8,14},{10,12},{12... | collective-permute-start | bytes 393224 | tf_op jit(solution)/shard_map/ppermute | solution.py:254
  71.6 14.7 %collective-permute-start.8 = (bf16[128,512]{1,0:T(8,128)(2,1)S(1)}, bf16[128,512]{1,0:T(8,128)(2,1)S(1)}, u32[]{:S(2)}, u32[]{:S(2)}) collective-permute-start(bf16[128,512]{1,0:T(8,128)(2,1)S(1)} %shard_map.83.refs_4_), channel_id=1, source_target_pairs={{0,2},{2,0},{4,6},{6,4},{1,3},{3,1},{5,7},{7,5},{8,10},{10,8},{12,... | collective-permute-start | bytes 393224 | tf_op jit(solution)/shard_map/ppermute | solution.py:254
  80.1 9.5 %collective-permute-start.7 = (bf16[128,512]{1,0:T(8,128)(2,1)S(1)}, bf16[128,512]{1,0:T(8,128)(2,1)S(1)}, u32[]{:S(2)}, u32[]{:S(2)}) collective-permute-start(bf16[128,512]{1,0:T(8,128)(2,1)S(1)} %shard_map.83.refs_4_), channel_id=1, source_target_pairs={{0,4},{2,6},{4,0},{6,2},{1,5},{3,7},{5,1},{7,3},{8,12},{10,14},{12... | collective-permute-start | bytes 393224 | tf_op jit(solution)/shard_map/ppermute | solution.py:254
  82.9 8.8 %collective-permute-start.9 = (bf16[128,512]{1,0:T(8,128)(2,1)S(1)}, bf16[128,512]{1,0:T(8,128)(2,1)S(1)}, u32[]{:S(2)}, u32[]{:S(2)}) collective-permute-start(bf16[128,512]{1,0:T(8,128)(2,1)S(1)} %shard_map.83.refs_4_), channel_id=1, source_target_pairs={{0,6},{2,4},{4,2},{6,0},{1,7},{3,5},{5,3},{7,1},{8,14},{10,12},{12... | collective-permute-start | bytes 393224 | tf_op jit(solution)/shard_map/ppermute | solution.py:254
  92.4 4.6 %collective-permute-start.10 = (bf16[1024,512]{1,0:T(8,128)(2,1)S(1)}, bf16[1024,512]{1,0:T(8,128)(2,1)S(1)}, u32[]{:S(2)}, u32[]{:S(2)}) collective-permute-start(bf16[1024,512]{1,0:T(8,128)(2,1)S(1)} %shard_map.87), channel_id=1, source_target_pairs={{0,1},{1,0},{2,3},{3,2},{4,5},{5,4},{6,7},{7,6},{8,9},{9,8},{10,11... | collective-permute-start | bytes 3145736 | tf_op jit(solution)/shard_map/ppermute | solution.py:289
  98.2 38.7 %copy-start.5 = (f32[1,16,512]{2,1,0:T(8,128)S(1)}, f32[1,16,512]{2,1,0:T(8,128)}, u32[]{:S(2)}) copy-start(f32[1,16,512]{2,1,0:T(8,128)} %a_ref.3) | copy-start | bytes 98308
  98.3 38.7 %copy-start.6 = (f32[1,16,512]{2,1,0:T(8,128)S(1)}, f32[1,16,512]{2,1,0:T(8,128)}, u32[]{:S(2)}) copy-start(f32[1,16,512]{2,1,0:T(8,128)} %m_ref.3) | copy-start | bytes 98308
  98.3 38.7 %all-to-all-start = ((bf16[32,32,512]{2,1,0:T(8,128)(2,1)}), bf16[32,32,512]{2,1,0:T(8,128)(2,1)S(1)}, u32[]{:S(2)}, u32[]{:S(2)}) async-start(bf16[32,32,512]{2,1,0:T(8,128)(2,1)} %bitcast.5), calls=%async_computation | async-start | bytes 2097152 | tf_op jit(solution)/shard_map/all_to_all | solution.py:291
  137.1 10.7 %collective-permute-start.11 = (bf16[32,512]{1,0:T(8,128)(2,1)S(1)}, bf16[32,512]{1,0:T(8,128)(2,1)S(1)}, u32[]{:S(2)}, u32[]{:S(2)}) collective-permute-start(bf16[32,512]{1,0:T(8,128)(2,1)S(1)} %get-tuple-element.43), channel_id=1, source_target_pairs={{0,32},{32,0},{1,33},{33,1},{2,34},{34,2},{3,35},{35,3},{4,36},{36... | collective-permute-start | bytes 98312 | tf_op jit(solution)/shard_map/ppermute | solution.py:293

commit v7 on v6

--- a/solution.py
+++ b/solution.py
@@ -52,18 +52,17 @@
 
 def slices(zl, tokens, distances):
     rows, width = tokens.shape
-    n = len(distances)
+    n, width = len(distances), width // SIZES[3]
     return call(
         functools.partial(slice_kernel, distances=distances),
-        (pltpu.VMEM((rows, width // SIZES[3]), BF),) * n,
-        limit=56 * 1024 * 1024,
+        (pltpu.VMEM((rows, width), BF),) * n,
         in_specs=[pl.BlockSpec(memory_space=pltpu.SMEM), pl.BlockSpec(memory_space=pl.ANY)],
         out_specs=(pl.BlockSpec(memory_space=pltpu.VMEM),) * n,
         scratch_shapes=[pltpu.SemaphoreType.DMA((n,))],
     )(zl.reshape(1), tokens)
 
 
-def project_kernel(core_ref, x_ref, own_ref, other_ref, out_ref):
+def project_kernel(core_ref, own_ref, other_ref, x_ref, out_ref):
     depth = own_ref.shape[0]
     mine = pl.ds(pl.multiple_of(core_ref[0] * depth, depth), depth)
     others = pl.ds(pl.multiple_of((1 - core_ref[0]) * depth, depth), depth)
@@ -73,16 +72,13 @@
 
 
 def project(core, x, own, other):
-    rows, depth = x.shape
-    features = own.shape[1]
     vmem = pl.BlockSpec(memory_space=pltpu.VMEM)
     return call(
         project_kernel,
-        jax.ShapeDtypeStruct((rows, features), BF),
-        flops=2 * rows * depth * features,
+        jax.ShapeDtypeStruct((x.shape[0], own.shape[1]), BF),
         in_specs=[pl.BlockSpec(memory_space=pltpu.SMEM)] + [vmem] * 3,
         out_specs=vmem,
-    )(core.reshape(1), x, own, other)
+    )(core.reshape(1), own, other, x)
 
 
 def norm_kernel(a_ref, b_ref, c_ref, d_ref, g_ref, out_ref):
@@ -114,10 +110,11 @@
     return call(flip_kernel, jax.ShapeDtypeStruct(x.shape[::-1], BF))(x)
 
 
-def grad_kernel(half_ref, *refs, block):
-    *refs, out_ref = refs
-    xs, ks = refs[: len(refs) // 2], refs[len(refs) // 2 :]
-    k = jnp.concatenate([ref[...] for ref in ks], axis=0)
+def grad_kernel(half_ref, zl_ref, *refs, block):
+    *xs, k_ref, out_ref = refs
+    rows = xs[0].shape[1]
+    starts = [pl.multiple_of((zl_ref[0] ^ k) * rows, rows) for k in range(len(xs))]
+    k = jnp.concatenate([k_ref[pl.ds(start, rows)] for start in starts], axis=0)
     depth = out_ref.shape[0]
     for i in range(depth // block):
         start = pl.multiple_of(half_ref[0] * depth + i * block, block)
@@ -126,17 +123,17 @@
         out_ref[pl.ds(i * block, block)] = grad.astype(out_ref.dtype)
 
 
-def gradient(half, xs, ks, dtype, block=256):
+def gradient(half, zl, xs, key_grads, dtype, block=256):
     depth, rows = xs[0].shape
-    features = ks[0].shape[1]
-    vmem = pl.BlockSpec(memory_space=pltpu.VMEM)
+    features = key_grads.shape[1]
+    smem, vmem = (pl.BlockSpec(memory_space=space) for space in (pltpu.SMEM, pltpu.VMEM))
     return call(
         functools.partial(grad_kernel, block=block),
         pltpu.VMEM((depth // 2, features), dtype),
         flops=len(xs) * depth * rows * features,
-        in_specs=[pl.BlockSpec(memory_space=pltpu.SMEM)] + [vmem] * (2 * len(xs)),
+        in_specs=[smem, smem] + [vmem] * (len(xs) + 1),
         out_specs=vmem,
-    )(half.reshape(1), *xs, *ks)
+    )(half.reshape(1), zl.reshape(1), *xs, key_grads)
 
 
 def inner_kernel(s_ref, o_ref, w_ref, out_ref):
@@ -163,38 +160,37 @@
     )(same, other, w)
 
 
-def total_kernel(zh_ref, l_ref, a_ref, m_ref, out_ref, low_ref):
-    own = a_ref.shape[1]
+def total_kernel(zh_ref, l_ref, held_ref, out_ref, low_ref):
+    own = held_ref.shape[2]
     total = l_ref[0].astype(F32)
     for i in range(1, l_ref.shape[0]):
         total += l_ref[i].astype(F32)
     out_ref[...] = total
     low_ref[...] = total.astype(BF)
     rows = pl.ds(pl.multiple_of(zh_ref[0] * own, own), own)
-    from_base = (1.0 - SHARE) * a_ref[0] - OUTER_RATE * MOMENT * MOMENT * m_ref[0]
+    from_base = (1.0 - SHARE) * held_ref[0, 0] - OUTER_RATE * MOMENT * MOMENT * held_ref[1, 0]
     low_ref[rows] = (out_ref[rows] + from_base * (N_REP / SHARE)).astype(BF)
 
 
-def half_total(zh, shares, anchor, momentum):
+def half_total(zh, shares, held):
     shape = shares.shape[1:]
-    vmem = pl.BlockSpec(memory_space=pltpu.VMEM)
+    smem, vmem = (pl.BlockSpec(memory_space=space) for space in (pltpu.SMEM, pltpu.VMEM))
     return call(
         total_kernel,
         (jax.ShapeDtypeStruct(shape, F32), jax.ShapeDtypeStruct(shape, BF)),
-        moved=2 * shares.size,
-        in_specs=[pl.BlockSpec(memory_space=pltpu.SMEM)] + [vmem] * 3,
+        in_specs=[smem, vmem, vmem],
         out_specs=(vmem,) * 2,
-    )(zh.reshape(1), shares, anchor, momentum)
-
-
-def outer_kernel(zh_ref, s_ref, o_ref, a_ref, m_ref, base_ref, mom_ref, all_ref):
-    own = a_ref.shape[1]
+    )(zh.reshape(1), shares, held)
+
+
+def outer_kernel(zh_ref, s_ref, o_ref, held_ref, base_ref, mom_ref, all_ref):
+    own = held_ref.shape[2]
     rows = pl.ds(pl.multiple_of(zh_ref[0] * own, own), own)
     partner_rows = pl.ds(pl.multiple_of((1 - zh_ref[0]) * own, own), own)
     average = (s_ref[rows] + o_ref[rows].astype(F32)) / N_REP
-    base = a_ref[0]
+    base = held_ref[0, 0]
     delta = base - average
-    new_mom = MOMENT * m_ref[0] + delta
+    new_mom = MOMENT * held_ref[1, 0] + delta
     new_base = base - OUTER_RATE * (delta + MOMENT * new_mom)
     mom_ref[0] = new_mom
     base_ref[0] = new_base
@@ -205,19 +201,24 @@
         all_ref[i, partner_rows] = partner_low
 
 
-def outer_step(zh, total, other, anchor, momentum, n):
-    vmem = pl.BlockSpec(memory_space=pltpu.VMEM)
+def outer_step(zh, total, other, held, n):
+    smem, vmem = (pl.BlockSpec(memory_space=space) for space in (pltpu.SMEM, pltpu.VMEM))
+    shape = jax.ShapeDtypeStruct(held.shape[1:], F32)
     return call(
         outer_kernel,
-        (
-            jax.ShapeDtypeStruct(anchor.shape, F32),
-            jax.ShapeDtypeStruct(anchor.shape, F32),
-            jax.ShapeDtypeStruct((n, *total.shape), BF),
-        ),
-        moved=2 * n * total.size,
-        in_specs=[pl.BlockSpec(memory_space=pltpu.SMEM)] + [vmem] * 4,
+        (shape, shape, jax.ShapeDtypeStruct((n, *total.shape), BF)),
+        in_specs=[smem] + [vmem] * 3,
         out_specs=(vmem,) * 3,
-    )(zh.reshape(1), total, other, anchor, momentum)
+    )(zh.reshape(1), total, other, held)
+
+
+def hold_kernel(a_ref, m_ref, out_ref):
+    out_ref[0] = a_ref[...]
+    out_ref[1] = m_ref[...]
+
+
+def hold(anchor, momentum):
+    return call(hold_kernel, pltpu.VMEM((2, *anchor.shape), F32))(anchor, momentum)
 
 
 def mix_kernel(l_ref, b_ref, out_ref, held_ref, sems):
@@ -259,39 +260,33 @@
     depth, features = own.shape
     width = tokens.shape[1] // SIZES[3]
     core, zl, zh = (lax.axis_index(name) for name in ("core", "zl", "zh"))
-    got = dict(enumerate(slices(zl, tokens, (0, 1, 2, 3))))
-    for k in (3, 2, 1):
-        got[k] = across(got[k], "zl", k)
+    got = [None] + [across(x, "zl", k) for k, x in zip((1, 2, 3), slices(zl, tokens, (1, 2, 3)))]
     swapped = lax.ppermute(own, "core", SWAP)
-
-    def partial(k):
-        return project(core, got[k], own, swapped)
-
-    turned = {0: flip(got[0])}
-    parts = [partial(0)]
-    got[1], parts, turned = lax.optimization_barrier((got[1], parts, turned))
-    parts.append(across(partial(1), "zl", 1))
-    turned[1] = flip(got[1])
-    got[2], parts, turned = lax.optimization_barrier((got[2], parts, turned))
-    made = partial(2)
-    parts.append(across(made, "zl", 2))
-    got[3], made = lax.optimization_barrier((got[3], made))
-    parts.append(across(partial(3), "zl", 3))
+    held = hold(anchor, momentum)
+    (got[0],) = slices(zl, tokens, (0,))
+    got[0], held = lax.optimization_barrier((got[0], held))
+    parts = [project(core, got[0], own, swapped)]
+    turned = [flip(got[0])]
+    got[2], got[1], parts, turned = lax.optimization_barrier((got[2], got[1], parts, turned))
+    made = project(core, got[1], own, swapped)
+    parts.append(across(made, "zl", 1))
+    for k in (2, 3):
+        got[k], made = lax.optimization_barrier((got[k], made))
+        made = project(core, got[k], own, swapped)
+        parts.append(across(made, "zl", k))
+    got, made = lax.optimization_barrier((got, made))
+    turned += [flip(x) for x in got[1:]]
+    parts, turned = lax.optimization_barrier((parts, turned))
     key_grad = norm_grad(parts, cotangent)
-    ks = [key_grad] + [across(key_grad, "zl", k) for k in (1, 2, 3)]
-    for k, near in ((3, 1), (2, 2)):
-        got[k], ks[near] = lax.optimization_barrier((got[k], ks[near]))
-        turned[k] = flip(got[k])
-    xs = [turned[k] for k in range(4)]
-    xs = [turned[k] for k in range(4)]
-    send = gradient(1 - core, xs, ks, BF)
-    same = gradient(core, xs, ks, F32)
+    key_grads = lax.all_gather(key_grad, "zl", axis=0, tiled=True)
+    send = gradient(1 - core, zl, turned, key_grads, BF)
+    same = gradient(core, zl, turned, key_grads, F32)
     local = inner_step(same, lax.ppermute(send, "core", SWAP), own)
     ny, nx, nz, rows, _ = local.shape
     shares = lax.all_to_all(local.reshape(ny * nx, nz * rows, features), ("y", "x"), 0, 0, tiled=True)
-    total, low = half_total(zh, shares, anchor, momentum)
+    total, low = half_total(zh, shares, held)
     partner_total = lax.ppermute(low, "zh", SWAP)
-    new_base, new_mom, spread = outer_step(zh, total, partner_total, anchor, momentum, ny * nx)
+    new_base, new_mom, spread = outer_step(zh, total, partner_total, held, ny * nx)
     base = lax.all_to_all(spread, ("y", "x"), 0, 0, tiled=True).reshape(local.shape)
     return mix(local, base), new_base, new_mom
 

time: 184 us -> 179 us (0.973)
  blocking collectives: 31.5 us -> 47.7 us
  starting transfers between devices: 58.7 us -> 45.2 us
  waiting for transfers between devices: 72.4 us -> 63.7 us
    all_gather x0 -> x1, blocking collectives: none -> 16.1 us  [body(): key_grads = lax.all_gather(key_grad, 'zl', axis=0, tiled=True)]
    ppermute x9 -> x6, starting transfers between devices: 35.6 us -> 22.7 us  [across(): return lax.ppermute(value, axis, [(i, i ^ k) for i in range(4)])]
    ppermute x9 -> x6, waiting for transfers between devices: 40.3 us -> 31.5 us  [across(): return lax.ppermute(value, axis, [(i, i ^ k) for i in range(4)])]
    pallas_call x5 -> x6, Pallas kernels: 4.51 us -> 5.56 us  [the longest x4 4.91 us: project(): call(project_kernel, jax.ShapeDtypeStruct((x.shape[0], own.shape[1]), BF)...]
  transfers between devices with their start and end apart: 13 -> 10, of which waited for: 9 -> 6; matrix products, arithmetic and copies ran while one was open for 0% -> 0% of each run, Pallas kernels for 6% -> 6%
where the time goes in v7:
time: 179 us; the launch traced here: 178 us
  waiting for transfers between devices  63.7 us (36%)
  blocking collectives  47.7 us (27%)
  starting transfers between devices  45.2 us (25%)
  Pallas kernels  17.2 us (10%)
  local copies, waits for them, and re-layouts  3.19 us (2%)
    all_to_all x1, blocking collectives, body(): lax.all_to_all(spread, ('y', 'x'), 0, 0, tiled=True).reshape(local.shape)  31.6 us
    ppermute x6, waiting for transfers between devices, across(): return lax.ppermute(value, axis, [(i, i ^ k) for i in range(4)])  31.5 us
    all_to_all x1, waiting for transfers between devices, body(): lax.all_to_all(local.reshape(ny * nx, nz * rows, features), ('y', 'x'), 0...  28.4 us
    ppermute x6, starting transfers between devices, across(): return lax.ppermute(value, axis, [(i, i ^ k) for i in range(4)])  22.7 us
    all_gather x1, blocking collectives, body(): key_grads = lax.all_gather(key_grad, 'zl', axis=0, tiled=True)  16.1 us
    all_to_all x1, starting transfers between devices, body(): lax.all_to_all(local.reshape(ny * nx, nz * rows, features), ('y', 'x'), 0...  10.2 us
    ppermute x1, starting transfers between devices, body(): partner_total = lax.ppermute(low, 'zh', SWAP)  8.48 us
    pallas_call x4, Pallas kernels, project(): call(project_kernel, jax.ShapeDtypeStruct((x.shape[0], own.shape[1]), BF)...  4.91 us
  transfers between devices with their start and end apart: 10, of which 6 were waited for; matrix products, arithmetic and copies ran while one was open for 0% of the time, Pallas kernels for 6%

profile of v7, /device:TPU:6, one launch (start us, length us, event | category | flops | bytes accessed | tf_op | source)
XLA Modules:
  0.0 177.8 jit_solution(5807185634995847170)
XLA Ops:
  0.6 1.9 %collective-permute-start.2 = (bf16[1024,512]{1,0:T(8,128)(2,1)}, bf16[1024,512]{1,0:T(8,128)(2,1)S(1)}, u32[]{:S(2)}, u32[]{:S(2)}) collective-permute-start(bf16[1024,512]{1,0:T(8,128)(2,1)} %bitcast.7), channel_id=1, source_target_pairs={{0,1},{1,0},{2,3},{3,2},{4,5},{5,4},{6,7},{7,6},{8,9},{9,8},{10,11... | collective-permute-start | bytes 3145736 | tf_op jit(solution)/shard_map/ppermute | solution.py:264
  2.6 0.0 copy-start.1
  2.6 1.6 copy-done.1
  4.2 0.0 copy-start.4
  4.2 0.0 copy-start.5
  4.2 1.3 shard_map.76
  5.5 0.0 copy-start
  5.5 6.2 %collective-permute-start = (bf16[128,2048]{1,0:T(8,128)(2,1)}, bf16[128,2048]{1,0:T(8,128)(2,1)}, u32[]{:S(2)}, u32[]{:S(2)}) collective-permute-start(bf16[128,2048]{1,0:T(8,128)(2,1)} %get-tuple-element.30), channel_id=1, source_target_pairs={{0,4},{2,6},{4,0},{6,2},{1,5},{3,7},{5,1},{7,3},{8,12},{10,14},{12... | collective-permute-start | bytes 1572872 | tf_op jit(solution)/shard_map/ppermute | solution.py:255
  11.7 4.3 %collective-permute-start.1 = (bf16[128,2048]{1,0:T(8,128)(2,1)}, bf16[128,2048]{1,0:T(8,128)(2,1)}, u32[]{:S(2)}, u32[]{:S(2)}) collective-permute-start(bf16[128,2048]{1,0:T(8,128)(2,1)} %get-tuple-element.31), channel_id=1, source_target_pairs={{0,2},{2,0},{4,6},{6,4},{1,3},{3,1},{5,7},{7,5},{8,10},{10,8},{12,... | collective-permute-start | bytes 1572872 | tf_op jit(solution)/shard_map/ppermute | solution.py:255
  16.0 1.9 %collective-permute-start.5 = (bf16[128,2048]{1,0:T(8,128)(2,1)}, bf16[128,2048]{1,0:T(8,128)(2,1)}, u32[]{:S(2)}, u32[]{:S(2)}) collective-permute-start(bf16[128,2048]{1,0:T(8,128)(2,1)} %get-tuple-element.37), channel_id=1, source_target_pairs={{0,6},{2,4},{4,2},{6,0},{1,7},{3,5},{5,3},{7,1},{8,14},{10,12},{12... | collective-permute-start | bytes 1572872 | tf_op jit(solution)/shard_map/ppermute | solution.py:255
  17.9 0.0 copy-start.2
  17.9 1.6 copy-done.2
  19.6 0.0 copy-done.4
  19.6 0.0 copy-done.5
  19.6 0.2 shard_map.80.refs_0_
  19.8 0.0 collective-permute-done.2.other_ref
  19.8 0.0 copy-done
  19.8 0.5 shard_map.79.a_ref
  20.3 15.8 %collective-permute-done.x_ref = bf16[128,2048]{1,0:T(8,128)(2,1)} collective-permute-done((bf16[128,2048]{1,0:T(8,128)(2,1)}, bf16[128,2048]{1,0:T(8,128)(2,1)}, u32[]{:S(2)}, u32[]{:S(2)}) %collective-permute-start) | collective-permute-done | bytes 524320 | tf_op jit(solution)/shard_map/ppermute | solution.py:255
  36.1 13.1 %collective-permute-done.1.x_ref = bf16[128,2048]{1,0:T(8,128)(2,1)} collective-permute-done((bf16[128,2048]{1,0:T(8,128)(2,1)}, bf16[128,2048]{1,0:T(8,128)(2,1)}, u32[]{:S(2)}, u32[]{:S(2)}) %collective-permute-start.1) | collective-permute-done | bytes 524320 | tf_op jit(solution)/shard_map/ppermute | solution.py:255
  49.2 1.5 shard_map.81
  50.7 1.9 %collective-permute-start.3 = (bf16[128,512]{1,0:T(8,128)(2,1)S(1)}, bf16[128,512]{1,0:T(8,128)(2,1)S(1)}, u32[]{:S(2)}, u32[]{:S(2)}) collective-permute-start(bf16[128,512]{1,0:T(8,128)(2,1)S(1)} %shard_map.81), channel_id=1, source_target_pairs={{0,2},{2,0},{4,6},{6,4},{1,3},{3,1},{5,7},{7,5},{8,10},{10,8},{12,... | collective-permute-start | bytes 393224 | tf_op jit(solution)/shard_map/ppermute | solution.py:255
  52.6 1.5 shard_map.82
  54.1 5.7 %collective-permute-start.4 = (bf16[128,512]{1,0:T(8,128)(2,1)S(1)}, bf16[128,512]{1,0:T(8,128)(2,1)}, u32[]{:S(2)}, u32[]{:S(2)}) collective-permute-start(bf16[128,512]{1,0:T(8,128)(2,1)S(1)} %shard_map.82), channel_id=1, source_target_pairs={{0,4},{2,6},{4,0},{6,2},{1,5},{3,7},{5,1},{7,3},{8,12},{10,14},{12... | collective-permute-start | bytes 393224 | tf_op jit(solution)/shard_map/ppermute | solution.py:255
  59.8 0.0 collective-permute-done.5.x_ref
  59.8 1.5 shard_map.83
  61.3 0.0 copy-start.3
  61.3 2.6 %collective-permute-start.6 = (bf16[128,512]{1,0:T(8,128)(2,1)S(1)}, bf16[128,512]{1,0:T(8,128)(2,1)}, u32[]{:S(2)}, u32[]{:S(2)}) collective-permute-start(bf16[128,512]{1,0:T(8,128)(2,1)S(1)} %shard_map.83), channel_id=1, source_target_pairs={{0,6},{2,4},{4,2},{6,0},{1,7},{3,5},{5,3},{7,1},{8,14},{10,12},{12... | collective-permute-start | bytes 393224 | tf_op jit(solution)/shard_map/ppermute | solution.py:255
  64.0 1.2 shard_map.84.refs_1_
  65.2 1.2 shard_map.85.refs_2_
  66.4 1.2 shard_map.86.refs_3_
  67.7 0.0 collective-permute-done.4.c_ref
  67.7 0.0 collective-permute-done.3.b_ref
  67.7 2.6 %collective-permute-done.6.d_ref = bf16[128,512]{1,0:T(8,128)(2,1)} collective-permute-done((bf16[128,512]{1,0:T(8,128)(2,1)S(1)}, bf16[128,512]{1,0:T(8,128)(2,1)}, u32[]{:S(2)}, u32[]{:S(2)}) %collective-permute-start.6) | collective-permute-done | bytes 131104 | tf_op jit(solution)/shard_map/ppermute | solution.py:255
  70.3 0.0 copy-done.3
  70.3 1.2 shard_map.87
  71.5 16.1 %all_gather.3.refs_4_ = bf16[512,512]{1,0:T(8,128)(2,1)S(1)} all-gather(bf16[128,512]{1,0:T(8,128)(2,1)S(1)} %shard_map.87), channel_id=1, replica_groups=mesh['y'=8,'zh'=2,'x'=4,'zl'=4,'core'=2] {'zl'}, dimensions={0}, use_global_device_ids=true | all-gather | bytes 655360 | tf_op jit(solution)/shard_map/all_gather | solution.py:281
  87.6 0.7 shard_map.89
  88.4 1.9 %collective-permute-start.7 = (bf16[1024,512]{1,0:T(8,128)(2,1)S(1)}, bf16[1024,512]{1,0:T(8,128)(2,1)S(1)}, u32[]{:S(2)}, u32[]{:S(2)}) collective-permute-start(bf16[1024,512]{1,0:T(8,128)(2,1)S(1)} %shard_map.89), channel_id=1, source_target_pairs={{0,1},{1,0},{2,3},{3,2},{4,5},{5,4},{6,7},{7,6},{8,9},{9,8},{10,11... | collective-permute-start | bytes 3145736 | tf_op jit(solution)/shard_map/ppermute | solution.py:284
  90.3 0.7 shard_map.88.s_ref
  91.0 1.9 %collective-permute-done.7.o_ref = bf16[1024,512]{1,0:T(8,128)(2,1)S(1)} collective-permute-done((bf16[1024,512]{1,0:T(8,128)(2,1)S(1)}, bf16[1024,512]{1,0:T(8,128)(2,1)S(1)}, u32[]{:S(2)}, u32[]{:S(2)}) %collective-permute-start.7) | collective-permute-done | bytes 1048608 | tf_op jit(solution)/shard_map/ppermute | solution.py:284
  92.9 1.3 shard_map.90.l_ref
  94.2 10.2 %all-to-all-start = ((bf16[32,32,512]{2,1,0:T(8,128)(2,1)}), bf16[32,32,512]{2,1,0:T(8,128)(2,1)S(1)}, u32[]{:S(2)}, u32[]{:S(2)}) async-start(bf16[32,32,512]{2,1,0:T(8,128)(2,1)} %bitcast.5), calls=%async_computation | async-start | bytes 2097152 | tf_op jit(solution)/shard_map/all_to_all | solution.py:286
  104.4 28.4 %all-to-all-done.l_ref = bf16[32,32,512]{2,1,0:T(8,128)(2,1)S(1)} async-done(((bf16[32,32,512]{2,1,0:T(8,128)(2,1)}), bf16[32,32,512]{2,1,0:T(8,128)(2,1)S(1)}, u32[]{:S(2)}, u32[]{:S(2)}) %all-to-all-start) | async-done | bytes 1048608 | tf_op jit(solution)/shard_map/all_to_all | solution.py:286
  132.8 0.1 shard_map.91
  133.0 8.5 %collective-permute-start.8 = (bf16[32,512]{1,0:T(8,128)(2,1)S(1)}, bf16[32,512]{1,0:T(8,128)(2,1)S(1)}, u32[]{:S(2)}, u32[]{:S(2)}) collective-permute-start(bf16[32,512]{1,0:T(8,128)(2,1)S(1)} %get-tuple-element.53), channel_id=1, source_target_pairs={{0,32},{32,0},{1,33},{33,1},{2,34},{34,2},{3,35},{35,3},{4,36},{36... | collective-permute-start | bytes 98312 | tf_op jit(solution)/shard_map/ppermute | solution.py:288
  141.4 1.9 %collective-permute-done.8.o_ref = bf16[32,512]{1,0:T(8,128)(2,1)S(1)} collective-permute-done((bf16[32,512]{1,0:T(8,128)(2,1)S(1)}, bf16[32,512]{1,0:T(8,128)(2,1)S(1)}, u32[]{:S(2)}, u32[]{:S(2)}) %collective-permute-start.8) | collective-permute-done | bytes 32800 | tf_op jit(solution)/shard_map/ppermute | solution.py:288
  143.3 0.6 shard_map.92
  144.0 31.6 %all_to_all.10 = bf16[32,32,512]{2,1,0:T(8,128)(2,1)S(1)} all-to-all(bf16[32,32,512]{2,1,0:T(8,128)(2,1)S(1)} %get-tuple-element.54), channel_id=1, replica_groups=mesh['y'=8,'zh'=2,'x'=4,'zl'=4,'core'=2] {'y','x'}, dimensions={0} | all-to-all | bytes 2097152 | tf_op jit(solution)/shard_map/all_to_all | solution.py:290
  175.5 2.3 %shard_map.93 = bf16[1,1024,512]{2,1,0:T(8,128)(2,1)} custom-call(bf16[8,4,2,16,512]{4,3,2,1,0:T(8,128)(2,1)} %shard_map.90.l_ref, bf16[8,4,2,16,512]{4,3,2,1,0:T(8,128)(2,1)S(1)} %bitcast.13), custom_call_target="tpu_custom_call" | custom-call | bytes 3145728 | tf_op jit(solution)/shard_map/pallas_call | solution.py:244
  (2 shorter events, 0.1 us)
Async XLA Ops:
  0.6 19.2 %collective-permute-start.2 = (bf16[1024,512]{1,0:T(8,128)(2,1)}, bf16[1024,512]{1,0:T(8,128)(2,1)S(1)}, u32[]{:S(2)}, u32[]{:S(2)}) collective-permute-start(bf16[1024,512]{1,0:T(8,128)(2,1)} %bitcast.7), channel_id=1, source_target_pairs={{0,1},{1,0},{2,3},{3,2},{4,5},{5,4},{6,7},{7,6},{8,9},{9,8},{10,11... | collective-permute-start | bytes 3145736 | tf_op jit(solution)/shard_map/ppermute | solution.py:264
  2.6 1.6 copy-start.1
  4.2 15.4 %copy-start.4 = (f32[1,16,512]{2,1,0:T(8,128)S(1)}, f32[1,16,512]{2,1,0:T(8,128)}, u32[]{:S(2)}) copy-start(f32[1,16,512]{2,1,0:T(8,128)} %a_ref.1) | copy-start | bytes 98308
  4.2 15.4 %copy-start.5 = (f32[1,16,512]{2,1,0:T(8,128)S(1)}, f32[1,16,512]{2,1,0:T(8,128)}, u32[]{:S(2)}) copy-start(f32[1,16,512]{2,1,0:T(8,128)} %m_ref.1) | copy-start | bytes 98308
  5.5 14.4 %copy-start = (bf16[1,1024,512]{2,1,0:T(8,128)(2,1)S(1)}, bf16[1,1024,512]{2,1,0:T(8,128)(2,1)}, u32[]{:S(2)}) copy-start(bf16[1,1024,512]{2,1,0:T(8,128)(2,1)} %param.7) | copy-start | bytes 3145732
  5.5 30.6 %collective-permute-start = (bf16[128,2048]{1,0:T(8,128)(2,1)}, bf16[128,2048]{1,0:T(8,128)(2,1)}, u32[]{:S(2)}, u32[]{:S(2)}) collective-permute-start(bf16[128,2048]{1,0:T(8,128)(2,1)} %get-tuple-element.30), channel_id=1, source_target_pairs={{0,4},{2,6},{4,0},{6,2},{1,5},{3,7},{5,1},{7,3},{8,12},{10,14},{12... | collective-permute-start | bytes 1572872 | tf_op jit(solution)/shard_map/ppermute | solution.py:255
  11.7 37.5 %collective-permute-start.1 = (bf16[128,2048]{1,0:T(8,128)(2,1)}, bf16[128,2048]{1,0:T(8,128)(2,1)}, u32[]{:S(2)}, u32[]{:S(2)}) collective-permute-start(bf16[128,2048]{1,0:T(8,128)(2,1)} %get-tuple-element.31), channel_id=1, source_target_pairs={{0,2},{2,0},{4,6},{6,4},{1,3},{3,1},{5,7},{7,5},{8,10},{10,8},{12,... | collective-permute-start | bytes 1572872 | tf_op jit(solution)/shard_map/ppermute | solution.py:255
  16.0 43.8 %collective-permute-start.5 = (bf16[128,2048]{1,0:T(8,128)(2,1)}, bf16[128,2048]{1,0:T(8,128)(2,1)}, u32[]{:S(2)}, u32[]{:S(2)}) collective-permute-start(bf16[128,2048]{1,0:T(8,128)(2,1)} %get-tuple-element.37), channel_id=1, source_target_pairs={{0,6},{2,4},{4,2},{6,0},{1,7},{3,5},{5,3},{7,1},{8,14},{10,12},{12... | collective-permute-start | bytes 1572872 | tf_op jit(solution)/shard_map/ppermute | solution.py:255
  17.9 1.6 copy-start.2
  50.7 17.0 %collective-permute-start.3 = (bf16[128,512]{1,0:T(8,128)(2,1)S(1)}, bf16[128,512]{1,0:T(8,128)(2,1)S(1)}, u32[]{:S(2)}, u32[]{:S(2)}) collective-permute-start(bf16[128,512]{1,0:T(8,128)(2,1)S(1)} %shard_map.81), channel_id=1, source_target_pairs={{0,2},{2,0},{4,6},{6,4},{1,3},{3,1},{5,7},{7,5},{8,10},{10,8},{12,... | collective-permute-start | bytes 393224 | tf_op jit(solution)/shard_map/ppermute | solution.py:255
  54.1 13.6 %collective-permute-start.4 = (bf16[128,512]{1,0:T(8,128)(2,1)S(1)}, bf16[128,512]{1,0:T(8,128)(2,1)}, u32[]{:S(2)}, u32[]{:S(2)}) collective-permute-start(bf16[128,512]{1,0:T(8,128)(2,1)S(1)} %shard_map.82), channel_id=1, source_target_pairs={{0,4},{2,6},{4,0},{6,2},{1,5},{3,7},{5,1},{7,3},{8,12},{10,14},{12... | collective-permute-start | bytes 393224 | tf_op jit(solution)/shard_map/ppermute | solution.py:255
  61.3 9.0 %copy-start.3 = (bf16[128,512]{1,0:T(8,128)(2,1)S(1)}, bf16[128,512]{1,0:T(8,128)(2,1)}, u32[]{:S(2)}) copy-start(bf16[128,512]{1,0:T(8,128)(2,1)} %g_ref.1) | copy-start | bytes 393220
  61.3 9.0 %collective-permute-start.6 = (bf16[128,512]{1,0:T(8,128)(2,1)S(1)}, bf16[128,512]{1,0:T(8,128)(2,1)}, u32[]{:S(2)}, u32[]{:S(2)}) collective-permute-start(bf16[128,512]{1,0:T(8,128)(2,1)S(1)} %shard_map.83), channel_id=1, source_target_pairs={{0,6},{2,4},{4,2},{6,0},{1,7},{3,5},{5,3},{7,1},{8,14},{10,12},{12... | collective-permute-start | bytes 393224 | tf_op jit(solution)/shard_map/ppermute | solution.py:255
  88.4 4.6 %collective-permute-start.7 = (bf16[1024,512]{1,0:T(8,128)(2,1)S(1)}, bf16[1024,512]{1,0:T(8,128)(2,1)S(1)}, u32[]{:S(2)}, u32[]{:S(2)}) collective-permute-start(bf16[1024,512]{1,0:T(8,128)(2,1)S(1)} %shard_map.89), channel_id=1, source_target_pairs={{0,1},{1,0},{2,3},{3,2},{4,5},{5,4},{6,7},{7,6},{8,9},{9,8},{10,11... | collective-permute-start | bytes 3145736 | tf_op jit(solution)/shard_map/ppermute | solution.py:284
  94.2 38.6 %all-to-all-start = ((bf16[32,32,512]{2,1,0:T(8,128)(2,1)}), bf16[32,32,512]{2,1,0:T(8,128)(2,1)S(1)}, u32[]{:S(2)}, u32[]{:S(2)}) async-start(bf16[32,32,512]{2,1,0:T(8,128)(2,1)} %bitcast.5), calls=%async_computation | async-start | bytes 2097152 | tf_op jit(solution)/shard_map/all_to_all | solution.py:286
  133.0 10.4 %collective-permute-start.8 = (bf16[32,512]{1,0:T(8,128)(2,1)S(1)}, bf16[32,512]{1,0:T(8,128)(2,1)S(1)}, u32[]{:S(2)}, u32[]{:S(2)}) collective-permute-start(bf16[32,512]{1,0:T(8,128)(2,1)S(1)} %get-tuple-element.53), channel_id=1, source_target_pairs={{0,32},{32,0},{1,33},{33,1},{2,34},{34,2},{3,35},{35,3},{4,36},{36... | collective-permute-start | bytes 98312 | tf_op jit(solution)/shard_map/ppermute | solution.py:288

commit v8 on v7

--- a/solution.py
+++ b/solution.py
@@ -187,7 +187,8 @@
     own = held_ref.shape[2]
     rows = pl.ds(pl.multiple_of(zh_ref[0] * own, own), own)
     partner_rows = pl.ds(pl.multiple_of((1 - zh_ref[0]) * own, own), own)
-    average = (s_ref[rows] + o_ref[rows].astype(F32)) / N_REP
+    partner = 1 - zh_ref[0]
+    average = (s_ref[rows] + o_ref[partner, rows].astype(F32)) / N_REP
     base = held_ref[0, 0]
     delta = base - average
     new_mom = MOMENT * held_ref[1, 0] + delta
@@ -195,7 +196,7 @@
     mom_ref[0] = new_mom
     base_ref[0] = new_base
     low = new_base.astype(BF)
-    partner_low = ((s_ref[partner_rows] + o_ref[partner_rows].astype(F32)) * (SHARE / N_REP)).astype(BF)
+    partner_low = ((s_ref[partner_rows] + o_ref[partner, partner_rows].astype(F32)) * (SHARE / N_REP)).astype(BF)
     for i in range(all_ref.shape[0]):
         all_ref[i, rows] = low
         all_ref[i, partner_rows] = partner_low
@@ -268,12 +269,12 @@
     parts = [project(core, got[0], own, swapped)]
     turned = [flip(got[0])]
     got[2], got[1], parts, turned = lax.optimization_barrier((got[2], got[1], parts, turned))
-    made = project(core, got[1], own, swapped)
-    parts.append(across(made, "zl", 1))
-    for k in (2, 3):
-        got[k], made = lax.optimization_barrier((got[k], made))
+    for k, before in ((2, None), (1, 2), (3, 1)):
+        if before:
+            got[k], made = lax.optimization_barrier((got[k], made))
         made = project(core, got[k], own, swapped)
         parts.append(across(made, "zl", k))
+    parts[1], parts[2] = parts[2], parts[1]
     got, made = lax.optimization_barrier((got, made))
     turned += [flip(x) for x in got[1:]]
     parts, turned = lax.optimization_barrier((parts, turned))
@@ -285,8 +286,8 @@
     ny, nx, nz, rows, _ = local.shape
     shares = lax.all_to_all(local.reshape(ny * nx, nz * rows, features), ("y", "x"), 0, 0, tiled=True)
     total, low = half_total(zh, shares, held)
-    partner_total = lax.ppermute(low, "zh", SWAP)
-    new_base, new_mom, spread = outer_step(zh, total, partner_total, held, ny * nx)
+    both = lax.all_gather(low, "zh")
+    new_base, new_mom, spread = outer_step(zh, total, both, held, ny * nx)
     base = lax.all_to_all(spread, ("y", "x"), 0, 0, tiled=True).reshape(local.shape)
     return mix(local, base), new_base, new_mom
 

time: 179 us -> 178 us (level)
  blocking collectives: 47.7 us -> 56.4 us
  starting transfers between devices: 45.2 us -> 36.7 us
  waiting for transfers between devices: 63.7 us -> 61.8 us
    all_gather x0 -> x1, blocking collectives: none -> 9.83 us  [body(): both = lax.all_gather(low, 'zh')]
    ppermute x1 -> x0, starting transfers between devices: 8.48 us -> none  [body(): partner_total = lax.ppermute(low, 'zh', SWAP)]
    ppermute x1 -> x0, waiting for transfers between devices: 1.88 us -> none  [body(): partner_total = lax.ppermute(low, 'zh', SWAP)]
  transfers between devices with their start and end apart: 10 -> 9, of which waited for: 6 -> 5; matrix products, arithmetic and copies ran while one was open for 0% -> 0% of each run, Pallas kernels for 6% -> 6%
where the time goes in v8:
time: 178 us; the launch traced here: 176 us
  waiting for transfers between devices  61.8 us (35%)
  blocking collectives  56.4 us (32%)
  starting transfers between devices  36.7 us (21%)
  Pallas kernels  17.2 us (10%)
  local copies, waits for them, and re-layouts  3.19 us (2%)
    all_to_all x1, blocking collectives, body(): lax.all_to_all(spread, ('y', 'x'), 0, 0, tiled=True).reshape(local.shape)  31.6 us
    ppermute x6, waiting for transfers between devices, across(): return lax.ppermute(value, axis, [(i, i ^ k) for i in range(4)])  31.5 us
    all_to_all x1, waiting for transfers between devices, body(): lax.all_to_all(local.reshape(ny * nx, nz * rows, features), ('y', 'x'), 0...  28.4 us
    ppermute x6, starting transfers between devices, across(): return lax.ppermute(value, axis, [(i, i ^ k) for i in range(4)])  22.7 us
    all_gather x1, blocking collectives, body(): key_grads = lax.all_gather(key_grad, 'zl', axis=0, tiled=True)  15 us
    all_to_all x1, starting transfers between devices, body(): lax.all_to_all(local.reshape(ny * nx, nz * rows, features), ('y', 'x'), 0...  10.2 us
    all_gather x1, blocking collectives, body(): both = lax.all_gather(low, 'zh')  9.83 us
    pallas_call x4, Pallas kernels, project(): call(project_kernel, jax.ShapeDtypeStruct((x.shape[0], own.shape[1]), BF)...  4.9 us
  transfers between devices with their start and end apart: 9, of which 5 were waited for; matrix products, arithmetic and copies ran while one was open for 0% of the time, Pallas kernels for 6%

profile of v8, /device:TPU:6, one launch (start us, length us, event | category | flops | bytes accessed | tf_op | source)
XLA Modules:
  0.0 176.2 jit_solution(750755166437337169)
XLA Ops:
  0.6 1.9 %collective-permute-start.2 = (bf16[1024,512]{1,0:T(8,128)(2,1)}, bf16[1024,512]{1,0:T(8,128)(2,1)S(1)}, u32[]{:S(2)}, u32[]{:S(2)}) collective-permute-start(bf16[1024,512]{1,0:T(8,128)(2,1)} %bitcast.8), channel_id=1, source_target_pairs={{0,1},{1,0},{2,3},{3,2},{4,5},{5,4},{6,7},{7,6},{8,9},{9,8},{10,11... | collective-permute-start | bytes 3145736 | tf_op jit(solution)/shard_map/ppermute | solution.py:265
  2.6 0.0 copy-start.1
  2.6 1.6 copy-done.1
  4.2 0.0 copy-start.4
  4.2 0.0 copy-start.5
  4.2 1.3 shard_map.76
  5.5 0.0 copy-start
  5.5 6.2 %collective-permute-start = (bf16[128,2048]{1,0:T(8,128)(2,1)}, bf16[128,2048]{1,0:T(8,128)(2,1)}, u32[]{:S(2)}, u32[]{:S(2)}) collective-permute-start(bf16[128,2048]{1,0:T(8,128)(2,1)} %get-tuple-element.30), channel_id=1, source_target_pairs={{0,4},{2,6},{4,0},{6,2},{1,5},{3,7},{5,1},{7,3},{8,12},{10,14},{12... | collective-permute-start | bytes 1572872 | tf_op jit(solution)/shard_map/ppermute | solution.py:256
  11.7 4.3 %collective-permute-start.1 = (bf16[128,2048]{1,0:T(8,128)(2,1)}, bf16[128,2048]{1,0:T(8,128)(2,1)}, u32[]{:S(2)}, u32[]{:S(2)}) collective-permute-start(bf16[128,2048]{1,0:T(8,128)(2,1)} %get-tuple-element.31), channel_id=1, source_target_pairs={{0,2},{2,0},{4,6},{6,4},{1,3},{3,1},{5,7},{7,5},{8,10},{10,8},{12,... | collective-permute-start | bytes 1572872 | tf_op jit(solution)/shard_map/ppermute | solution.py:256
  16.0 1.9 %collective-permute-start.5 = (bf16[128,2048]{1,0:T(8,128)(2,1)}, bf16[128,2048]{1,0:T(8,128)(2,1)}, u32[]{:S(2)}, u32[]{:S(2)}) collective-permute-start(bf16[128,2048]{1,0:T(8,128)(2,1)} %get-tuple-element.37), channel_id=1, source_target_pairs={{0,6},{2,4},{4,2},{6,0},{1,7},{3,5},{5,3},{7,1},{8,14},{10,12},{12... | collective-permute-start | bytes 1572872 | tf_op jit(solution)/shard_map/ppermute | solution.py:256
  17.9 0.0 copy-start.2
  18.0 1.6 copy-done.2
  19.6 0.0 copy-done.4
  19.6 0.0 copy-done.5
  19.6 0.2 shard_map.80.refs_0_
  19.8 0.0 collective-permute-done.2.other_ref
  19.8 0.0 copy-done
  19.8 0.4 shard_map.79.a_ref
  20.3 15.8 %collective-permute-done.x_ref = bf16[128,2048]{1,0:T(8,128)(2,1)} collective-permute-done((bf16[128,2048]{1,0:T(8,128)(2,1)}, bf16[128,2048]{1,0:T(8,128)(2,1)}, u32[]{:S(2)}, u32[]{:S(2)}) %collective-permute-start) | collective-permute-done | bytes 524320 | tf_op jit(solution)/shard_map/ppermute | solution.py:256
  36.1 13.1 %collective-permute-done.1.x_ref = bf16[128,2048]{1,0:T(8,128)(2,1)} collective-permute-done((bf16[128,2048]{1,0:T(8,128)(2,1)}, bf16[128,2048]{1,0:T(8,128)(2,1)}, u32[]{:S(2)}, u32[]{:S(2)}) %collective-permute-start.1) | collective-permute-done | bytes 524320 | tf_op jit(solution)/shard_map/ppermute | solution.py:256
  49.2 1.5 shard_map.81
  50.7 3.3 %collective-permute-start.4 = (bf16[128,512]{1,0:T(8,128)(2,1)S(1)}, bf16[128,512]{1,0:T(8,128)(2,1)S(1)}, u32[]{:S(2)}, u32[]{:S(2)}) collective-permute-start(bf16[128,512]{1,0:T(8,128)(2,1)S(1)} %shard_map.81), channel_id=1, source_target_pairs={{0,4},{2,6},{4,0},{6,2},{1,5},{3,7},{5,1},{7,3},{8,12},{10,14},{12... | collective-permute-start | bytes 393224 | tf_op jit(solution)/shard_map/ppermute | solution.py:256
  53.9 1.5 shard_map.82
  55.4 4.4 %collective-permute-start.3 = (bf16[128,512]{1,0:T(8,128)(2,1)S(1)}, bf16[128,512]{1,0:T(8,128)(2,1)}, u32[]{:S(2)}, u32[]{:S(2)}) collective-permute-start(bf16[128,512]{1,0:T(8,128)(2,1)S(1)} %shard_map.82), channel_id=1, source_target_pairs={{0,2},{2,0},{4,6},{6,4},{1,3},{3,1},{5,7},{7,5},{8,10},{10,8},{12,... | collective-permute-start | bytes 393224 | tf_op jit(solution)/shard_map/ppermute | solution.py:256
  59.8 0.0 collective-permute-done.5.x_ref
  59.8 1.5 shard_map.83
  61.3 0.0 copy-start.3
  61.3 2.6 %collective-permute-start.6 = (bf16[128,512]{1,0:T(8,128)(2,1)S(1)}, bf16[128,512]{1,0:T(8,128)(2,1)}, u32[]{:S(2)}, u32[]{:S(2)}) collective-permute-start(bf16[128,512]{1,0:T(8,128)(2,1)S(1)} %shard_map.83), channel_id=1, source_target_pairs={{0,6},{2,4},{4,2},{6,0},{1,7},{3,5},{5,3},{7,1},{8,14},{10,12},{12... | collective-permute-start | bytes 393224 | tf_op jit(solution)/shard_map/ppermute | solution.py:256
  63.9 1.2 shard_map.84.refs_1_
  65.2 1.2 shard_map.85.refs_2_
  66.4 1.2 shard_map.86.refs_3_
  67.6 0.0 collective-permute-done.3.b_ref
  67.7 0.0 collective-permute-done.4.c_ref
  67.7 2.6 %collective-permute-done.6.d_ref = bf16[128,512]{1,0:T(8,128)(2,1)} collective-permute-done((bf16[128,512]{1,0:T(8,128)(2,1)S(1)}, bf16[128,512]{1,0:T(8,128)(2,1)}, u32[]{:S(2)}, u32[]{:S(2)}) %collective-permute-start.6) | collective-permute-done | bytes 131104 | tf_op jit(solution)/shard_map/ppermute | solution.py:256
  70.3 0.0 copy-done.3
  70.3 1.2 shard_map.87
  71.5 15.0 %all_gather.9.refs_4_ = bf16[512,512]{1,0:T(8,128)(2,1)S(1)} all-gather(bf16[128,512]{1,0:T(8,128)(2,1)S(1)} %shard_map.87), channel_id=1, replica_groups=mesh['y'=8,'zh'=2,'x'=4,'zl'=4,'core'=2] {'zl'}, dimensions={0}, use_global_device_ids=true | all-gather | bytes 655360 | tf_op jit(solution)/shard_map/all_gather | solution.py:282
  86.6 0.7 shard_map.89
  87.3 1.9 %collective-permute-start.7 = (bf16[1024,512]{1,0:T(8,128)(2,1)S(1)}, bf16[1024,512]{1,0:T(8,128)(2,1)S(1)}, u32[]{:S(2)}, u32[]{:S(2)}) collective-permute-start(bf16[1024,512]{1,0:T(8,128)(2,1)S(1)} %shard_map.89), channel_id=1, source_target_pairs={{0,1},{1,0},{2,3},{3,2},{4,5},{5,4},{6,7},{7,6},{8,9},{9,8},{10,11... | collective-permute-start | bytes 3145736 | tf_op jit(solution)/shard_map/ppermute | solution.py:285
  89.2 0.7 shard_map.88.s_ref
  89.9 1.9 %collective-permute-done.7.o_ref = bf16[1024,512]{1,0:T(8,128)(2,1)S(1)} collective-permute-done((bf16[1024,512]{1,0:T(8,128)(2,1)S(1)}, bf16[1024,512]{1,0:T(8,128)(2,1)S(1)}, u32[]{:S(2)}, u32[]{:S(2)}) %collective-permute-start.7) | collective-permute-done | bytes 1048608 | tf_op jit(solution)/shard_map/ppermute | solution.py:285
  91.8 1.3 shard_map.90.l_ref
  93.1 10.2 %all-to-all-start = ((bf16[32,32,512]{2,1,0:T(8,128)(2,1)}), bf16[32,32,512]{2,1,0:T(8,128)(2,1)S(1)}, u32[]{:S(2)}, u32[]{:S(2)}) async-start(bf16[32,32,512]{2,1,0:T(8,128)(2,1)} %bitcast.5), calls=%async_computation | async-start | bytes 2097152 | tf_op jit(solution)/shard_map/all_to_all | solution.py:287
  103.4 28.4 %all-to-all-done.l_ref = bf16[32,32,512]{2,1,0:T(8,128)(2,1)S(1)} async-done(((bf16[32,32,512]{2,1,0:T(8,128)(2,1)}), bf16[32,32,512]{2,1,0:T(8,128)(2,1)S(1)}, u32[]{:S(2)}, u32[]{:S(2)}) %all-to-all-start) | async-done | bytes 1048608 | tf_op jit(solution)/shard_map/all_to_all | solution.py:287
  131.7 0.1 shard_map.91
  131.9 9.8 %all-gather = bf16[64,512]{1,0:T(8,128)(2,1)S(1)} all-gather(bf16[32,512]{1,0:T(8,128)(2,1)S(1)} %get-tuple-element.53), channel_id=2, replica_groups=mesh['y'=8,'zh'=2,'x'=4,'zl'=4,'core'=2] {'zh'}, dimensions={0}, use_global_device_ids=true | all-gather | bytes 98304 | tf_op jit(solution)/shard_map/all_gather | solution.py:289
  141.7 0.6 shard_map.92
  142.3 31.6 %all_to_all.10 = bf16[32,32,512]{2,1,0:T(8,128)(2,1)S(1)} all-to-all(bf16[32,32,512]{2,1,0:T(8,128)(2,1)S(1)} %get-tuple-element.54), channel_id=1, replica_groups=mesh['y'=8,'zh'=2,'x'=4,'zl'=4,'core'=2] {'y','x'}, dimensions={0} | all-to-all | bytes 2097152 | tf_op jit(solution)/shard_map/all_to_all | solution.py:291
  173.9 2.3 %shard_map.93 = bf16[1,1024,512]{2,1,0:T(8,128)(2,1)} custom-call(bf16[8,4,2,16,512]{4,3,2,1,0:T(8,128)(2,1)} %shard_map.90.l_ref, bf16[8,4,2,16,512]{4,3,2,1,0:T(8,128)(2,1)S(1)} %bitcast.14), custom_call_target="tpu_custom_call" | custom-call | bytes 3145728 | tf_op jit(solution)/shard_map/pallas_call | solution.py:245
  (2 shorter events, 0.1 us)
Async XLA Ops:
  0.6 19.2 %collective-permute-start.2 = (bf16[1024,512]{1,0:T(8,128)(2,1)}, bf16[1024,512]{1,0:T(8,128)(2,1)S(1)}, u32[]{:S(2)}, u32[]{:S(2)}) collective-permute-start(bf16[1024,512]{1,0:T(8,128)(2,1)} %bitcast.8), channel_id=1, source_target_pairs={{0,1},{1,0},{2,3},{3,2},{4,5},{5,4},{6,7},{7,6},{8,9},{9,8},{10,11... | collective-permute-start | bytes 3145736 | tf_op jit(solution)/shard_map/ppermute | solution.py:265
  2.6 1.6 copy-start.1
  4.2 15.4 %copy-start.4 = (f32[1,16,512]{2,1,0:T(8,128)S(1)}, f32[1,16,512]{2,1,0:T(8,128)}, u32[]{:S(2)}) copy-start(f32[1,16,512]{2,1,0:T(8,128)} %a_ref.1) | copy-start | bytes 98308
  4.2 15.4 %copy-start.5 = (f32[1,16,512]{2,1,0:T(8,128)S(1)}, f32[1,16,512]{2,1,0:T(8,128)}, u32[]{:S(2)}) copy-start(f32[1,16,512]{2,1,0:T(8,128)} %m_ref.1) | copy-start | bytes 98308
  5.5 14.4 %copy-start = (bf16[1,1024,512]{2,1,0:T(8,128)(2,1)S(1)}, bf16[1,1024,512]{2,1,0:T(8,128)(2,1)}, u32[]{:S(2)}) copy-start(bf16[1,1024,512]{2,1,0:T(8,128)(2,1)} %param.7) | copy-start | bytes 3145732
  5.5 30.6 %collective-permute-start = (bf16[128,2048]{1,0:T(8,128)(2,1)}, bf16[128,2048]{1,0:T(8,128)(2,1)}, u32[]{:S(2)}, u32[]{:S(2)}) collective-permute-start(bf16[128,2048]{1,0:T(8,128)(2,1)} %get-tuple-element.30), channel_id=1, source_target_pairs={{0,4},{2,6},{4,0},{6,2},{1,5},{3,7},{5,1},{7,3},{8,12},{10,14},{12... | collective-permute-start | bytes 1572872 | tf_op jit(solution)/shard_map/ppermute | solution.py:256
  11.7 37.5 %collective-permute-start.1 = (bf16[128,2048]{1,0:T(8,128)(2,1)}, bf16[128,2048]{1,0:T(8,128)(2,1)}, u32[]{:S(2)}, u32[]{:S(2)}) collective-permute-start(bf16[128,2048]{1,0:T(8,128)(2,1)} %get-tuple-element.31), channel_id=1, source_target_pairs={{0,2},{2,0},{4,6},{6,4},{1,3},{3,1},{5,7},{7,5},{8,10},{10,8},{12,... | collective-permute-start | bytes 1572872 | tf_op jit(solution)/shard_map/ppermute | solution.py:256
  16.0 43.8 %collective-permute-start.5 = (bf16[128,2048]{1,0:T(8,128)(2,1)}, bf16[128,2048]{1,0:T(8,128)(2,1)}, u32[]{:S(2)}, u32[]{:S(2)}) collective-permute-start(bf16[128,2048]{1,0:T(8,128)(2,1)} %get-tuple-element.37), channel_id=1, source_target_pairs={{0,6},{2,4},{4,2},{6,0},{1,7},{3,5},{5,3},{7,1},{8,14},{10,12},{12... | collective-permute-start | bytes 1572872 | tf_op jit(solution)/shard_map/ppermute | solution.py:256
  17.9 1.6 copy-start.2
  50.7 17.0 %collective-permute-start.4 = (bf16[128,512]{1,0:T(8,128)(2,1)S(1)}, bf16[128,512]{1,0:T(8,128)(2,1)S(1)}, u32[]{:S(2)}, u32[]{:S(2)}) collective-permute-start(bf16[128,512]{1,0:T(8,128)(2,1)S(1)} %shard_map.81), channel_id=1, source_target_pairs={{0,4},{2,6},{4,0},{6,2},{1,5},{3,7},{5,1},{7,3},{8,12},{10,14},{12... | collective-permute-start | bytes 393224 | tf_op jit(solution)/shard_map/ppermute | solution.py:256
  55.4 12.2 %collective-permute-start.3 = (bf16[128,512]{1,0:T(8,128)(2,1)S(1)}, bf16[128,512]{1,0:T(8,128)(2,1)}, u32[]{:S(2)}, u32[]{:S(2)}) collective-permute-start(bf16[128,512]{1,0:T(8,128)(2,1)S(1)} %shard_map.82), channel_id=1, source_target_pairs={{0,2},{2,0},{4,6},{6,4},{1,3},{3,1},{5,7},{7,5},{8,10},{10,8},{12,... | collective-permute-start | bytes 393224 | tf_op jit(solution)/shard_map/ppermute | solution.py:256
  61.3 9.0 %copy-start.3 = (bf16[128,512]{1,0:T(8,128)(2,1)S(1)}, bf16[128,512]{1,0:T(8,128)(2,1)}, u32[]{:S(2)}) copy-start(bf16[128,512]{1,0:T(8,128)(2,1)} %g_ref.1) | copy-start | bytes 393220
  61.3 9.0 %collective-permute-start.6 = (bf16[128,512]{1,0:T(8,128)(2,1)S(1)}, bf16[128,512]{1,0:T(8,128)(2,1)}, u32[]{:S(2)}, u32[]{:S(2)}) collective-permute-start(bf16[128,512]{1,0:T(8,128)(2,1)S(1)} %shard_map.83), channel_id=1, source_target_pairs={{0,6},{2,4},{4,2},{6,0},{1,7},{3,5},{5,3},{7,1},{8,14},{10,12},{12... | collective-permute-start | bytes 393224 | tf_op jit(solution)/shard_map/ppermute | solution.py:256
  87.3 4.6 %collective-permute-start.7 = (bf16[1024,512]{1,0:T(8,128)(2,1)S(1)}, bf16[1024,512]{1,0:T(8,128)(2,1)S(1)}, u32[]{:S(2)}, u32[]{:S(2)}) collective-permute-start(bf16[1024,512]{1,0:T(8,128)(2,1)S(1)} %shard_map.89), channel_id=1, source_target_pairs={{0,1},{1,0},{2,3},{3,2},{4,5},{5,4},{6,7},{7,6},{8,9},{9,8},{10,11... | collective-permute-start | bytes 3145736 | tf_op jit(solution)/shard_map/ppermute | solution.py:285
  93.1 38.6 %all-to-all-start = ((bf16[32,32,512]{2,1,0:T(8,128)(2,1)}), bf16[32,32,512]{2,1,0:T(8,128)(2,1)S(1)}, u32[]{:S(2)}, u32[]{:S(2)}) async-start(bf16[32,32,512]{2,1,0:T(8,128)(2,1)} %bitcast.5), calls=%async_computation | async-start | bytes 2097152 | tf_op jit(solution)/shard_map/all_to_all | solution.py:287

commit v9 on v8

--- a/solution.py
+++ b/solution.py
@@ -222,20 +222,24 @@
     return call(hold_kernel, pltpu.VMEM((2, *anchor.shape), F32))(anchor, momentum)
 
 
-def mix_kernel(l_ref, b_ref, out_ref, held_ref, sems):
-    ny, nx, nz, own, _ = l_ref.shape
+def mix_kernel(l_ref, b_ref, out_ref, lh_ref, held_ref, sems):
+    ny, nx, nz, own, _ = b_ref.shape
     rows = nz * nx * own
-    copies = []
+    reads = [pltpu.make_async_copy(l_ref.at[y], lh_ref.at[y], sems.at[0, y]) for y in range(ny)]
+    for copy in reads:
+        copy.start()
+    writes = []
     for y in range(ny):
-        mixed = (1.0 - MIX_RATE) * l_ref[y].astype(F32) + MIX_RATE * b_ref[y].astype(F32)
+        reads[y].wait()
+        mixed = (1.0 - MIX_RATE) * lh_ref[y].astype(F32) + MIX_RATE * b_ref[y].astype(F32)
         mixed = mixed.astype(BF)
         for z in range(nz):
             for x in range(nx):
                 held_ref[pl.ds(((y * nz + z) * nx + x) * own, own)] = mixed[x, z]
         part = pl.ds(y * rows, rows)
-        copies.append(pltpu.make_async_copy(held_ref.at[part], out_ref.at[0, part], sems.at[y]))
-        copies[-1].start()
-    for copy in copies:
+        writes.append(pltpu.make_async_copy(held_ref.at[part], out_ref.at[0, part], sems.at[1, y]))
+        writes[-1].start()
+    for copy in writes:
         copy.wait()
 
 
@@ -245,10 +249,13 @@
     return call(
         mix_kernel,
         jax.ShapeDtypeStruct((1, rows, features), BF),
-        moved=6 * local.size,
-        in_specs=[pl.BlockSpec(memory_space=pltpu.VMEM)] * 2,
+        in_specs=[pl.BlockSpec(memory_space=pl.ANY), pl.BlockSpec(memory_space=pltpu.VMEM)],
         out_specs=pl.BlockSpec(memory_space=pl.ANY),
-        scratch_shapes=[pltpu.VMEM((rows, features), BF), pltpu.SemaphoreType.DMA((ny,))],
+        scratch_shapes=[
+            pltpu.VMEM(local.shape, BF),
+            pltpu.VMEM((rows, features), BF),
+            pltpu.SemaphoreType.DMA((2, ny)),
+        ],
     )(local, base)
 
 

time: 178 us -> 177 us (level)
  no operation moved by 1% of the time
where the time goes in v9:
time: 177 us; the launch traced here: 176 us
  waiting for transfers between devices  61.8 us (35%)
  blocking collectives  56.4 us (32%)
  starting transfers between devices  36.7 us (21%)
  Pallas kernels  17 us (10%)
  local copies, waits for them, and re-layouts  3.19 us (2%)
    all_to_all x1, blocking collectives, body(): lax.all_to_all(spread, ('y', 'x'), 0, 0, tiled=True).reshape(local.shape)  31.6 us
    ppermute x6, waiting for transfers between devices, across(): return lax.ppermute(value, axis, [(i, i ^ k) for i in range(4)])  31.5 us
    all_to_all x1, waiting for transfers between devices, body(): lax.all_to_all(local.reshape(ny * nx, nz * rows, features), ('y', 'x'), 0...  28.4 us
    ppermute x6, starting transfers between devices, across(): return lax.ppermute(value, axis, [(i, i ^ k) for i in range(4)])  22.7 us
    all_gather x1, blocking collectives, body(): key_grads = lax.all_gather(key_grad, 'zl', axis=0, tiled=True)  15 us
    all_to_all x1, starting transfers between devices, body(): lax.all_to_all(local.reshape(ny * nx, nz * rows, features), ('y', 'x'), 0...  10.2 us
    all_gather x1, blocking collectives, body(): both = lax.all_gather(low, 'zh')  9.83 us
    pallas_call x4, Pallas kernels, project(): call(project_kernel, jax.ShapeDtypeStruct((x.shape[0], own.shape[1]), BF)...  4.9 us
  transfers between devices with their start and end apart: 9, of which 5 were waited for; matrix products, arithmetic and copies ran while one was open for 0% of the time, Pallas kernels for 6%

profile of v9, /device:TPU:6, one launch (start us, length us, event | category | flops | bytes accessed | tf_op | source)
XLA Modules:
  0.0 176.1 jit_solution(12636745913802497155)
XLA Ops:
  0.6 1.9 %collective-permute-start.2 = (bf16[1024,512]{1,0:T(8,128)(2,1)}, bf16[1024,512]{1,0:T(8,128)(2,1)S(1)}, u32[]{:S(2)}, u32[]{:S(2)}) collective-permute-start(bf16[1024,512]{1,0:T(8,128)(2,1)} %bitcast.8), channel_id=1, source_target_pairs={{0,1},{1,0},{2,3},{3,2},{4,5},{5,4},{6,7},{7,6},{8,9},{9,8},{10,11... | collective-permute-start | bytes 3145736 | tf_op jit(solution)/shard_map/ppermute | solution.py:272
  2.6 0.0 copy-start.1
  2.6 1.6 copy-done.1
  4.2 0.0 copy-start.4
  4.2 0.0 copy-start.5
  4.2 1.3 shard_map.76
  5.5 0.0 copy-start
  5.5 6.2 %collective-permute-start = (bf16[128,2048]{1,0:T(8,128)(2,1)}, bf16[128,2048]{1,0:T(8,128)(2,1)}, u32[]{:S(2)}, u32[]{:S(2)}) collective-permute-start(bf16[128,2048]{1,0:T(8,128)(2,1)} %get-tuple-element.30), channel_id=1, source_target_pairs={{0,4},{2,6},{4,0},{6,2},{1,5},{3,7},{5,1},{7,3},{8,12},{10,14},{12... | collective-permute-start | bytes 1572872 | tf_op jit(solution)/shard_map/ppermute | solution.py:263
  11.7 4.3 %collective-permute-start.1 = (bf16[128,2048]{1,0:T(8,128)(2,1)}, bf16[128,2048]{1,0:T(8,128)(2,1)}, u32[]{:S(2)}, u32[]{:S(2)}) collective-permute-start(bf16[128,2048]{1,0:T(8,128)(2,1)} %get-tuple-element.31), channel_id=1, source_target_pairs={{0,2},{2,0},{4,6},{6,4},{1,3},{3,1},{5,7},{7,5},{8,10},{10,8},{12,... | collective-permute-start | bytes 1572872 | tf_op jit(solution)/shard_map/ppermute | solution.py:263
  16.0 1.9 %collective-permute-start.5 = (bf16[128,2048]{1,0:T(8,128)(2,1)}, bf16[128,2048]{1,0:T(8,128)(2,1)}, u32[]{:S(2)}, u32[]{:S(2)}) collective-permute-start(bf16[128,2048]{1,0:T(8,128)(2,1)} %get-tuple-element.37), channel_id=1, source_target_pairs={{0,6},{2,4},{4,2},{6,0},{1,7},{3,5},{5,3},{7,1},{8,14},{10,12},{12... | collective-permute-start | bytes 1572872 | tf_op jit(solution)/shard_map/ppermute | solution.py:263
  17.9 0.0 copy-start.2
  18.0 1.6 copy-done.2
  19.6 0.0 copy-done.4
  19.6 0.0 copy-done.5
  19.6 0.2 shard_map.80.refs_0_
  19.8 0.0 collective-permute-done.2.other_ref
  19.8 0.0 copy-done
  19.8 0.4 shard_map.79.a_ref
  20.3 15.8 %collective-permute-done.x_ref = bf16[128,2048]{1,0:T(8,128)(2,1)} collective-permute-done((bf16[128,2048]{1,0:T(8,128)(2,1)}, bf16[128,2048]{1,0:T(8,128)(2,1)}, u32[]{:S(2)}, u32[]{:S(2)}) %collective-permute-start) | collective-permute-done | bytes 524320 | tf_op jit(solution)/shard_map/ppermute | solution.py:263
  36.1 13.1 %collective-permute-done.1.x_ref = bf16[128,2048]{1,0:T(8,128)(2,1)} collective-permute-done((bf16[128,2048]{1,0:T(8,128)(2,1)}, bf16[128,2048]{1,0:T(8,128)(2,1)}, u32[]{:S(2)}, u32[]{:S(2)}) %collective-permute-start.1) | collective-permute-done | bytes 524320 | tf_op jit(solution)/shard_map/ppermute | solution.py:263
  49.2 1.5 shard_map.81
  50.7 3.3 %collective-permute-start.4 = (bf16[128,512]{1,0:T(8,128)(2,1)S(1)}, bf16[128,512]{1,0:T(8,128)(2,1)S(1)}, u32[]{:S(2)}, u32[]{:S(2)}) collective-permute-start(bf16[128,512]{1,0:T(8,128)(2,1)S(1)} %shard_map.81), channel_id=1, source_target_pairs={{0,4},{2,6},{4,0},{6,2},{1,5},{3,7},{5,1},{7,3},{8,12},{10,14},{12... | collective-permute-start | bytes 393224 | tf_op jit(solution)/shard_map/ppermute | solution.py:263
  53.9 1.5 shard_map.82
  55.4 4.4 %collective-permute-start.3 = (bf16[128,512]{1,0:T(8,128)(2,1)S(1)}, bf16[128,512]{1,0:T(8,128)(2,1)}, u32[]{:S(2)}, u32[]{:S(2)}) collective-permute-start(bf16[128,512]{1,0:T(8,128)(2,1)S(1)} %shard_map.82), channel_id=1, source_target_pairs={{0,2},{2,0},{4,6},{6,4},{1,3},{3,1},{5,7},{7,5},{8,10},{10,8},{12,... | collective-permute-start | bytes 393224 | tf_op jit(solution)/shard_map/ppermute | solution.py:263
  59.8 0.0 collective-permute-done.5.x_ref
  59.8 1.5 shard_map.83
  61.3 0.0 copy-start.3
  61.3 2.6 %collective-permute-start.6 = (bf16[128,512]{1,0:T(8,128)(2,1)S(1)}, bf16[128,512]{1,0:T(8,128)(2,1)}, u32[]{:S(2)}, u32[]{:S(2)}) collective-permute-start(bf16[128,512]{1,0:T(8,128)(2,1)S(1)} %shard_map.83), channel_id=1, source_target_pairs={{0,6},{2,4},{4,2},{6,0},{1,7},{3,5},{5,3},{7,1},{8,14},{10,12},{12... | collective-permute-start | bytes 393224 | tf_op jit(solution)/shard_map/ppermute | solution.py:263
  63.9 1.2 shard_map.84.refs_1_
  65.2 1.2 shard_map.85.refs_2_
  66.4 1.2 shard_map.86.refs_3_
  67.6 0.0 collective-permute-done.3.b_ref
  67.7 0.0 collective-permute-done.4.c_ref
  67.7 2.6 %collective-permute-done.6.d_ref = bf16[128,512]{1,0:T(8,128)(2,1)} collective-permute-done((bf16[128,512]{1,0:T(8,128)(2,1)S(1)}, bf16[128,512]{1,0:T(8,128)(2,1)}, u32[]{:S(2)}, u32[]{:S(2)}) %collective-permute-start.6) | collective-permute-done | bytes 131104 | tf_op jit(solution)/shard_map/ppermute | solution.py:263
  70.3 0.0 copy-done.3
  70.3 1.2 shard_map.87
  71.5 15.0 %all_gather.9.refs_4_ = bf16[512,512]{1,0:T(8,128)(2,1)S(1)} all-gather(bf16[128,512]{1,0:T(8,128)(2,1)S(1)} %shard_map.87), channel_id=1, replica_groups=mesh['y'=8,'zh'=2,'x'=4,'zl'=4,'core'=2] {'zl'}, dimensions={0}, use_global_device_ids=true | all-gather | bytes 655360 | tf_op jit(solution)/shard_map/all_gather | solution.py:289
  86.6 0.7 shard_map.89
  87.3 1.9 %collective-permute-start.7 = (bf16[1024,512]{1,0:T(8,128)(2,1)S(1)}, bf16[1024,512]{1,0:T(8,128)(2,1)S(1)}, u32[]{:S(2)}, u32[]{:S(2)}) collective-permute-start(bf16[1024,512]{1,0:T(8,128)(2,1)S(1)} %shard_map.89), channel_id=1, source_target_pairs={{0,1},{1,0},{2,3},{3,2},{4,5},{5,4},{6,7},{7,6},{8,9},{9,8},{10,11... | collective-permute-start | bytes 3145736 | tf_op jit(solution)/shard_map/ppermute | solution.py:292
  89.2 0.7 shard_map.88.s_ref
  89.9 1.9 %collective-permute-done.7.o_ref = bf16[1024,512]{1,0:T(8,128)(2,1)S(1)} collective-permute-done((bf16[1024,512]{1,0:T(8,128)(2,1)S(1)}, bf16[1024,512]{1,0:T(8,128)(2,1)S(1)}, u32[]{:S(2)}, u32[]{:S(2)}) %collective-permute-start.7) | collective-permute-done | bytes 1048608 | tf_op jit(solution)/shard_map/ppermute | solution.py:292
  91.8 1.3 shard_map.90.l_ref
  93.1 10.2 %all-to-all-start = ((bf16[32,32,512]{2,1,0:T(8,128)(2,1)}), bf16[32,32,512]{2,1,0:T(8,128)(2,1)S(1)}, u32[]{:S(2)}, u32[]{:S(2)}) async-start(bf16[32,32,512]{2,1,0:T(8,128)(2,1)} %bitcast.5), calls=%async_computation | async-start | bytes 2097152 | tf_op jit(solution)/shard_map/all_to_all | solution.py:294
  103.4 28.4 %all-to-all-done.l_ref = bf16[32,32,512]{2,1,0:T(8,128)(2,1)S(1)} async-done(((bf16[32,32,512]{2,1,0:T(8,128)(2,1)}), bf16[32,32,512]{2,1,0:T(8,128)(2,1)S(1)}, u32[]{:S(2)}, u32[]{:S(2)}) %all-to-all-start) | async-done | bytes 1048608 | tf_op jit(solution)/shard_map/all_to_all | solution.py:294
  131.7 0.1 shard_map.91
  131.9 9.8 %all-gather = bf16[64,512]{1,0:T(8,128)(2,1)S(1)} all-gather(bf16[32,512]{1,0:T(8,128)(2,1)S(1)} %get-tuple-element.53), channel_id=2, replica_groups=mesh['y'=8,'zh'=2,'x'=4,'zl'=4,'core'=2] {'zh'}, dimensions={0}, use_global_device_ids=true | all-gather | bytes 98304 | tf_op jit(solution)/shard_map/all_gather | solution.py:296
  141.7 0.6 shard_map.92
  142.3 31.6 %all_to_all.10 = bf16[32,32,512]{2,1,0:T(8,128)(2,1)S(1)} all-to-all(bf16[32,32,512]{2,1,0:T(8,128)(2,1)S(1)} %get-tuple-element.54), channel_id=1, replica_groups=mesh['y'=8,'zh'=2,'x'=4,'zl'=4,'core'=2] {'y','x'}, dimensions={0} | all-to-all | bytes 2097152 | tf_op jit(solution)/shard_map/all_to_all | solution.py:298
  173.9 2.2 %shard_map.93 = bf16[1,1024,512]{2,1,0:T(8,128)(2,1)} custom-call(bf16[8,4,2,16,512]{4,3,2,1,0:T(8,128)(2,1)} %shard_map.90.l_ref, bf16[8,4,2,16,512]{4,3,2,1,0:T(8,128)(2,1)S(1)} %bitcast.14), custom_call_target="tpu_custom_call" | custom-call | tf_op jit(solution)/shard_map/pallas_call | solution.py:249
  (2 shorter events, 0.1 us)
Async XLA Ops:
  0.6 19.2 %collective-permute-start.2 = (bf16[1024,512]{1,0:T(8,128)(2,1)}, bf16[1024,512]{1,0:T(8,128)(2,1)S(1)}, u32[]{:S(2)}, u32[]{:S(2)}) collective-permute-start(bf16[1024,512]{1,0:T(8,128)(2,1)} %bitcast.8), channel_id=1, source_target_pairs={{0,1},{1,0},{2,3},{3,2},{4,5},{5,4},{6,7},{7,6},{8,9},{9,8},{10,11... | collective-permute-start | bytes 3145736 | tf_op jit(solution)/shard_map/ppermute | solution.py:272
  2.6 1.6 copy-start.1
  4.2 15.4 %copy-start.4 = (f32[1,16,512]{2,1,0:T(8,128)S(1)}, f32[1,16,512]{2,1,0:T(8,128)}, u32[]{:S(2)}) copy-start(f32[1,16,512]{2,1,0:T(8,128)} %a_ref.1) | copy-start | bytes 98308
  4.2 15.4 %copy-start.5 = (f32[1,16,512]{2,1,0:T(8,128)S(1)}, f32[1,16,512]{2,1,0:T(8,128)}, u32[]{:S(2)}) copy-start(f32[1,16,512]{2,1,0:T(8,128)} %m_ref.1) | copy-start | bytes 98308
  5.5 14.4 %copy-start = (bf16[1,1024,512]{2,1,0:T(8,128)(2,1)S(1)}, bf16[1,1024,512]{2,1,0:T(8,128)(2,1)}, u32[]{:S(2)}) copy-start(bf16[1,1024,512]{2,1,0:T(8,128)(2,1)} %param.7) | copy-start | bytes 3145732
  5.5 30.6 %collective-permute-start = (bf16[128,2048]{1,0:T(8,128)(2,1)}, bf16[128,2048]{1,0:T(8,128)(2,1)}, u32[]{:S(2)}, u32[]{:S(2)}) collective-permute-start(bf16[128,2048]{1,0:T(8,128)(2,1)} %get-tuple-element.30), channel_id=1, source_target_pairs={{0,4},{2,6},{4,0},{6,2},{1,5},{3,7},{5,1},{7,3},{8,12},{10,14},{12... | collective-permute-start | bytes 1572872 | tf_op jit(solution)/shard_map/ppermute | solution.py:263
  11.7 37.5 %collective-permute-start.1 = (bf16[128,2048]{1,0:T(8,128)(2,1)}, bf16[128,2048]{1,0:T(8,128)(2,1)}, u32[]{:S(2)}, u32[]{:S(2)}) collective-permute-start(bf16[128,2048]{1,0:T(8,128)(2,1)} %get-tuple-element.31), channel_id=1, source_target_pairs={{0,2},{2,0},{4,6},{6,4},{1,3},{3,1},{5,7},{7,5},{8,10},{10,8},{12,... | collective-permute-start | bytes 1572872 | tf_op jit(solution)/shard_map/ppermute | solution.py:263
  16.0 43.8 %collective-permute-start.5 = (bf16[128,2048]{1,0:T(8,128)(2,1)}, bf16[128,2048]{1,0:T(8,128)(2,1)}, u32[]{:S(2)}, u32[]{:S(2)}) collective-permute-start(bf16[128,2048]{1,0:T(8,128)(2,1)} %get-tuple-element.37), channel_id=1, source_target_pairs={{0,6},{2,4},{4,2},{6,0},{1,7},{3,5},{5,3},{7,1},{8,14},{10,12},{12... | collective-permute-start | bytes 1572872 | tf_op jit(solution)/shard_map/ppermute | solution.py:263
  17.9 1.6 copy-start.2
  50.7 17.0 %collective-permute-start.4 = (bf16[128,512]{1,0:T(8,128)(2,1)S(1)}, bf16[128,512]{1,0:T(8,128)(2,1)S(1)}, u32[]{:S(2)}, u32[]{:S(2)}) collective-permute-start(bf16[128,512]{1,0:T(8,128)(2,1)S(1)} %shard_map.81), channel_id=1, source_target_pairs={{0,4},{2,6},{4,0},{6,2},{1,5},{3,7},{5,1},{7,3},{8,12},{10,14},{12... | collective-permute-start | bytes 393224 | tf_op jit(solution)/shard_map/ppermute | solution.py:263
  55.4 12.2 %collective-permute-start.3 = (bf16[128,512]{1,0:T(8,128)(2,1)S(1)}, bf16[128,512]{1,0:T(8,128)(2,1)}, u32[]{:S(2)}, u32[]{:S(2)}) collective-permute-start(bf16[128,512]{1,0:T(8,128)(2,1)S(1)} %shard_map.82), channel_id=1, source_target_pairs={{0,2},{2,0},{4,6},{6,4},{1,3},{3,1},{5,7},{7,5},{8,10},{10,8},{12,... | collective-permute-start | bytes 393224 | tf_op jit(solution)/shard_map/ppermute | solution.py:263
  61.3 9.0 %copy-start.3 = (bf16[128,512]{1,0:T(8,128)(2,1)S(1)}, bf16[128,512]{1,0:T(8,128)(2,1)}, u32[]{:S(2)}) copy-start(bf16[128,512]{1,0:T(8,128)(2,1)} %g_ref.1) | copy-start | bytes 393220
  61.3 9.0 %collective-permute-start.6 = (bf16[128,512]{1,0:T(8,128)(2,1)S(1)}, bf16[128,512]{1,0:T(8,128)(2,1)}, u32[]{:S(2)}, u32[]{:S(2)}) collective-permute-start(bf16[128,512]{1,0:T(8,128)(2,1)S(1)} %shard_map.83), channel_id=1, source_target_pairs={{0,6},{2,4},{4,2},{6,0},{1,7},{3,5},{5,3},{7,1},{8,14},{10,12},{12... | collective-permute-start | bytes 393224 | tf_op jit(solution)/shard_map/ppermute | solution.py:263
  87.3 4.6 %collective-permute-start.7 = (bf16[1024,512]{1,0:T(8,128)(2,1)S(1)}, bf16[1024,512]{1,0:T(8,128)(2,1)S(1)}, u32[]{:S(2)}, u32[]{:S(2)}) collective-permute-start(bf16[1024,512]{1,0:T(8,128)(2,1)S(1)} %shard_map.89), channel_id=1, source_target_pairs={{0,1},{1,0},{2,3},{3,2},{4,5},{5,4},{6,7},{7,6},{8,9},{9,8},{10,11... | collective-permute-start | bytes 3145736 | tf_op jit(solution)/shard_map/ppermute | solution.py:292
  93.1 38.6 %all-to-all-start = ((bf16[32,32,512]{2,1,0:T(8,128)(2,1)}), bf16[32,32,512]{2,1,0:T(8,128)(2,1)S(1)}, u32[]{:S(2)}, u32[]{:S(2)}) async-start(bf16[32,32,512]{2,1,0:T(8,128)(2,1)} %bitcast.5), calls=%async_computation | async-start | bytes 2097152 | tf_op jit(solution)/shard_map/all_to_all | solution.py:294
